TPU v7x, 512 devices: a whole 4x4x16 slice. The times are simulated.
512 devices in a mesh: seq: 32 (over z_hi, x, core), chan: 16 (over z_lo, y).
Axes of the slice: x: 4, y: 4, z: 16 (z_hi: 4, z_lo: 4; z = z_hi * 4 + z_lo), core: 2. Of those that a mesh axis runs over, the one named last changes fastest.
Arguments:
- tokens: bfloat16 [3, 1024, 131072], P(None, 'chan', 'seq'), may hold values from -6 to 6
- kernel: bfloat16 [1024, 131072], P('chan', 'seq'), may hold values from -6 to 6
- left_factor: bfloat16 [512, 512], replicated, may hold values from -0.25 to 0.25
- right_factor: bfloat16 [256, 256], replicated, may hold values from -0.375 to 0.375
- norm_gain: float32 [1024], replicated, may hold values from 0.1 to 1.9
- up_weight: bfloat16 [4, 256, 1024], P(None, None, 'seq'), may hold values from -0.375 to 0.375
- down_weight: bfloat16 [4, 1024, 256], P(None, 'seq'), may hold values from -0.1875 to 0.1875
Outputs:
- layer_out: bfloat16 [3, 131072, 1024], P(None, ('seq', 'chan'))
All inputs are finite; a program needn't handle non-finite values.
Results may differ from a plain program's by a relative error of at most 0.0057.
Values may be sent and summed in bfloat16 or wider, within the bound.
No kernel may reach another device: no remote copies, remote signals or barrier semaphores. Data moves between devices by JAX's collectives and lax.ppermute only.
A program may use at most 64 MiB of HBM per device.

v0:
```python
import jax
import jax.numpy as jnp
from jax import lax
from jax.sharding import PartitionSpec as P


def per_device(tokens, kernel, left_factor, right_factor, norm_gain, up_weight, down_weight):
    blk = left_factor.shape[0]
    groups = up_weight.shape[0]
    nseq, chans, local_len = tokens.shape
    brows = local_len // blk
    x4 = tokens.reshape(nseq, chans, brows, blk)
    first = jnp.einsum("ncab,bj->ncaj", x4, left_factor, preferred_element_type=jnp.float32)
    middle = (first * kernel.reshape(1, chans, brows, blk).astype(jnp.float32)).astype(jnp.bfloat16)
    seqmix = jnp.einsum(
        "ncaj,ak->ncjk",
        lax.all_to_all(middle, "seq", split_axis=3, concat_axis=2, tiled=True),
        right_factor,
        preferred_element_type=jnp.float32,
    )
    xfloat = tokens.astype(jnp.float32)
    mixed = seqmix.reshape(nseq, chans, local_len)
    gated = (xfloat + jax.nn.sigmoid(xfloat) * mixed).astype(jnp.bfloat16)
    gathered = lax.all_to_all(gated, "chan", split_axis=2, concat_axis=1, tiled=True)
    width = gathered.shape[1]
    per_seq = gathered.shape[2]
    rows = gathered.transpose(0, 2, 1).reshape(nseq * per_seq, width)
    count = rows.shape[0]
    hfloat = rows.astype(jnp.float32)
    mean = jnp.mean(hfloat, axis=1, keepdims=True)
    var = jnp.mean((hfloat - mean) ** 2, axis=1, keepdims=True)
    normed = ((hfloat - mean) * lax.rsqrt(var + 1e-05) * norm_gain).astype(jnp.bfloat16)
    normed4 = normed.reshape(count, groups, width // groups)
    value = jnp.einsum(
        "tgr,grm->tgm",
        normed4,
        lax.all_gather(up_weight, "seq", axis=2, tiled=True),
        preferred_element_type=jnp.float32,
    )
    hidden = jax.nn.gelu(value).astype(jnp.bfloat16)
    regrouped = (
        hidden.reshape(count, groups, groups, width // groups)
        .transpose(0, 2, 1, 3)
        .reshape(count, groups, width)
    )
    down = jnp.einsum(
        "thn,hnr->thr",
        regrouped,
        lax.all_gather(down_weight, "seq", axis=1, tiled=True),
        preferred_element_type=jnp.float32,
    )
    result = (hfloat + down.reshape(count, width)).astype(jnp.bfloat16)
    return result.reshape(nseq, per_seq, width)


def solution(mesh):
    placed = (
        P(None, "chan", "seq"),
        P("chan", "seq"),
        P(),
        P(),
        P(),
        P(None, None, "seq"),
        P(None, "seq", None),
    )
    return jax.shard_map(
        per_device,
        mesh=mesh,
        in_specs=placed,
        out_specs=P(None, ("seq", "chan"), None),
        check_vma=False,
    )
```

profile of v0, /device:TPU:1, one launch (start us, length us, event | category | flops | bytes accessed | tf_op | source)
XLA Modules:
  0.0 351.4 jit_solution(10753072476404126404)
XLA Ops:
  6.5 0.0 copy-start
  6.5 2.1 copy.73
  8.7 0.2 copy.74
  8.9 1.0 multiply_convert_fusion.1
  9.9 4.2 %copy.57 = bf16[3,64,8,512]{1,2,0,3:T(8,128)(2,1)} copy(bf16[3,64,8,512]{3,2,1,0:T(8,128)(2,1)S(1)} %multiply_convert_fusion.1) | data formatting | bytes 3145728 | tf_op jit(solution)/shard_map/convert_element_type | solution.py:14
  14.0 5.3 %reshape.97 = bf16[32,2,12288]{2,1,0:T(2,128)(2,1)S(1)} reshape(bf16[512,3,8,64]{3,2,1,0:T(8,128)(2,1)} %bitcast.63) | data formatting | bytes 3145728
  19.3 93.9 %all_to_all.30 = bf16[32,2,12288]{2,1,0:T(2,128)(2,1)} all-to-all(bf16[32,2,12288]{2,1,0:T(2,128)(2,1)S(1)} %reshape.97), channel_id=1, replica_groups=mesh['seq'=32,'chan'=16] {'seq'}, dimensions={0} | all-to-all | bytes 3145728 | tf_op jit(solution)/shard_map/all_to_all | solution.py:17
  113.2 6.3 %reshape.98 = bf16[512,3,8,64]{3,2,1,0:T(8,128)(2,1)} reshape(bf16[32,2,12288]{2,1,0:T(2,128)(2,1)} %all_to_all.30) | data formatting | bytes 3145728
  119.5 4.6 %copy.59 = bf16[3,64,32,8,16]{1,4,3,2,0:T(8,128)(2,1)} copy(bf16[3,64,32,8,16]{1,3,0,4,2:T(8,128)(2,1)} %bitcast.64) | data formatting | bytes 3145728 | tf_op jit(solution)/shard_map/all_to_all | solution.py:17
  124.1 5.5 %copy.60 = bf16[3,64,256,16]{2,3,1,0:T(8,128)(2,1)S(1)} copy(bf16[3,64,256,16]{1,3,2,0:T(8,128)(2,1)} %bitcast.65) | data formatting | bytes 3145728 | tf_op jit(solution)/shard_map/all_to_all | solution.py:17
  129.6 0.0 copy-done.5
  129.6 2.2 fusion.16
  131.8 4.7 %reshape.85 = f32[3,64,4096]{2,1,0:T(8,128)} reshape(f32[3,64,16,256]{3,2,1,0:T(8,128)} %fusion.16) | data formatting | bytes 6291456 | tf_op jit(solution)/shard_map/reshape | solution.py:22
  136.6 0.0 copy-done.3
  136.6 4.0 %fusion.12 = bf16[3,64,4096]{2,1,0:T(8,128)(2,1)} fusion(f32[3,64,4096]{2,1,0:T(8,128)} %reshape.85, bf16[3,64,4096]{2,1,0:T(8,128)(2,1)S(1)} %copy-done.3), kind=kLoop, calls=%fused_computation.20 | loop fusion | flops 5505024 | bytes 6291456 | tf_op jit(solution)/shard_map/convert_element_type | solution.py:23
  140.5 6.4 %copy.61 = bf16[3,64,4096]{1,0,2:T(4,128)(2,1)} copy(bf16[3,64,4096]{2,1,0:T(8,128)(2,1)} %fusion.12) | data formatting | bytes 3145728 | tf_op jit(solution)/shard_map/convert_element_type | solution.py:23
  146.9 7.3 %reshape.99 = bf16[16,2,24576]{2,1,0:T(2,128)(2,1)} reshape(bf16[4096,3,64]{2,1,0:T(4,128)(2,1)} %bitcast.61) | data formatting | bytes 3145728
  154.2 9.6 %all-to-all-start.1 = ((bf16[16,2,24576]{2,1,0:T(2,128)(2,1)}), bf16[16,2,24576]{2,1,0:T(2,128)(2,1)S(1)}, u32[]{:S(2)}, u32[]{:S(2)}) async-start(bf16[16,2,24576]{2,1,0:T(2,128)(2,1)} %reshape.99), calls=%async_computation.1 | async-start | bytes 3145728 | tf_op jit(solution)/shard_map/all_to_all | solution.py:24
  163.7 0.0 all-gather.3.cloned.1.call-start
  163.8 0.7 all-gather.3.cloned.1.call-update
  164.5 0.2 all-gather.5.cloned.1.call-start
  164.7 0.5 all-gather.5.cloned.1.call-update
  165.2 0.0 copy-done.6
  165.2 34.9 %all-to-all-done.1 = bf16[16,2,24576]{2,1,0:T(2,128)(2,1)S(1)} async-done(((bf16[16,2,24576]{2,1,0:T(2,128)(2,1)}), bf16[16,2,24576]{2,1,0:T(2,128)(2,1)S(1)}, u32[]{:S(2)}, u32[]{:S(2)}) %all-to-all-start.1) | async-done | bytes 1572896 | tf_op jit(solution)/shard_map/all_to_all | solution.py:24
  200.1 4.7 %reshape.100 = bf16[4096,3,64]{2,1,0:T(4,128)(2,1)} reshape(bf16[16,2,24576]{2,1,0:T(2,128)(2,1)S(1)} %all-to-all-done.1) | data formatting | bytes 3145728
  204.9 5.5 %copy.62 = bf16[3,64,4096]{2,1,0:T(8,128)(2,1)S(1)} copy(bf16[3,64,4096]{1,0,2:T(4,128)(2,1)} %bitcast.62) | data formatting | bytes 3145728 | tf_op jit(solution)/shard_map/all_to_all | solution.py:24
  210.4 0.5 copy.75
  210.9 0.3 bitcast_bitcast_fusion
  211.2 1.8 copy.63
  213.1 0.0 copy-start.2
  213.1 1.6 copy-done.2
  214.7 0.2 bitcast_reduce_fusion
  214.9 2.4 multiply_reduce_fusion
  217.3 3.5 copy.64
  220.8 5.2 %reshape.90 = f32[768,4,256]{2,1,0:T(4,128)} reshape(f32[3,256,1024]{2,1,0:T(8,128)} %copy.64) | data formatting | bytes 6291456 | tf_op jit(solution)/shard_map/convert_element_type | solution.py:29
  226.0 4.5 %multiply_convert_fusion = bf16[768,4,256]{2,1,0:T(4,128)(2,1)S(1)} fusion(f32[768,4,256]{2,1,0:T(4,128)} %reshape.90, f32[4,256]{1,0:T(4,128)S(1)} %mul.57, f32[768]{0:T(1024)S(1)} %rsqrt.12, f32[768]{0:T(1024)S(1)} %div.13), kind=kLoop, calls=%fused_computation.17 | loop fusion | flops 3145728 | bytes 4728832 | tf_op jit(solution)/shard_map/convert_element_type | solution.py:32
  230.5 15.3 %all-gather.3.cloned.1.call-done = bf16[4,256,1024]{1,2,0:T(8,128)(2,1)} async-done(((bf16[4,256,32]{1,2,0:T(8,128)(2,1)}), bf16[4,256,1024]{1,2,0:T(8,128)(2,1)}) %all-gather.3.cloned.1.call-update) | async-done | bytes 2097168 | tf_op jit(solution)/shard_map/all_gather | solution.py:37
  245.9 7.8 %fusion.7 = bf16[768,4,1024]{2,0,1:T(8,128)(2,1)} fusion(bf16[4,256,1024]{1,2,0:T(8,128)(2,1)} %all-gather.3.cloned.1.call-done, bf16[768,4,256]{2,1,0:T(4,128)(2,1)S(1)} %multiply_convert_fusion), kind=kOutput, calls=%fused_computation.8 | convolution fusion | flops 1638924288 | bytes 9961472 | tf_op jit(solution)/shard_map/tgr,grm->tgm/dot_general | solution.py:34
  253.7 11.2 %reshape.86 = bf16[768,4,4,256]{3,2,0,1:T(4,128)(2,1)} reshape(bf16[768,4,1024]{2,0,1:T(8,128)(2,1)} %fusion.7) | data formatting | bytes 12582912 | tf_op jit(solution)/shard_map/reshape | solution.py:42
  264.9 10.3 %copy.66 = bf16[768,4,4,256]{3,2,0,1:T(4,128)(2,1)} copy(bf16[768,4,4,256]{3,1,0,2:T(4,128)(2,1)} %bitcast.60) | data formatting | bytes 12582912 | tf_op jit(solution)/shard_map/transpose | solution.py:43
  275.2 11.0 %reshape.87 = bf16[768,4,1024]{2,0,1:T(8,128)(2,1)} reshape(bf16[768,4,4,256]{3,2,0,1:T(4,128)(2,1)} %copy.66) | data formatting | bytes 12582912 | tf_op jit(solution)/shard_map/reshape | solution.py:44
  286.2 35.7 %all-gather.5.cloned.1.call-done = bf16[4,1024,256]{2,1,0:T(8,128)(2,1)} async-done(((bf16[4,32,256]{2,1,0:T(8,128)(2,1)}), bf16[4,1024,256]{2,1,0:T(8,128)(2,1)}) %all-gather.5.cloned.1.call-update) | async-done | bytes 2097168 | tf_op jit(solution)/shard_map/all_gather | solution.py:49
  321.9 5.2 %convolution_bitcast_fusion = f32[768,4,256]{2,0,1:T(8,128)S(1)} fusion(bf16[768,4,1024]{2,0,1:T(8,128)(2,1)} %reshape.87, bf16[4,1024,256]{2,1,0:T(8,128)(2,1)} %all-gather.5.cloned.1.call-done), kind=kOutput, calls=%fused_computation.21 | convolution fusion | flops 1610612736 | bytes 11534336 | tf_op jit(solution)/shard_map/thn,hnr->thr/dot_general | solution.py:46
  327.1 3.7 %copy.67 = f32[768,4,256]{2,1,0:T(4,128)} copy(f32[768,4,256]{2,0,1:T(8,128)S(1)} %convolution_bitcast_fusion) | data formatting | bytes 6291456 | tf_op jit(solution)/shard_map/thn,hnr->thr/transpose | solution.py:46
  330.8 5.2 %reshape.88 = f32[3,256,1024]{2,1,0:T(8,128)} reshape(f32[768,4,256]{2,1,0:T(4,128)} %copy.67) | data formatting | bytes 6291456 | tf_op jit(solution)/shard_map/reshape | solution.py:52
  336.0 3.6 %copy.68 = f32[3,256,1024]{1,2,0:T(8,128)} copy(f32[3,256,1024]{2,1,0:T(8,128)} %reshape.88) | data formatting | bytes 6291456 | tf_op jit(solution)/shard_map/reshape | solution.py:52
  339.6 3.2 add_convert_fusion
  342.8 1.7 copy.69
  (13 shorter events, 0.1 us)
Async XLA Ops:
  6.5 2.3 copy-start
  6.5 2.1 copy-start.4
  124.1 5.5 %copy-start.5 = (bf16[256,256]{1,0:T(8,128)(2,1)S(1)}, bf16[256,256]{1,0:T(8,128)(2,1)}, u32[]{:S(2)}) copy-start(bf16[256,256]{1,0:T(8,128)(2,1)} %param.10) | copy-start | bytes 393220
  131.8 4.7 %copy-start.3 = (bf16[3,64,4096]{2,1,0:T(8,128)(2,1)S(1)}, bf16[3,64,4096]{2,1,0:T(8,128)(2,1)}, u32[]{:S(2)}) copy-start(bf16[3,64,4096]{2,1,0:T(8,128)(2,1)} %param.7) | copy-start | bytes 4718596
  146.9 18.3 %copy-start.6 = (f32[1024]{0:T(1024)S(1)}, f32[1024]{0:T(1024)}, u32[]{:S(2)}) copy-start(f32[1024]{0:T(1024)} %param.11) | copy-start | bytes 12292
  154.2 46.0 %all-to-all-start.1 = ((bf16[16,2,24576]{2,1,0:T(2,128)(2,1)}), bf16[16,2,24576]{2,1,0:T(2,128)(2,1)S(1)}, u32[]{:S(2)}, u32[]{:S(2)}) async-start(bf16[16,2,24576]{2,1,0:T(2,128)(2,1)} %reshape.99), calls=%async_computation.1 | async-start | bytes 3145728 | tf_op jit(solution)/shard_map/all_to_all | solution.py:24
  163.7 82.1 %all-gather.3.cloned.1.call-start = ((), (), s32[]{:S(2)}) async-start(), calls=%async_computation.2 | async-start | bytes 2162688 | tf_op jit(solution)/shard_map/all_gather | solution.py:37
  164.5 157.4 %all-gather.5.cloned.1.call-start = ((), (), s32[]{:S(2)}) async-start(), calls=%async_computation.3 | async-start | bytes 2162688 | tf_op jit(solution)/shard_map/all_gather | solution.py:49
  213.1 1.6 copy-start.2
  339.6 5.0 %copy-start.1 = (bf16[512,512]{1,0:T(8,128)(2,1)S(1)}, bf16[512,512]{1,0:T(8,128)(2,1)}, u32[]{:S(2)}) copy-start(bf16[512,512]{1,0:T(8,128)(2,1)} %param.9) | copy-start | bytes 1572868
Sparse Core Ops, SparseCore 0:
  167.7 78.0 all-gather.2
  249.0 72.8 all-gather.4
where the time goes:
time: 353 us; the launch traced here: 351 us
  local copies, waits for them, and re-layouts  117 us (33%)
  blocking collectives  93.9 us (27%)
  waiting for transfers between devices  87.1 us (25%)
  matrix products  16.2 us (5%)
  other arithmetic  14.3 us (4%)
  between operations  13.6 us (4%)
  starting transfers between devices  9.82 us (3%)
    all_to_all x1, blocking collectives, per_device(): lax.all_to_all(middle, 'seq', split_axis=3, concat_axis=2, tiled=True)  93.9 us
    all_gather x1, waiting for transfers between devices, per_device(): lax.all_gather(down_weight, 'seq', axis=1, tiled=True)  35.7 us
    all_to_all x1, waiting for transfers between devices, per_device(): lax.all_to_all(gated, 'chan', split_axis=2, concat_axis=1, tiled=True)  34.9 us
    unnamed x21, local copies, waits for them, and re-layouts  28 us
    all_gather x1, waiting for transfers between devices, per_device(): lax.all_gather(up_weight, 'seq', axis=2, tiled=True)  15.3 us
    reshape x1, local copies, waits for them, and re-layouts, per_device(): hidden.reshape(count, groups, groups, width // groups).transpose(0, 2, 1, 3)  11.2 us
    reshape x1, local copies, waits for them, and re-layouts, per_device(): regrouped = hidden.reshape(count, groups, groups, width // groups).transp...  11 us
    convert_element_type x4, local copies, waits for them, and re-layouts, per_device(): hfloat = rows.astype(jnp.float32)  10.8 us
  transfers between devices with their start and end apart: 3, of which 3 were waited for; matrix products, arithmetic and copies ran while one was open for 20% of the time, Pallas kernels for 0%

commit v1 on v0

v1 whole, which is shorter than its diff:
```python
import jax
import jax.numpy as jnp
from jax import lax
from jax.experimental import pallas as pl
from jax.experimental.pallas import tpu as pltpu
from jax.sharding import PartitionSpec as P

F32 = jnp.float32
BF16 = jnp.bfloat16
SEQ = 32
CHAN = 16
ROWS = 8
BLK = 512
BROWS = 256
CH = 64
GROUPS = 4
PARAMS = pltpu.CompilerParams(vmem_limit_bytes=48 * 1024 * 1024)


def first_kernel(tok_ref, ker_ref, left_ref, out_ref, pair_ref, last_ref):
    left_t = left_ref[...].astype(F32).T.astype(BF16)

    def piece(ref, lead, a):
        if lead is None:
            return ref[:, a * BLK:(a + 1) * BLK]
        return ref[lead, :, a * BLK:(a + 1) * BLK]

    def matmul_t(x):
        return lax.dot_general(left_t, x, (((1,), (1,)), ((), ())), preferred_element_type=F32)

    for quad in range(ROWS // 4):
        rows = range(quad * 4, quad * 4 + 4)
        taps = jnp.concatenate([piece(ker_ref, None, a) for a in rows], axis=0).astype(F32).T
        prod = matmul_t(jnp.concatenate([piece(tok_ref, 2, a) for a in rows], axis=0)) * taps
        for i, a in enumerate(rows):
            one = prod[:, i * CH:(i + 1) * CH].reshape(SEQ, 2, 8, CH)
            for jh in range(2):
                last_ref[a * 256:(a + 1) * 256, jh * CH:(jh + 1) * CH] = one[:, jh].reshape(256, CH)
        for i in range(2):
            two = [quad * 4 + 2 * i, quad * 4 + 2 * i + 1]
            stacked = [piece(tok_ref, n, a) for a in two for n in range(2)]
            prod = matmul_t(jnp.concatenate(stacked, axis=0))
            for k, a in enumerate(two):
                tap = taps[:, (2 * i + k) * CH:(2 * i + k + 1) * CH]
                tap2 = jnp.concatenate([tap, tap], axis=1)
                pair_ref[a * BLK:(a + 1) * BLK, :] = prod[:, k * 128:(k + 1) * 128] * tap2
    for dst in range(SEQ):
        for jl in range(8):
            both = [pair_ref[pl.ds(dst * 16 + jh * 8 + jl, 8, stride=BLK), :] for jh in range(2)]
            out_ref[dst, :, jl * 128:(jl + 1) * 128] = jnp.concatenate(both, axis=0).astype(BF16)
        for jq in range(4):
            both = [last_ref[pl.ds(dst * 8 + jm * 4 + jq, 8, stride=256), :] for jm in range(2)]
            out_ref[dst, :, 1024 + jq * 128:1024 + (jq + 1) * 128] = jnp.concatenate(both, axis=0).astype(BF16)


def gate(x, mixed):
    x = x.astype(F32)
    return (x + (0.5 * jnp.tanh(0.5 * x) + 0.5) * mixed).astype(BF16)


def second_kernel(mid_ref, right_ref, tok_ref, out_ref):
    right = right_ref[...].astype(F32).reshape(SEQ, ROWS, BROWS)
    zero = jnp.zeros_like(right)
    upper = jnp.concatenate([right, zero], axis=1).reshape(512, BROWS)
    lower = jnp.concatenate([zero, right], axis=1).reshape(512, BROWS)
    wide = jnp.concatenate([upper, lower], axis=1).astype(BF16)

    def mix(at):
        rows = mid_ref[:, :, at * 128:(at + 1) * 128].reshape(512, 128)
        return lax.dot_general(rows, wide, (((0,), (0,)), ((), ())), preferred_element_type=F32)

    def put(n, j, value):
        x = tok_ref[n, :, j * BROWS:(j + 1) * BROWS]
        out_ref[j, :, n * BROWS:(n + 1) * BROWS] = gate(x, value)

    for jl in range(8):
        mixed = mix(jl)
        for n in range(2):
            for jh in range(2):
                put(n, jh * 8 + jl, mixed[n * CH:(n + 1) * CH, jh * BROWS:(jh + 1) * BROWS])
    for jq in range(4):
        mixed = mix(8 + jq)
        for jh in range(2):
            for jm in range(2):
                put(2, jh * 8 + jm * 4 + jq, mixed[jh * CH:(jh + 1) * CH, jm * BROWS:(jm + 1) * BROWS])


def mlp_kernel(x_ref, gain_ref, w_ref, out_ref):
    width = CHAN * CH
    x = x_ref[...].reshape(width, BROWS).astype(F32).T
    mean = jnp.mean(x, axis=1, keepdims=True)
    cent = x - mean
    var = jnp.mean(cent * cent, axis=1, keepdims=True)
    normed = (cent * lax.rsqrt(var + 1e-05) * gain_ref[...]).astype(BF16)
    acc = [None] * GROUPS
    for g in range(GROUPS):
        part = normed[:, g * 256:(g + 1) * 256]
        for h in range(GROUPS):
            up = w_ref[h * 8:(h + 1) * 8, 0, g].reshape(256, 256)
            value = lax.dot_general(part, up, (((1,), (1,)), ((), ())), preferred_element_type=F32)
            hidden = jax.nn.gelu(value).astype(BF16)
            down = w_ref[g * 8:(g + 1) * 8, 1, h].reshape(256, 256)
            term = jnp.dot(hidden, down, preferred_element_type=F32)
            acc[h] = term if acc[h] is None else acc[h] + term
    for h in range(GROUPS):
        out_ref[0, :, h * 256:(h + 1) * 256] = (x[:, h * 256:(h + 1) * 256] + acc[h]).astype(BF16)


def per_device(tokens, kernel, left_factor, right_factor, norm_gain, up_weight, down_weight):
    weights = jnp.stack([up_weight.transpose(0, 2, 1), down_weight])
    weights = lax.all_gather(weights, "seq", axis=0)
    middle = pl.pallas_call(
        first_kernel,
        out_shape=jax.ShapeDtypeStruct((SEQ, 16, 1536), BF16),
        scratch_shapes=[pltpu.VMEM((ROWS * BLK, 128), F32), pltpu.VMEM((ROWS * 256, 128), F32)],
        compiler_params=PARAMS,
        name="first",
    )(tokens, kernel, left_factor)
    middle = lax.all_to_all(middle, "seq", 0, 0, tiled=True)
    gated = pl.pallas_call(
        second_kernel,
        out_shape=jax.ShapeDtypeStruct((CHAN, CH, 3 * BROWS), BF16),
        compiler_params=PARAMS,
        name="second",
    )(middle, right_factor, tokens)
    gated = lax.all_to_all(gated, "chan", 0, 0, tiled=True)
    return pl.pallas_call(
        mlp_kernel,
        grid=(3,),
        in_specs=[
            pl.BlockSpec((CHAN, CH, BROWS), lambda n: (0, 0, n)),
            pl.BlockSpec((1, CHAN * CH), lambda n: (0, 0)),
            pl.BlockSpec((SEQ, 2, GROUPS, 32, 256), lambda n: (0, 0, 0, 0, 0)),
        ],
        out_specs=pl.BlockSpec((1, BROWS, CHAN * CH), lambda n: (n, 0, 0)),
        out_shape=jax.ShapeDtypeStruct((3, BROWS, CHAN * CH), BF16),
        compiler_params=PARAMS,
        name="mlp",
    )(gated, norm_gain.reshape(1, CHAN * CH), weights)


def solution(mesh):
    placed = (
        P(None, "chan", "seq"),
        P("chan", "seq"),
        P(),
        P(),
        P(),
        P(None, None, "seq"),
        P(None, "seq", None),
    )
    return jax.shard_map(
        per_device,
        mesh=mesh,
        in_specs=placed,
        out_specs=P(None, ("seq", "chan"), None),
        check_vma=False,
    )
```

time: 353 us -> 212 us (0.60)
  the two profiles are of different devices: /device:TPU:1 before, /device:TPU:64 now
where the time goes in v1:
time: 212 us
  waiting for transfers between devices  154 us (73%)
  starting transfers between devices  23.8 us (11%)
  Pallas kernels  14.4 us (7%)
  between operations  13.4 us (6%)
  local copies, waits for them, and re-layouts  5.7 us (3%)
    all_to_all x1, waiting for transfers between devices, per_device(): middle = lax.all_to_all(middle, 'seq', 0, 0, tiled=True)  82.9 us
    all_gather x1, waiting for transfers between devices, per_device(): weights = lax.all_gather(weights, 'seq', axis=0)  65 us
    all_to_all x1, starting transfers between devices, per_device(): middle = lax.all_to_all(middle, 'seq', 0, 0, tiled=True)  16.3 us
    pallas_call x1, Pallas kernels, per_device(): pl.pallas_call(mlp_kernel, grid=(3,), in_specs=[pl.BlockSpec((CHAN, CH, B...  8.1 us
    all_to_all x1, starting transfers between devices, per_device(): gated = lax.all_to_all(gated, 'chan', 0, 0, tiled=True)  7.44 us
    all_to_all x1, waiting for transfers between devices, per_device(): gated = lax.all_to_all(gated, 'chan', 0, 0, tiled=True)  6.21 us
    unnamed x18, local copies, waits for them, and re-layouts  5.7 us
  transfers between devices with their start and end apart: 3, of which 3 were waited for; matrix products, arithmetic and copies ran while one was open for 0% of the time, Pallas kernels for 1%

profile of v1, /device:TPU:64, one launch (start us, length us, event | category | flops | bytes accessed | tf_op | source)
XLA Modules:
  0.0 212.0 jit_solution(2190603061668312731)
XLA Ops:
  6.5 0.0 copy-start
  6.5 1.4 copy-done
  7.9 0.0 copy-start.3
  7.9 1.0 copy-done.3
  9.0 0.0 copy-start.4
  9.0 1.0 copy-done.4
  10.0 4.0 %first.1 = bf16[32,16,1536]{2,1,0:T(8,128)(2,1)} custom-call(bf16[3,64,4096]{2,1,0:T(8,128)(2,1)S(1)} %copy-done, bf16[64,4096]{1,0:T(8,128)(2,1)S(1)} %copy-done.3, bf16[512,512]{1,0:T(8,128)(2,1)S(1)} %copy-done.4), custom_call_target="tpu_custom_call" | custom-call | tf_op jit(solution)/shard_map/first/pallas_call | solution.py:112
  14.1 0.0 copy-start.7
  14.1 0.0 copy-start.8
  14.1 0.0 copy-start.1
  14.1 0.0 copy-start.5
  14.1 16.3 %all-to-all-start = ((bf16[32,16,1536]{2,1,0:T(8,128)(2,1)}), bf16[32,16,1536]{2,1,0:T(8,128)(2,1)S(1)}, u32[]{:S(2)}, u32[]{:S(2)}) async-start(bf16[32,16,1536]{2,1,0:T(8,128)(2,1)} %first.1), calls=%async_computation | async-start | bytes 3145728 | tf_op jit(solution)/shard_map/all_to_all | solution.py:119
  30.4 0.0 all-gather.3.cloned.1.call-start
  30.4 0.0 copy-done.7
  30.4 0.0 copy-done.8
  30.5 0.7 pad_maximum_fusion
  31.1 0.0 all-gather.3.cloned.1.call-update
  31.1 82.9 %all-to-all-done.mid_ref = bf16[32,16,1536]{2,1,0:T(8,128)(2,1)S(1)} async-done(((bf16[32,16,1536]{2,1,0:T(8,128)(2,1)}), bf16[32,16,1536]{2,1,0:T(8,128)(2,1)S(1)}, u32[]{:S(2)}, u32[]{:S(2)}) %all-to-all-start) | async-done | bytes 1572896 | tf_op jit(solution)/shard_map/all_to_all | solution.py:119
  114.0 0.0 copy-done.1
  114.0 0.0 copy-done.5
  114.0 2.2 %second.1 = bf16[16,64,768]{2,1,0:T(8,128)(2,1)} custom-call(bf16[32,16,1536]{2,1,0:T(8,128)(2,1)S(1)} %all-to-all-done.mid_ref, bf16[256,256]{1,0:T(8,128)(2,1)S(1)} %copy-done.5, bf16[3,64,4096]{2,1,0:T(8,128)(2,1)S(1)} %copy-done.1), custom_call_target="tpu_custom_call" | custom-call | tf_op jit(solution)/shard_map/second/pallas_call | solution.py:120
  116.2 0.0 copy-start.6
  116.2 7.4 %all-to-all-start.1 = ((bf16[16,64,768]{2,1,0:T(8,128)(2,1)}), bf16[16,64,768]{2,1,0:T(8,128)(2,1)S(1)}, u32[]{:S(2)}, u32[]{:S(2)}) async-start(bf16[16,64,768]{2,1,0:T(8,128)(2,1)} %second.1), calls=%async_computation.1 | async-start | bytes 3145728 | tf_op jit(solution)/shard_map/all_to_all | solution.py:126
  123.7 65.0 %all-gather.3.cloned.1.call-done = bf16[64,4,32,256]{3,2,1,0:T(8,128)(2,1)} async-done(((bf16[2,4,32,256]{3,2,1,0:T(8,128)(2,1)}), bf16[64,4,32,256]{3,2,1,0:T(8,128)(2,1)}) %all-gather.3.cloned.1.call-update) | async-done | bytes 4194320 | tf_op jit(solution)/shard_map/all_gather | solution.py:111
  188.7 6.2 %all-to-all-done.1.x_ref = bf16[16,64,768]{2,1,0:T(8,128)(2,1)S(1)} async-done(((bf16[16,64,768]{2,1,0:T(8,128)(2,1)}), bf16[16,64,768]{2,1,0:T(8,128)(2,1)S(1)}, u32[]{:S(2)}, u32[]{:S(2)}) %all-to-all-start.1) | async-done | bytes 1572896 | tf_op jit(solution)/shard_map/all_to_all | solution.py:126
  194.9 0.0 copy-done.6
  194.9 0.0 copy-start.2
  194.9 2.2 %copy-done.2 = bf16[64,4,32,256]{3,2,1,0:T(8,128)(2,1)S(1)} copy-done((bf16[64,4,32,256]{3,2,1,0:T(8,128)(2,1)S(1)}, bf16[64,4,32,256]{3,2,1,0:T(8,128)(2,1)}, u32[]{:S(2)}) %copy-start.2) | copy-done | bytes 4194328
  197.1 8.1 %mlp.1 = bf16[3,256,1024]{2,1,0:T(8,128)(2,1)} custom-call(bf16[16,64,768]{2,1,0:T(8,128)(2,1)S(1)} %all-to-all-done.1.x_ref, f32[1,1024]{1,0:T(1,128)S(1)} %bitcast.7, bf16[32,2,4,32,256]{4,3,2,1,0:T(8,128)(2,1)S(1)} %bitcast.6), custom_call_target="tpu_custom_call" | custom-call | tf_op jit(solution)/shard_map/mlp/pallas_call | solution.py:127
Async XLA Ops:
  6.5 1.4 copy-start
  7.9 1.0 copy-start.3
  9.0 1.0 copy-start.4
  14.1 16.4 %copy-start.7 = (bf16[4,32,256]{2,1,0:T(8,128)(2,1)S(1)}, bf16[4,32,256]{2,1,0:T(8,128)(2,1)}, u32[]{:S(2)}) copy-start(bf16[4,32,256]{2,1,0:T(8,128)(2,1)} %param.13) | copy-start | bytes 196612
  14.1 16.4 %copy-start.8 = (bf16[4,256,32]{1,2,0:T(8,128)(2,1)S(1)}, bf16[4,256,32]{1,2,0:T(8,128)(2,1)}, u32[]{:S(2)}) copy-start(bf16[4,256,32]{1,2,0:T(8,128)(2,1)} %param.12) | copy-start | bytes 196612
  14.1 99.9 %copy-start.1 = (bf16[3,64,4096]{2,1,0:T(8,128)(2,1)S(1)}, bf16[3,64,4096]{2,1,0:T(8,128)(2,1)}, u32[]{:S(2)}) copy-start(bf16[3,64,4096]{2,1,0:T(8,128)(2,1)} %tok_ref.3) | copy-start | bytes 4718596
  14.1 99.9 %copy-start.5 = (bf16[256,256]{1,0:T(8,128)(2,1)S(1)}, bf16[256,256]{1,0:T(8,128)(2,1)}, u32[]{:S(2)}) copy-start(bf16[256,256]{1,0:T(8,128)(2,1)} %right_ref.1) | copy-start | bytes 393220
  14.1 99.9 %all-to-all-start = ((bf16[32,16,1536]{2,1,0:T(8,128)(2,1)}), bf16[32,16,1536]{2,1,0:T(8,128)(2,1)S(1)}, u32[]{:S(2)}, u32[]{:S(2)}) async-start(bf16[32,16,1536]{2,1,0:T(8,128)(2,1)} %first.1), calls=%async_computation | async-start | bytes 3145728 | tf_op jit(solution)/shard_map/all_to_all | solution.py:119
  30.4 158.3 %all-gather.3.cloned.1.call-start = ((), (), s32[]{:S(2)}) async-start(), calls=%async_computation.2 | async-start | bytes 4325376 | tf_op jit(solution)/shard_map/all_gather | solution.py:111
  116.2 78.7 %copy-start.6 = (f32[1024]{0:T(1024)S(1)}, f32[1024]{0:T(1024)}, u32[]{:S(2)}) copy-start(f32[1024]{0:T(1024)} %param.11) | copy-start | bytes 12292
  116.2 78.6 %all-to-all-start.1 = ((bf16[16,64,768]{2,1,0:T(8,128)(2,1)}), bf16[16,64,768]{2,1,0:T(8,128)(2,1)S(1)}, u32[]{:S(2)}, u32[]{:S(2)}) async-start(bf16[16,64,768]{2,1,0:T(8,128)(2,1)} %second.1), calls=%async_computation.1 | async-start | bytes 3145728 | tf_op jit(solution)/shard_map/all_to_all | solution.py:126
  194.9 2.2 %copy-start.2 = (bf16[64,4,32,256]{3,2,1,0:T(8,128)(2,1)S(1)}, bf16[64,4,32,256]{3,2,1,0:T(8,128)(2,1)}, u32[]{:S(2)}) copy-start(bf16[64,4,32,256]{3,2,1,0:T(8,128)(2,1)} %all-gather.3.cloned.1.call-done) | copy-start | bytes 12582916
Sparse Core Ops, SparseCore 0:
  34.4 154.2 all-gather.2

commit v2 on v1

v2 whole, which is shorter than its diff:
```python
import jax
import jax.numpy as jnp
from jax import lax
from jax.experimental import pallas as pl
from jax.experimental.pallas import tpu as pltpu
from jax.sharding import PartitionSpec as P

F32 = jnp.float32
BF16 = jnp.bfloat16
SEQ = 32
CHAN = 16
ROWS = 8
BLK = 512
BROWS = 256
CH = 64
GROUPS = 4
SEQ_AXES = ("z_hi", "x", "core")
CHAN_AXES = ("z_lo", "y")
PARAMS = pltpu.CompilerParams(vmem_limit_bytes=60 * 1024 * 1024)
WEIGHTS = 128
ANY = pl.BlockSpec(memory_space=pl.ANY)


def rows_of(ref, lead, a):
    return ref[:, a * BLK:(a + 1) * BLK] if lead is None else ref[lead, :, a * BLK:(a + 1) * BLK]


def matmul_t(left_t, x):
    return lax.dot_general(left_t, x, (((1,), (1,)), ((), ())), preferred_element_type=F32)


def transposed(ref):
    return ref[...].astype(F32).T.astype(BF16)


def first_last_kernel(tok_ref, ker_ref, left_ref, up_ref, down_ref, *refs):
    *outs, work_ref = refs
    own_z, own_x, own_core = lax.axis_index("z_hi"), lax.axis_index("x"), lax.axis_index("core")
    left_t = transposed(left_ref)
    for quad in range(ROWS // 4):
        rows = range(quad * 4, quad * 4 + 4)
        taps = jnp.concatenate([rows_of(ker_ref, None, a) for a in rows], axis=0).astype(F32).T
        prod = matmul_t(left_t, jnp.concatenate([rows_of(tok_ref, 0, a) for a in rows], axis=0)) * taps
        for i, a in enumerate(rows):
            one = prod[:, i * CH:(i + 1) * CH].reshape(SEQ, 2, 8, CH)
            for jh in range(2):
                work_ref[a * 256:(a + 1) * 256, jh * CH:(jh + 1) * CH] = one[:, jh].reshape(256, CH)
    own_y = lax.axis_index("y")
    for step in range(4):
        for kind, ref in enumerate((up_ref, down_ref)):
            for i in range(2):
                outs[step][8 + kind, :, i * 256:(i + 1) * 256] = ref[own_y, i * 16:(i + 1) * 16, :]
        for x_step in range(4):
            for core_step in range(2):
                core = own_core if core_step == 0 else 1 - own_core
                dst = lax.rem(own_z + step, 4) * 8 + lax.rem(own_x + x_step, 4) * 2 + core
                for jq in range(4):
                    both = [work_ref[pl.ds(dst * 8 + (jm * 4 + jq), 8, stride=256), :] for jm in range(2)]
                    block = jnp.concatenate(both, axis=0).astype(BF16)
                    outs[step][x_step * 2 + core_step, :, jq * 128:(jq + 1) * 128] = block


def first_pair_kernel(tok_ref, ker_ref, left_ref, out_ref, work_ref):
    left_t = transposed(left_ref)
    for quad in range(ROWS // 4):
        rows = range(quad * 4, quad * 4 + 4)
        taps = jnp.concatenate([rows_of(ker_ref, None, a) for a in rows], axis=0).astype(F32).T
        for i in range(2):
            two = [quad * 4 + 2 * i, quad * 4 + 2 * i + 1]
            prod = matmul_t(left_t, jnp.concatenate([rows_of(tok_ref, n, a) for a in two for n in range(2)], axis=0))
            for k, a in enumerate(two):
                tap = taps[:, (2 * i + k) * CH:(2 * i + k + 1) * CH]
                tap2 = jnp.concatenate([tap, tap], axis=1)
                work_ref[a * BLK:(a + 1) * BLK, :] = prod[:, k * 128:(k + 1) * 128] * tap2
    for dst in range(SEQ):
        for jl in range(8):
            both = [work_ref[pl.ds(dst * 16 + jh * 8 + jl, 8, stride=BLK), :] for jh in range(2)]
            out_ref[dst, :, jl * 128:(jl + 1) * 128] = jnp.concatenate(both, axis=0).astype(BF16)


def z_join_kernel(*refs):
    parts, outs = refs[:4], refs[4:]
    for x_step, out in enumerate(outs):
        for step, part in enumerate(parts):
            for core_step in range(2):
                out[core_step * 4 + step] = part[x_step * 2 + core_step]
            out[8 + 2 * step:10 + 2 * step] = part[8:10]


def x_join_kernel(*refs):
    *parts, weights, blocks = refs
    for i, part in enumerate(parts):
        weights[8 * i:8 * i + 8] = part[8:16]
        blocks[4 * i:4 * i + 4] = part[4:8]


def y_join_kernel(*refs):
    *parts, out = refs
    for i, part in enumerate(parts):
        out[32 * i:32 * i + 32] = part[...]


def gate(x, mixed):
    x = x.astype(F32)
    return (x + (0.5 * jnp.tanh(0.5 * x) + 0.5) * mixed).astype(BF16)


def mix(rows, wide):
    return lax.dot_general(rows, wide, (((0,), (0,)), ((), ())), preferred_element_type=F32)


def second_last_kernel(*refs):
    parts, far_ref, right_ref, tok_ref, out_ref, wide_ref = refs[:4], *refs[4:]
    own_z, own_x, own_core = lax.axis_index("z_hi"), lax.axis_index("x"), lax.axis_index("core")
    wide_ref[...] = jnp.zeros_like(wide_ref)
    for i in range(32):
        core = own_core if i < 16 else 1 - own_core
        x, z = lax.rem(own_x + 4 - i // 4 % 4, 4), lax.rem(own_z + 4 - i % 4, 4)
        at = pl.multiple_of((z * 8 + x * 2 + core) * 8, 8)
        rows = right_ref[pl.ds(at, 8), :]
        wide_ref[i * 16:i * 16 + 8, :BROWS] = rows
        wide_ref[i * 16 + 8:i * 16 + 16, BROWS:] = rows
    wide = wide_ref[...].astype(BF16)
    for jq in range(4):
        lanes = slice(jq * 128, (jq + 1) * 128)
        rows = [part[:4, :, lanes].reshape(64, 128) for part in parts] + [far_ref[:, :, lanes].reshape(256, 128)]
        mixed = mix(jnp.concatenate(rows, axis=0), wide)
        for jh in range(2):
            for jm in range(2):
                j = jh * 8 + jm * 4 + jq
                x = tok_ref[0, :, j * BROWS:(j + 1) * BROWS]
                out_ref[j] = gate(x, mixed[jh * CH:(jh + 1) * CH, jm * BROWS:(jm + 1) * BROWS])


def second_pair_kernel(mid_ref, right_ref, tok_ref, kept_ref, out_ref):
    right = right_ref[...].reshape(SEQ, ROWS, BROWS)
    zero = jnp.zeros_like(right)
    upper = jnp.concatenate([right, zero], axis=1).reshape(512, BROWS)
    lower = jnp.concatenate([zero, right], axis=1).reshape(512, BROWS)
    wide = jnp.concatenate([upper, lower], axis=1).astype(BF16)
    for jl in range(8):
        mixed = mix(mid_ref[:, :, jl * 128:(jl + 1) * 128].reshape(512, 128), wide)
        for n in range(2):
            for jh in range(2):
                j = jh * 8 + jl
                x = tok_ref[n, :, j * BROWS:(j + 1) * BROWS]
                value = mixed[n * CH:(n + 1) * CH, jh * BROWS:(jh + 1) * BROWS]
                out_ref[j, :, n * BROWS:(n + 1) * BROWS] = gate(x, value)


def mlp_kernel(x_ref, gain_ref, near_ref, far_ref, out_ref):
    x = x_ref[...].reshape(CHAN * CH, BROWS).astype(F32).T
    mean = jnp.mean(x, axis=1, keepdims=True)
    cent = x - mean
    var = jnp.mean(cent * cent, axis=1, keepdims=True)
    normed = (cent * lax.rsqrt(var + 1e-05) * gain_ref[...]).astype(BF16)
    own_y, own_z = lax.axis_index("y"), lax.axis_index("z_hi")

    def weight(y, z, kind):
        base = lax.rem(own_y + 4 - y, 4) * 32 + lax.rem(own_z + 4 - z, 4) * 2 + kind
        blocks = [ref[base + x_step * 8] for ref in (near_ref, far_ref) for x_step in range(4)]
        return jnp.concatenate([block[:, i * 256:(i + 1) * 256] for block in blocks for i in range(2)], axis=0)

    acc = [None] * GROUPS
    for g in range(GROUPS):
        part = normed[:, g * 256:(g + 1) * 256]
        for h in range(GROUPS):
            value = matmul_t(part, weight(g, h, 0))
            hidden = jax.nn.gelu(value).astype(BF16)
            term = jnp.dot(hidden, weight(h, g, 1), preferred_element_type=F32)
            acc[h] = term if acc[h] is None else acc[h] + term
    for h in range(GROUPS):
        out_ref[0, :, h * 256:(h + 1) * 256] = (x[:, h * 256:(h + 1) * 256] + acc[h]).astype(BF16)


def shift(x, axis, step, size=4):
    return lax.ppermute(x, axis, [(i, (i + step) % size) for i in range(size)])


def spread(parts, axis):
    return [parts[0]] + [shift(parts[step], axis, step) for step in (1, 2, 3)]


def shape(*dims):
    return jax.ShapeDtypeStruct(dims, BF16)


def whole(*dims):
    return pl.BlockSpec(dims, lambda i: (0,) * len(dims))


def join(kernel, out_shape, name, *args, flops=0):
    return pl.pallas_call(
        kernel,
        out_shape=out_shape,
        compiler_params=PARAMS,
        cost_estimate=pl.CostEstimate(flops=flops, bytes_accessed=0, transcendentals=0),
        name=name,
    )(*args)


def per_device(tokens, kernel, left_factor, right_factor, norm_gain, up_weight, down_weight):
    chans = tokens.shape[1]
    local = tokens.shape[2]
    parts = pl.pallas_call(
        first_last_kernel,
        grid=(1,),
        in_specs=[
            pl.BlockSpec((1, chans, local), lambda i: (2, 0, 0)),
            whole(chans, local),
            whole(BLK, BLK),
            whole(GROUPS, 32, 256),
            whole(GROUPS, 32, 256),
        ],
        out_specs=[whole(10, 16, 512)] * 4,
        out_shape=[shape(10, 16, 512)] * 4,
        scratch_shapes=[pltpu.VMEM((ROWS * 256, 128), F32)],
        compiler_params=PARAMS,
        name="first_last",
    )(tokens, kernel, left_factor, up_weight.transpose(0, 2, 1), down_weight)
    parts = spread(parts, "z_hi")
    middle = pl.pallas_call(
        first_pair_kernel,
        grid=(1,),
        in_specs=[
            pl.BlockSpec((2, chans, local), lambda i: (0, 0, 0)),
            whole(chans, local),
            whole(BLK, BLK),
        ],
        out_specs=whole(SEQ, 16, 1024),
        out_shape=shape(SEQ, 16, 1024),
        scratch_shapes=[pltpu.VMEM((ROWS * BLK, 128), F32)],
        compiler_params=PARAMS,
        name="first_pair",
    )(tokens, kernel, left_factor)
    middle = lax.all_to_all(middle, SEQ_AXES, 0, 0, tiled=True)

    parts = join(z_join_kernel, [shape(16, 16, 512)] * 4, "z_join", *parts, flops=200 * 10**9)
    parts = spread(parts, "x")
    weights, blocks = join(x_join_kernel, [shape(32, 16, 512), shape(16, 16, 512)], "x_join", *parts)
    blocks = lax.ppermute(blocks, "core", [(0, 1), (1, 0)])
    near = join(y_join_kernel, shape(WEIGHTS, 16, 512), "y_join", *spread([weights] * 4, "y"), flops=200 * 10**9)
    far = lax.ppermute(near, "core", [(0, 1), (1, 0)])

    right = right_factor.astype(F32)
    gated = pl.pallas_call(
        second_last_kernel,
        grid=(1,),
        in_specs=[
            whole(16, 16, 512),
            whole(16, 16, 512),
            whole(16, 16, 512),
            whole(16, 16, 512),
            whole(16, 16, 512),
            whole(BROWS, BROWS),
            pl.BlockSpec((1, chans, local), lambda i: (2, 0, 0)),
        ],
        out_specs=pl.BlockSpec((CHAN, CH, BROWS), lambda i: (0, 0, 2)),
        out_shape=shape(CHAN, CH, 3 * BROWS),
        scratch_shapes=[pltpu.VMEM((512, 512), F32)],
        compiler_params=PARAMS,
        name="second_last",
    )(*parts, blocks, right, tokens)
    gated = pl.pallas_call(
        second_pair_kernel,
        grid=(1,),
        in_specs=[
            whole(SEQ, 16, 1024),
            whole(BROWS, BROWS),
            pl.BlockSpec((2, chans, local), lambda i: (0, 0, 0)),
            ANY,
        ],
        out_specs=pl.BlockSpec((CHAN, CH, 2 * BROWS), lambda i: (0, 0, 0)),
        out_shape=shape(CHAN, CH, 3 * BROWS),
        input_output_aliases={3: 0},
        compiler_params=PARAMS,
        name="second_pair",
    )(middle, right, tokens, gated)
    gated = lax.all_to_all(gated, CHAN_AXES, 0, 0, tiled=True)
    return pl.pallas_call(
        mlp_kernel,
        grid=(3,),
        in_specs=[
            pl.BlockSpec((CHAN, CH, BROWS), lambda n: (0, 0, n)),
            pl.BlockSpec((1, CHAN * CH), lambda n: (0, 0)),
            pl.BlockSpec((WEIGHTS, 16, 512), lambda n: (0, 0, 0)),
            pl.BlockSpec((WEIGHTS, 16, 512), lambda n: (0, 0, 0)),
        ],
        out_specs=pl.BlockSpec((1, BROWS, CHAN * CH), lambda n: (n, 0, 0)),
        out_shape=shape(3, BROWS, CHAN * CH),
        compiler_params=PARAMS,
        name="mlp",
    )(gated, norm_gain.reshape(1, CHAN * CH), near, far)


def solution(mesh):
    fine = jax.sharding.Mesh(mesh.devices.reshape(4, 4, 2, 4, 4), SEQ_AXES + CHAN_AXES)
    placed = (
        P(None, CHAN_AXES, SEQ_AXES),
        P(CHAN_AXES, SEQ_AXES),
        P(),
        P(),
        P(),
        P(None, None, SEQ_AXES),
        P(None, SEQ_AXES, None),
    )
    return jax.shard_map(
        per_device,
        mesh=fine,
        in_specs=placed,
        out_specs=P(None, SEQ_AXES + CHAN_AXES, None),
        check_vma=False,
    )
```

time: 212 us -> 161 us (0.76)
  the two profiles are of different devices: /device:TPU:64 before, /device:TPU:38 now
where the time goes in v2:
time: 161 us; the launch traced here: 160 us
  starting transfers between devices  73.7 us (46%)
  waiting for transfers between devices  49.6 us (31%)
  Pallas kernels  31.9 us (20%)
  local copies, waits for them, and re-layouts  3.77 us (2%)
    ppermute x9, starting transfers between devices, shift(): return lax.ppermute(x, axis, [(i, (i + step) % size) for i in range(size)])  43.6 us
    all_to_all x1, waiting for transfers between devices, per_device(): gated = lax.all_to_all(gated, CHAN_AXES, 0, 0, tiled=True)  25.6 us
    all_to_all x1, starting transfers between devices, per_device(): gated = lax.all_to_all(gated, CHAN_AXES, 0, 0, tiled=True)  19.5 us
    ppermute x9, waiting for transfers between devices, shift(): return lax.ppermute(x, axis, [(i, (i + step) % size) for i in range(size)])  15.9 us
    pallas_call x1, Pallas kernels, per_device(): pl.pallas_call(mlp_kernel, grid=(3,), in_specs=[pl.BlockSpec((CHAN, CH, B...  10.5 us
    pallas_call x3, Pallas kernels, join(): pl.pallas_call(kernel, out_shape=out_shape, compiler_params=PARAMS, cost_...  7.28 us
    all_to_all x1, starting transfers between devices, per_device(): middle = lax.all_to_all(middle, SEQ_AXES, 0, 0, tiled=True)  6.82 us
    pallas_call x1, Pallas kernels, per_device(): pl.pallas_call(first_pair_kernel, grid=(1,), in_specs=[pl.BlockSpec((2, c...  4.5 us
  transfers between devices with their start and end apart: 13, of which 8 were waited for; matrix products, arithmetic and copies ran while one was open for 0% of the time, Pallas kernels for 11%

profile of v2, /device:TPU:38, one launch (start us, length us, event | category | flops | bytes accessed | tf_op | source)
XLA Modules:
  0.0 160.0 jit_solution(7991727149759792246)
XLA Ops:
  0.0 3.4 %first_last.1 = (bf16[10,16,512]{2,1,0:T(8,128)(2,1)}, bf16[10,16,512]{2,1,0:T(8,128)(2,1)}, bf16[10,16,512]{2,1,0:T(8,128)(2,1)}, bf16[10,16,512]{2,1,0:T(8,128)(2,1)}) custom-call(bf16[3,64,4096]{2,1,0:T(8,128)(2,1)} %tok_ref.5, bf16[64,4096]{1,0:T(8,128)(2,1)} %ker_ref.3, bf16[512,512]{1,0:T(8,128)(2,1)} %left_ref.3, bf16[4,32,256]{2,1,0:T(8,128)(2,1)} %bitcast.2, ...), custom_call_target="tpu_custom_call" | custom-call | tf_op jit(solution)/shard_map/first_last/pallas_call | solution.py:205
  3.4 9.1 %collective-permute-start = (bf16[10,16,512]{2,1,0:T(8,128)(2,1)}, bf16[10,16,512]{2,1,0:T(8,128)(2,1)S(1)}, u32[]{:S(2)}, u32[]{:S(2)}) collective-permute-start(bf16[10,16,512]{2,1,0:T(8,128)(2,1)} %get-tuple-element.16), channel_id=1, source_target_pairs={{0,128},{128,256},{256,384},{384,0},{1,129},{129,257},{257,385},{3... | collective-permute-start | bytes 491528 | tf_op jit(solution)/shard_map/ppermute | solution.py:177
  12.5 10.0 %collective-permute-start.1 = (bf16[10,16,512]{2,1,0:T(8,128)(2,1)}, bf16[10,16,512]{2,1,0:T(8,128)(2,1)S(1)}, u32[]{:S(2)}, u32[]{:S(2)}) collective-permute-start(bf16[10,16,512]{2,1,0:T(8,128)(2,1)} %get-tuple-element.17), channel_id=1, source_target_pairs={{0,256},{128,384},{256,0},{384,128},{1,257},{129,385},{257,1},{385... | collective-permute-start | bytes 491528 | tf_op jit(solution)/shard_map/ppermute | solution.py:177
  22.5 5.5 %collective-permute-start.2 = (bf16[10,16,512]{2,1,0:T(8,128)(2,1)}, bf16[10,16,512]{2,1,0:T(8,128)(2,1)S(1)}, u32[]{:S(2)}, u32[]{:S(2)}) collective-permute-start(bf16[10,16,512]{2,1,0:T(8,128)(2,1)} %get-tuple-element.18), channel_id=1, source_target_pairs={{0,384},{128,0},{256,128},{384,256},{1,385},{129,1},{257,129},{385... | collective-permute-start | bytes 491528 | tf_op jit(solution)/shard_map/ppermute | solution.py:177
  28.0 4.5 %first_pair.1 = bf16[32,16,1024]{2,1,0:T(8,128)(2,1)} custom-call(bf16[3,64,4096]{2,1,0:T(8,128)(2,1)} %tok_ref.5, bf16[64,4096]{1,0:T(8,128)(2,1)} %ker_ref.3, bf16[512,512]{1,0:T(8,128)(2,1)} %left_ref.3), custom_call_target="tpu_custom_call" | custom-call | tf_op jit(solution)/shard_map/first_pair/pallas_call | solution.py:222
  32.5 6.8 %all-to-all-start = ((bf16[32,16,1024]{2,1,0:T(8,128)(2,1)}), bf16[32,16,1024]{2,1,0:T(8,128)(2,1)}, u32[]{:S(2)}, u32[]{:S(2)}) async-start(bf16[32,16,1024]{2,1,0:T(8,128)(2,1)} %first_pair.1), calls=%async_computation | async-start | bytes 2097152 | tf_op jit(solution)/shard_map/all_to_all | solution.py:236
  39.3 0.0 collective-permute-done.refs_1_
  39.3 0.0 copy-start.9
  39.3 0.0 collective-permute-done.1.refs_2_
  39.3 0.0 copy-start.10
  39.3 4.9 %collective-permute-done.2.refs_3_ = bf16[10,16,512]{2,1,0:T(8,128)(2,1)S(1)} collective-permute-done((bf16[10,16,512]{2,1,0:T(8,128)(2,1)}, bf16[10,16,512]{2,1,0:T(8,128)(2,1)S(1)}, u32[]{:S(2)}, u32[]{:S(2)}) %collective-permute-start.2) | collective-permute-done | bytes 163872 | tf_op jit(solution)/shard_map/ppermute | solution.py:177
  44.3 0.0 copy-done.9
  44.3 0.0 copy-done.10
  44.3 0.6 copy-done.11
  44.9 2.2 %z_join.1 = (bf16[16,16,512]{2,1,0:T(8,128)(2,1)}, bf16[16,16,512]{2,1,0:T(8,128)(2,1)}, bf16[16,16,512]{2,1,0:T(8,128)(2,1)}, bf16[16,16,512]{2,1,0:T(8,128)(2,1)}) custom-call(bf16[10,16,512]{2,1,0:T(8,128)(2,1)} %get-tuple-element.15.refs_0_, bf16[10,16,512]{2,1,0:T(8,128)(2,1)} %copy-done.9, bf16[10,16,512]{2,1,0:T(8,128)(2,1)} %copy-done.10, ...), custom_call_target="tpu_custom_call" | custom-call | flops 199999995904 | tf_op jit(solution)/shard_map/z_join/pallas_call | solution.py:193
  47.1 2.3 %collective-permute-start.3 = (bf16[16,16,512]{2,1,0:T(8,128)(2,1)}, bf16[16,16,512]{2,1,0:T(8,128)(2,1)S(1)}, u32[]{:S(2)}, u32[]{:S(2)}) collective-permute-start(bf16[16,16,512]{2,1,0:T(8,128)(2,1)} %get-tuple-element.20), channel_id=1, source_target_pairs={{0,32},{32,64},{64,96},{96,0},{1,33},{33,65},{65,97},{97,1},{2,34}... | collective-permute-start | bytes 786440 | tf_op jit(solution)/shard_map/ppermute | solution.py:177
  49.5 4.3 %collective-permute-start.4 = (bf16[16,16,512]{2,1,0:T(8,128)(2,1)}, bf16[16,16,512]{2,1,0:T(8,128)(2,1)S(1)}, u32[]{:S(2)}, u32[]{:S(2)}) collective-permute-start(bf16[16,16,512]{2,1,0:T(8,128)(2,1)} %get-tuple-element.21), channel_id=1, source_target_pairs={{0,64},{32,96},{64,0},{96,32},{1,65},{33,97},{65,1},{97,33},{2,66}... | collective-permute-start | bytes 786440 | tf_op jit(solution)/shard_map/ppermute | solution.py:177
  53.8 1.9 %collective-permute-start.5 = (bf16[16,16,512]{2,1,0:T(8,128)(2,1)}, bf16[16,16,512]{2,1,0:T(8,128)(2,1)S(1)}, u32[]{:S(2)}, u32[]{:S(2)}) collective-permute-start(bf16[16,16,512]{2,1,0:T(8,128)(2,1)} %get-tuple-element.22), channel_id=1, source_target_pairs={{0,96},{32,0},{64,32},{96,64},{1,97},{33,1},{65,33},{97,65},{2,98}... | collective-permute-start | bytes 786440 | tf_op jit(solution)/shard_map/ppermute | solution.py:177
  55.7 3.6 %collective-permute-done.3.refs_1_ = bf16[16,16,512]{2,1,0:T(8,128)(2,1)S(1)} collective-permute-done((bf16[16,16,512]{2,1,0:T(8,128)(2,1)}, bf16[16,16,512]{2,1,0:T(8,128)(2,1)S(1)}, u32[]{:S(2)}, u32[]{:S(2)}) %collective-permute-start.3) | collective-permute-done | bytes 262176 | tf_op jit(solution)/shard_map/ppermute | solution.py:177
  59.3 3.9 %collective-permute-done.4.refs_2_ = bf16[16,16,512]{2,1,0:T(8,128)(2,1)S(1)} collective-permute-done((bf16[16,16,512]{2,1,0:T(8,128)(2,1)}, bf16[16,16,512]{2,1,0:T(8,128)(2,1)S(1)}, u32[]{:S(2)}, u32[]{:S(2)}) %collective-permute-start.4) | collective-permute-done | bytes 262176 | tf_op jit(solution)/shard_map/ppermute | solution.py:177
  63.2 3.5 %collective-permute-done.5.refs_3_ = bf16[16,16,512]{2,1,0:T(8,128)(2,1)S(1)} collective-permute-done((bf16[16,16,512]{2,1,0:T(8,128)(2,1)}, bf16[16,16,512]{2,1,0:T(8,128)(2,1)S(1)}, u32[]{:S(2)}, u32[]{:S(2)}) %collective-permute-start.5) | collective-permute-done | bytes 262176 | tf_op jit(solution)/shard_map/ppermute | solution.py:177
  66.7 0.0 copy-done.1
  66.8 0.7 copy-done.3
  67.4 2.1 %x_join.1 = (bf16[32,16,512]{2,1,0:T(8,128)(2,1)}, bf16[16,16,512]{2,1,0:T(8,128)(2,1)}) custom-call(bf16[16,16,512]{2,1,0:T(8,128)(2,1)} %get-tuple-element.19.refs_0_, bf16[16,16,512]{2,1,0:T(8,128)(2,1)} %copy-done.1, bf16[16,16,512]{2,1,0:T(8,128)(2,1)} %copy-done.2, bf16[16,16,512]{2,1,0:T(8,128)(2,1)} %copy-done.3), custom_call_target="tpu_custom_call" | custom-call | tf_op jit(solution)/shard_map/x_join/pallas_call | solution.py:193
  69.5 5.1 %collective-permute-start.9 = (bf16[32,16,512]{2,1,0:T(8,128)(2,1)}, bf16[32,16,512]{2,1,0:T(8,128)(2,1)S(1)}, u32[]{:S(2)}, u32[]{:S(2)}) collective-permute-start(bf16[32,16,512]{2,1,0:T(8,128)(2,1)} %get-tuple-element.24.refs_0_), channel_id=1, source_target_pairs={{0,3},{1,0},{2,1},{3,2},{4,7},{5,4},{6,5},{7,6},{8,11},{9,8},{10,9... | collective-permute-start | bytes 1572872 | tf_op jit(solution)/shard_map/ppermute | solution.py:177
  74.6 2.6 %collective-permute-start.8 = (bf16[32,16,512]{2,1,0:T(8,128)(2,1)}, bf16[32,16,512]{2,1,0:T(8,128)(2,1)S(1)}, u32[]{:S(2)}, u32[]{:S(2)}) collective-permute-start(bf16[32,16,512]{2,1,0:T(8,128)(2,1)} %get-tuple-element.24.refs_0_), channel_id=1, source_target_pairs={{0,2},{1,3},{2,0},{3,1},{4,6},{5,7},{6,4},{7,5},{8,10},{9,11},{10,... | collective-permute-start | bytes 1572872 | tf_op jit(solution)/shard_map/ppermute | solution.py:177
  77.2 2.9 %collective-permute-start.7 = (bf16[32,16,512]{2,1,0:T(8,128)(2,1)}, bf16[32,16,512]{2,1,0:T(8,128)(2,1)S(1)}, u32[]{:S(2)}, u32[]{:S(2)}) collective-permute-start(bf16[32,16,512]{2,1,0:T(8,128)(2,1)} %get-tuple-element.24.refs_0_), channel_id=1, source_target_pairs={{0,1},{1,2},{2,3},{3,0},{4,5},{5,6},{6,7},{7,4},{8,9},{9,10},{10,1... | collective-permute-start | bytes 1572872 | tf_op jit(solution)/shard_map/ppermute | solution.py:177
  80.0 1.9 %collective-permute-start.6 = (bf16[16,16,512]{2,1,0:T(8,128)(2,1)}, bf16[16,16,512]{2,1,0:T(8,128)(2,1)S(1)}, u32[]{:S(2)}, u32[]{:S(2)}) collective-permute-start(bf16[16,16,512]{2,1,0:T(8,128)(2,1)} %get-tuple-element.23), channel_id=1, source_target_pairs={{0,16},{16,0},{1,17},{17,1},{2,18},{18,2},{3,19},{19,3},{4,20},{20... | collective-permute-start | bytes 786440 | tf_op jit(solution)/shard_map/ppermute | solution.py:241
  82.0 0.0 copy-done.5
  82.0 0.7 convert_element_type.3.refs_5_.right_ref
  82.7 1.0 collective-permute-done.6.refs_4_
  83.7 0.7 copy-done.4
  84.4 2.8 %second_last.1.kept_ref = bf16[16,64,768]{2,1,0:T(8,128)(2,1)} custom-call(bf16[16,16,512]{2,1,0:T(8,128)(2,1)} %get-tuple-element.19.refs_0_, bf16[16,16,512]{2,1,0:T(8,128)(2,1)} %copy-done.1, bf16[16,16,512]{2,1,0:T(8,128)(2,1)} %copy-done.2, bf16[16,16,512]{2,1,0:T(8,128)(2,1)} %copy-done.3, bf16[16,16,512]{2,1,0:T(8,128)(2,1)} %copy-done.4, ...), custom_call_target="tpu_custom_call" | custom-call | tf_op jit(solution)/shard_map/second_last/pallas_call | solution.py:246
  87.2 2.7 %all-to-all-done.mid_ref = bf16[32,16,1024]{2,1,0:T(8,128)(2,1)} async-done(((bf16[32,16,1024]{2,1,0:T(8,128)(2,1)}), bf16[32,16,1024]{2,1,0:T(8,128)(2,1)}, u32[]{:S(2)}, u32[]{:S(2)}) %all-to-all-start) | async-done | bytes 1048608 | tf_op jit(solution)/shard_map/all_to_all | solution.py:236
  89.9 3.4 %second_pair.1 = bf16[16,64,768]{2,1,0:T(8,128)(2,1)} custom-call(bf16[32,16,1024]{2,1,0:T(8,128)(2,1)} %all-to-all-done.mid_ref, f32[256,256]{1,0:T(8,128)} %convert_element_type.3.refs_5_.right_ref, bf16[3,64,4096]{2,1,0:T(8,128)(2,1)} %tok_ref.5, bf16[16,64,768]{2,1,0:T(8,128)(2,1)} %second_last.1.kept_ref), custom_call_target="tpu_custom_call", output_to_operand_aliasing={{}: (3, {})} | custom-call | tf_op jit(solution)/shard_map/second_pair/pallas_call | solution.py:264
  93.3 19.5 %all-to-all-start.1 = ((bf16[16,64,768]{2,1,0:T(8,128)(2,1)}), bf16[16,64,768]{2,1,0:T(8,128)(2,1)}, u32[]{:S(2)}, u32[]{:S(2)}) async-start(bf16[16,64,768]{2,1,0:T(8,128)(2,1)} %second_pair.1), calls=%async_computation.1 | async-start | bytes 3145728 | tf_op jit(solution)/shard_map/all_to_all | solution.py:279
  112.8 0.0 collective-permute-done.9.refs_3_
  112.8 0.0 collective-permute-done.8.refs_2_
  112.8 0.0 collective-permute-done.7.refs_1_
  112.8 0.7 copy-done.6
  113.6 0.2 copy-done.7
  113.8 0.8 copy-done.8
  114.6 3.0 %y_join.1.near_ref = bf16[128,16,512]{2,1,0:T(8,128)(2,1)} custom-call(bf16[32,16,512]{2,1,0:T(8,128)(2,1)} %get-tuple-element.24.refs_0_, bf16[32,16,512]{2,1,0:T(8,128)(2,1)} %copy-done.8, bf16[32,16,512]{2,1,0:T(8,128)(2,1)} %copy-done.7, bf16[32,16,512]{2,1,0:T(8,128)(2,1)} %copy-done.6), custom_call_target="tpu_custom_call" | custom-call | flops 199999995904 | tf_op jit(solution)/shard_map/y_join/pallas_call | solution.py:193
  117.5 1.9 %collective-permute-start.10 = (bf16[128,16,512]{2,1,0:T(8,128)(2,1)}, bf16[128,16,512]{2,1,0:T(8,128)(2,1)S(1)}, u32[]{:S(2)}, u32[]{:S(2)}) collective-permute-start(bf16[128,16,512]{2,1,0:T(8,128)(2,1)} %y_join.1.near_ref), channel_id=1, source_target_pairs={{0,16},{16,0},{1,17},{17,1},{2,18},{18,2},{3,19},{19,3},{4,20},{20... | collective-permute-start | bytes 6291464 | tf_op jit(solution)/shard_map/ppermute | solution.py:243
  119.5 4.3 %collective-permute-done.10.far_ref = bf16[128,16,512]{2,1,0:T(8,128)(2,1)S(1)} collective-permute-done((bf16[128,16,512]{2,1,0:T(8,128)(2,1)}, bf16[128,16,512]{2,1,0:T(8,128)(2,1)S(1)}, u32[]{:S(2)}, u32[]{:S(2)}) %collective-permute-start.10) | collective-permute-done | bytes 2097184 | tf_op jit(solution)/shard_map/ppermute | solution.py:243
  123.8 25.6 %all-to-all-done.1.x_ref = bf16[16,64,768]{2,1,0:T(8,128)(2,1)} async-done(((bf16[16,64,768]{2,1,0:T(8,128)(2,1)}), bf16[16,64,768]{2,1,0:T(8,128)(2,1)}, u32[]{:S(2)}, u32[]{:S(2)}) %all-to-all-start.1) | async-done | bytes 1572896 | tf_op jit(solution)/shard_map/all_to_all | solution.py:279
  149.4 0.0 copy-done
  149.4 10.5 %mlp.1 = bf16[3,256,1024]{2,1,0:T(8,128)(2,1)} custom-call(bf16[16,64,768]{2,1,0:T(8,128)(2,1)} %all-to-all-done.1.x_ref, f32[1,1024]{1,0:T(1,128)} %bitcast.3, bf16[128,16,512]{2,1,0:T(8,128)(2,1)} %y_join.1.near_ref, bf16[128,16,512]{2,1,0:T(8,128)(2,1)} %copy-done), custom_call_target="tpu_custom_call" | custom-call | tf_op jit(solution)/shard_map/mlp/pallas_call | solution.py:280
  (11 shorter events, 0.0 us)
Async XLA Ops:
  3.4 35.9 %collective-permute-start = (bf16[10,16,512]{2,1,0:T(8,128)(2,1)}, bf16[10,16,512]{2,1,0:T(8,128)(2,1)S(1)}, u32[]{:S(2)}, u32[]{:S(2)}) collective-permute-start(bf16[10,16,512]{2,1,0:T(8,128)(2,1)} %get-tuple-element.16), channel_id=1, source_target_pairs={{0,128},{128,256},{256,384},{384,0},{1,129},{129,257},{257,385},{3... | collective-permute-start | bytes 491528 | tf_op jit(solution)/shard_map/ppermute | solution.py:177
  12.5 26.8 %collective-permute-start.1 = (bf16[10,16,512]{2,1,0:T(8,128)(2,1)}, bf16[10,16,512]{2,1,0:T(8,128)(2,1)S(1)}, u32[]{:S(2)}, u32[]{:S(2)}) collective-permute-start(bf16[10,16,512]{2,1,0:T(8,128)(2,1)} %get-tuple-element.17), channel_id=1, source_target_pairs={{0,256},{128,384},{256,0},{384,128},{1,257},{129,385},{257,1},{385... | collective-permute-start | bytes 491528 | tf_op jit(solution)/shard_map/ppermute | solution.py:177
  22.5 21.8 %collective-permute-start.2 = (bf16[10,16,512]{2,1,0:T(8,128)(2,1)}, bf16[10,16,512]{2,1,0:T(8,128)(2,1)S(1)}, u32[]{:S(2)}, u32[]{:S(2)}) collective-permute-start(bf16[10,16,512]{2,1,0:T(8,128)(2,1)} %get-tuple-element.18), channel_id=1, source_target_pairs={{0,384},{128,0},{256,128},{384,256},{1,385},{129,1},{257,129},{385... | collective-permute-start | bytes 491528 | tf_op jit(solution)/shard_map/ppermute | solution.py:177
  32.5 57.4 %all-to-all-start = ((bf16[32,16,1024]{2,1,0:T(8,128)(2,1)}), bf16[32,16,1024]{2,1,0:T(8,128)(2,1)}, u32[]{:S(2)}, u32[]{:S(2)}) async-start(bf16[32,16,1024]{2,1,0:T(8,128)(2,1)} %first_pair.1), calls=%async_computation | async-start | bytes 2097152 | tf_op jit(solution)/shard_map/all_to_all | solution.py:236
  39.3 5.0 %copy-start.9 = (bf16[10,16,512]{2,1,0:T(8,128)(2,1)}, bf16[10,16,512]{2,1,0:T(8,128)(2,1)S(1)}, u32[]{:S(2)}) copy-start(bf16[10,16,512]{2,1,0:T(8,128)(2,1)S(1)} %collective-permute-done.refs_1_) | copy-start | bytes 491524
  39.3 4.9 %copy-start.10 = (bf16[10,16,512]{2,1,0:T(8,128)(2,1)}, bf16[10,16,512]{2,1,0:T(8,128)(2,1)S(1)}, u32[]{:S(2)}) copy-start(bf16[10,16,512]{2,1,0:T(8,128)(2,1)S(1)} %collective-permute-done.1.refs_2_) | copy-start | bytes 491524
  44.3 0.7 copy-start.11
  44.9 37.0 %copy-start.5 = (bf16[256,256]{1,0:T(8,128)(2,1)S(1)}, bf16[256,256]{1,0:T(8,128)(2,1)}, u32[]{:S(2)}) copy-start(bf16[256,256]{1,0:T(8,128)(2,1)} %param.10) | copy-start | bytes 393220
  47.1 12.2 %collective-permute-start.3 = (bf16[16,16,512]{2,1,0:T(8,128)(2,1)}, bf16[16,16,512]{2,1,0:T(8,128)(2,1)S(1)}, u32[]{:S(2)}, u32[]{:S(2)}) collective-permute-start(bf16[16,16,512]{2,1,0:T(8,128)(2,1)} %get-tuple-element.20), channel_id=1, source_target_pairs={{0,32},{32,64},{64,96},{96,0},{1,33},{33,65},{65,97},{97,1},{2,34}... | collective-permute-start | bytes 786440 | tf_op jit(solution)/shard_map/ppermute | solution.py:177
  49.5 13.8 %collective-permute-start.4 = (bf16[16,16,512]{2,1,0:T(8,128)(2,1)}, bf16[16,16,512]{2,1,0:T(8,128)(2,1)S(1)}, u32[]{:S(2)}, u32[]{:S(2)}) collective-permute-start(bf16[16,16,512]{2,1,0:T(8,128)(2,1)} %get-tuple-element.21), channel_id=1, source_target_pairs={{0,64},{32,96},{64,0},{96,32},{1,65},{33,97},{65,1},{97,33},{2,66}... | collective-permute-start | bytes 786440 | tf_op jit(solution)/shard_map/ppermute | solution.py:177
  53.8 12.9 %collective-permute-start.5 = (bf16[16,16,512]{2,1,0:T(8,128)(2,1)}, bf16[16,16,512]{2,1,0:T(8,128)(2,1)S(1)}, u32[]{:S(2)}, u32[]{:S(2)}) collective-permute-start(bf16[16,16,512]{2,1,0:T(8,128)(2,1)} %get-tuple-element.22), channel_id=1, source_target_pairs={{0,96},{32,0},{64,32},{96,64},{1,97},{33,1},{65,33},{97,65},{2,98}... | collective-permute-start | bytes 786440 | tf_op jit(solution)/shard_map/ppermute | solution.py:177
  59.3 7.4 %copy-start.1 = (bf16[16,16,512]{2,1,0:T(8,128)(2,1)}, bf16[16,16,512]{2,1,0:T(8,128)(2,1)S(1)}, u32[]{:S(2)}) copy-start(bf16[16,16,512]{2,1,0:T(8,128)(2,1)S(1)} %collective-permute-done.3.refs_1_) | copy-start | bytes 786436
  63.2 3.5 %copy-start.2 = (bf16[16,16,512]{2,1,0:T(8,128)(2,1)}, bf16[16,16,512]{2,1,0:T(8,128)(2,1)S(1)}, u32[]{:S(2)}) copy-start(bf16[16,16,512]{2,1,0:T(8,128)(2,1)S(1)} %collective-permute-done.4.refs_2_) | copy-start | bytes 786436
  66.7 0.7 copy-start.3
  69.5 43.3 %collective-permute-start.9 = (bf16[32,16,512]{2,1,0:T(8,128)(2,1)}, bf16[32,16,512]{2,1,0:T(8,128)(2,1)S(1)}, u32[]{:S(2)}, u32[]{:S(2)}) collective-permute-start(bf16[32,16,512]{2,1,0:T(8,128)(2,1)} %get-tuple-element.24.refs_0_), channel_id=1, source_target_pairs={{0,3},{1,0},{2,1},{3,2},{4,7},{5,4},{6,5},{7,6},{8,11},{9,8},{10,9... | collective-permute-start | bytes 1572872 | tf_op jit(solution)/shard_map/ppermute | solution.py:177
  74.6 38.2 %collective-permute-start.8 = (bf16[32,16,512]{2,1,0:T(8,128)(2,1)}, bf16[32,16,512]{2,1,0:T(8,128)(2,1)S(1)}, u32[]{:S(2)}, u32[]{:S(2)}) collective-permute-start(bf16[32,16,512]{2,1,0:T(8,128)(2,1)} %get-tuple-element.24.refs_0_), channel_id=1, source_target_pairs={{0,2},{1,3},{2,0},{3,1},{4,6},{5,7},{6,4},{7,5},{8,10},{9,11},{10,... | collective-permute-start | bytes 1572872 | tf_op jit(solution)/shard_map/ppermute | solution.py:177
  77.2 35.7 %collective-permute-start.7 = (bf16[32,16,512]{2,1,0:T(8,128)(2,1)}, bf16[32,16,512]{2,1,0:T(8,128)(2,1)S(1)}, u32[]{:S(2)}, u32[]{:S(2)}) collective-permute-start(bf16[32,16,512]{2,1,0:T(8,128)(2,1)} %get-tuple-element.24.refs_0_), channel_id=1, source_target_pairs={{0,1},{1,2},{2,3},{3,0},{4,5},{5,6},{6,7},{7,4},{8,9},{9,10},{10,1... | collective-permute-start | bytes 1572872 | tf_op jit(solution)/shard_map/ppermute | solution.py:177
  80.0 3.6 %collective-permute-start.6 = (bf16[16,16,512]{2,1,0:T(8,128)(2,1)}, bf16[16,16,512]{2,1,0:T(8,128)(2,1)S(1)}, u32[]{:S(2)}, u32[]{:S(2)}) collective-permute-start(bf16[16,16,512]{2,1,0:T(8,128)(2,1)} %get-tuple-element.23), channel_id=1, source_target_pairs={{0,16},{16,0},{1,17},{17,1},{2,18},{18,2},{3,19},{19,3},{4,20},{20... | collective-permute-start | bytes 786440 | tf_op jit(solution)/shard_map/ppermute | solution.py:241
  83.7 0.7 copy-start.4
  93.3 56.1 %all-to-all-start.1 = ((bf16[16,64,768]{2,1,0:T(8,128)(2,1)}), bf16[16,64,768]{2,1,0:T(8,128)(2,1)}, u32[]{:S(2)}, u32[]{:S(2)}) async-start(bf16[16,64,768]{2,1,0:T(8,128)(2,1)} %second_pair.1), calls=%async_computation.1 | async-start | bytes 3145728 | tf_op jit(solution)/shard_map/all_to_all | solution.py:279
  112.8 0.8 copy-start.6
  112.8 0.9 copy-start.7
  113.8 0.8 copy-start.8
  117.5 6.3 %collective-permute-start.10 = (bf16[128,16,512]{2,1,0:T(8,128)(2,1)}, bf16[128,16,512]{2,1,0:T(8,128)(2,1)S(1)}, u32[]{:S(2)}, u32[]{:S(2)}) collective-permute-start(bf16[128,16,512]{2,1,0:T(8,128)(2,1)} %y_join.1.near_ref), channel_id=1, source_target_pairs={{0,16},{16,0},{1,17},{17,1},{2,18},{18,2},{3,19},{19,3},{4,20},{20... | collective-permute-start | bytes 6291464 | tf_op jit(solution)/shard_map/ppermute | solution.py:243
  123.8 25.7 %copy-start = (bf16[128,16,512]{2,1,0:T(8,128)(2,1)}, bf16[128,16,512]{2,1,0:T(8,128)(2,1)S(1)}, u32[]{:S(2)}) copy-start(bf16[128,16,512]{2,1,0:T(8,128)(2,1)S(1)} %collective-permute-done.10.far_ref) | copy-start | bytes 6291460

commit v3 on v2

--- a/solution.py
+++ b/solution.py
@@ -17,6 +17,7 @@
 SEQ_AXES = ("z_hi", "x", "core")
 CHAN_AXES = ("z_lo", "y")
 PARAMS = pltpu.CompilerParams(vmem_limit_bytes=60 * 1024 * 1024)
+SMALL = pltpu.CompilerParams(vmem_limit_bytes=24 * 1024 * 1024)
 WEIGHTS = 128
 ANY = pl.BlockSpec(memory_space=pl.ANY)
 
@@ -79,25 +80,27 @@
 
 
 def z_join_kernel(*refs):
-    parts, outs = refs[:4], refs[4:]
-    for x_step, out in enumerate(outs):
-        for step, part in enumerate(parts):
+    parts, outs, weights = refs[:4], refs[4:8], refs[8]
+    for step, part in enumerate(parts):
+        for x_step, out in enumerate(outs):
             for core_step in range(2):
                 out[core_step * 4 + step] = part[x_step * 2 + core_step]
-            out[8 + 2 * step:10 + 2 * step] = part[8:10]
-
-
-def x_join_kernel(*refs):
-    *parts, weights, blocks = refs
+        weights[2 * step:2 * step + 2] = part[8:10]
+
+
+def plane_join_kernel(*refs):
+    parts, weights, out, joined = refs[:4], refs[4:8], refs[8], refs[9]
     for i, part in enumerate(parts):
-        weights[8 * i:8 * i + 8] = part[8:16]
-        blocks[4 * i:4 * i + 4] = part[4:8]
-
-
-def y_join_kernel(*refs):
+        out[4 * i:4 * i + 4] = part[4:8]
+    for i, part in enumerate(weights):
+        joined[8 * i:8 * i + 8] = part[...]
+
+
+def join_kernel(*refs):
     *parts, out = refs
+    size = parts[0].shape[0]
     for i, part in enumerate(parts):
-        out[32 * i:32 * i + 32] = part[...]
+        out[size * i:size * (i + 1)] = part[...]
 
 
 def gate(x, mixed):
@@ -110,17 +113,21 @@
 
 
 def second_last_kernel(*refs):
-    parts, far_ref, right_ref, tok_ref, out_ref, wide_ref = refs[:4], *refs[4:]
+    parts, far_ref, right_ref, tok_hbm, out_ref, wide_ref, copy_ref, tok_ref, sem = refs[:4], *refs[4:]
     own_z, own_x, own_core = lax.axis_index("z_hi"), lax.axis_index("x"), lax.axis_index("core")
+    load = pltpu.make_async_copy(tok_hbm.at[2], tok_ref, sem)
+    load.start()
     wide_ref[...] = jnp.zeros_like(wide_ref)
+    copy_ref[...] = right_ref[...].astype(F32)
     for i in range(32):
         core = own_core if i < 16 else 1 - own_core
         x, z = lax.rem(own_x + 4 - i // 4 % 4, 4), lax.rem(own_z + 4 - i % 4, 4)
         at = pl.multiple_of((z * 8 + x * 2 + core) * 8, 8)
-        rows = right_ref[pl.ds(at, 8), :]
+        rows = copy_ref[pl.ds(at, 8), :]
         wide_ref[i * 16:i * 16 + 8, :BROWS] = rows
         wide_ref[i * 16 + 8:i * 16 + 16, BROWS:] = rows
     wide = wide_ref[...].astype(BF16)
+    load.wait()
     for jq in range(4):
         lanes = slice(jq * 128, (jq + 1) * 128)
         rows = [part[:4, :, lanes].reshape(64, 128) for part in parts] + [far_ref[:, :, lanes].reshape(256, 128)]
@@ -128,12 +135,12 @@
         for jh in range(2):
             for jm in range(2):
                 j = jh * 8 + jm * 4 + jq
-                x = tok_ref[0, :, j * BROWS:(j + 1) * BROWS]
-                out_ref[j] = gate(x, mixed[jh * CH:(jh + 1) * CH, jm * BROWS:(jm + 1) * BROWS])
+                x = tok_ref[:, j * BROWS:(j + 1) * BROWS]
+                out_ref[jh, jm * 4 + jq] = gate(x, mixed[jh * CH:(jh + 1) * CH, jm * BROWS:(jm + 1) * BROWS])
 
 
 def second_pair_kernel(mid_ref, right_ref, tok_ref, kept_ref, out_ref):
-    right = right_ref[...].reshape(SEQ, ROWS, BROWS)
+    right = right_ref[...].astype(F32).reshape(SEQ, ROWS, BROWS)
     zero = jnp.zeros_like(right)
     upper = jnp.concatenate([right, zero], axis=1).reshape(512, BROWS)
     lower = jnp.concatenate([zero, right], axis=1).reshape(512, BROWS)
@@ -145,32 +152,59 @@
                 j = jh * 8 + jl
                 x = tok_ref[n, :, j * BROWS:(j + 1) * BROWS]
                 value = mixed[n * CH:(n + 1) * CH, jh * BROWS:(jh + 1) * BROWS]
-                out_ref[j, :, n * BROWS:(n + 1) * BROWS] = gate(x, value)
-
-
-def mlp_kernel(x_ref, gain_ref, near_ref, far_ref, out_ref):
-    x = x_ref[...].reshape(CHAN * CH, BROWS).astype(F32).T
-    mean = jnp.mean(x, axis=1, keepdims=True)
-    cent = x - mean
-    var = jnp.mean(cent * cent, axis=1, keepdims=True)
-    normed = (cent * lax.rsqrt(var + 1e-05) * gain_ref[...]).astype(BF16)
+                out_ref[jh, jl, :, n * BROWS:(n + 1) * BROWS] = gate(x, value)
+
+
+def twice_gelu(x):
+    return x + x * jnp.tanh(x * (0.7978845608028654 + 0.035677408136300125 * (x * x)))
+
+
+def mlp_kernel(x_hbm, gain_ref, near_hbm, far_hbm, out_hbm, x_ref, rows_ref, normed_ref, out_ref, weight_ref, *sems):
+    in_sems, weight_sems, out_sems = sems
+    loads = [
+        pltpu.make_async_copy(x_hbm.at[:, :, pl.ds(n * BROWS, BROWS)], x_ref.at[n], in_sems.at[n]) for n in range(3)
+    ]
+    weights = [
+        pltpu.make_async_copy(share, weight_ref.at[pl.ds(core * WEIGHTS, WEIGHTS)], weight_sems.at[core])
+        for core, share in enumerate((near_hbm, far_hbm))
+    ]
+    for load in loads + weights:
+        load.start()
+    for n, load in enumerate(loads):
+        load.wait()
+        rows = x_ref[n].reshape(CHAN * CH, BROWS).T
+        x = rows.astype(F32)
+        mean = jnp.mean(x, axis=1, keepdims=True)
+        cent = x - mean
+        var = jnp.mean(cent * cent, axis=1, keepdims=True)
+        normed = (cent * lax.rsqrt(var + 1e-05) * gain_ref[...]).astype(BF16)
+        rows_ref[n * BROWS:(n + 1) * BROWS, :] = rows
+        normed_ref[n * BROWS:(n + 1) * BROWS, :] = normed
     own_y, own_z = lax.axis_index("y"), lax.axis_index("z_hi")
 
     def weight(y, z, kind):
-        base = lax.rem(own_y + 4 - y, 4) * 32 + lax.rem(own_z + 4 - z, 4) * 2 + kind
-        blocks = [ref[base + x_step * 8] for ref in (near_ref, far_ref) for x_step in range(4)]
+        base = lax.rem(own_y + 4 - y, 4) * 8 + lax.rem(own_z + 4 - z, 4) * 2 + kind
+        blocks = [weight_ref[base + step * 32] for step in range(8)]
         return jnp.concatenate([block[:, i * 256:(i + 1) * 256] for block in blocks for i in range(2)], axis=0)
 
-    acc = [None] * GROUPS
-    for g in range(GROUPS):
-        part = normed[:, g * 256:(g + 1) * 256]
-        for h in range(GROUPS):
-            value = matmul_t(part, weight(g, h, 0))
-            hidden = jax.nn.gelu(value).astype(BF16)
-            term = jnp.dot(hidden, weight(h, g, 1), preferred_element_type=F32)
-            acc[h] = term if acc[h] is None else acc[h] + term
+    for load in weights:
+        load.wait()
+    stores = []
     for h in range(GROUPS):
-        out_ref[0, :, h * 256:(h + 1) * 256] = (x[:, h * 256:(h + 1) * 256] + acc[h]).astype(BF16)
+        lanes = slice(h * 256, (h + 1) * 256)
+        hidden = [
+            twice_gelu(matmul_t(normed_ref[:, g * 256:(g + 1) * 256], weight(g, h, 0))).astype(BF16)
+            for g in range(GROUPS)
+        ]
+        down = jnp.concatenate([weight(h, g, 1) for g in range(GROUPS)], axis=0)
+        acc = jnp.dot(jnp.concatenate(hidden, axis=1), down, preferred_element_type=F32)
+        out = (rows_ref[:, lanes].astype(F32) + 0.5 * acc).astype(BF16)
+        out_ref[:, :, lanes] = out.reshape(3, BROWS, 256)
+        at = pl.ds(h * 256, 256)
+        stores.append(pltpu.make_async_copy(out_ref.at[:, :, at], out_hbm.at[:, :, at], out_sems.at[h]))
+        stores[h].start()
+    for store in stores:
+        store.wait()
 
 
 def shift(x, axis, step, size=4):
@@ -193,7 +227,7 @@
     return pl.pallas_call(
         kernel,
         out_shape=out_shape,
-        compiler_params=PARAMS,
+        compiler_params=pltpu.CompilerParams(vmem_limit_bytes=16 * 1024 * 1024),
         cost_estimate=pl.CostEstimate(flops=flops, bytes_accessed=0, transcendentals=0),
         name=name,
     )(*args)
@@ -235,32 +269,38 @@
     )(tokens, kernel, left_factor)
     middle = lax.all_to_all(middle, SEQ_AXES, 0, 0, tiled=True)
 
-    parts = join(z_join_kernel, [shape(16, 16, 512)] * 4, "z_join", *parts, flops=200 * 10**9)
+    *parts, weights = join(z_join_kernel, [shape(8, 16, 512)] * 5, "z_join", *parts, flops=200 * 10**9)
     parts = spread(parts, "x")
-    weights, blocks = join(x_join_kernel, [shape(32, 16, 512), shape(16, 16, 512)], "x_join", *parts)
+    weights = spread([weights] * 4, "y")
+    blocks, weights = join(plane_join_kernel, [shape(16, 16, 512), shape(32, 16, 512)], "plane_join", *parts, *weights)
     blocks = lax.ppermute(blocks, "core", [(0, 1), (1, 0)])
-    near = join(y_join_kernel, shape(WEIGHTS, 16, 512), "y_join", *spread([weights] * 4, "y"), flops=200 * 10**9)
+    blocks, weights = lax.optimization_barrier((blocks, weights))
+    near = join(join_kernel, shape(WEIGHTS, 16, 512), "x_join", *spread([weights] * 4, "x"), flops=200 * 10**9)
     far = lax.ppermute(near, "core", [(0, 1), (1, 0)])
 
-    right = right_factor.astype(F32)
     gated = pl.pallas_call(
         second_last_kernel,
         grid=(1,),
         in_specs=[
-            whole(16, 16, 512),
-            whole(16, 16, 512),
-            whole(16, 16, 512),
-            whole(16, 16, 512),
+            whole(8, 16, 512),
+            whole(8, 16, 512),
+            whole(8, 16, 512),
+            whole(8, 16, 512),
             whole(16, 16, 512),
             whole(BROWS, BROWS),
-            pl.BlockSpec((1, chans, local), lambda i: (2, 0, 0)),
-        ],
-        out_specs=pl.BlockSpec((CHAN, CH, BROWS), lambda i: (0, 0, 2)),
-        out_shape=shape(CHAN, CH, 3 * BROWS),
-        scratch_shapes=[pltpu.VMEM((512, 512), F32)],
-        compiler_params=PARAMS,
+            ANY,
+        ],
+        out_specs=pl.BlockSpec((2, 8, CH, BROWS), lambda i: (0, 0, 0, 2)),
+        out_shape=shape(2, 8, CH, 3 * BROWS),
+        scratch_shapes=[
+            pltpu.VMEM((512, 512), F32),
+            pltpu.VMEM((BROWS, BROWS), F32),
+            pltpu.VMEM((chans, local), BF16),
+            pltpu.SemaphoreType.DMA,
+        ],
+        compiler_params=SMALL,
         name="second_last",
-    )(*parts, blocks, right, tokens)
+    )(*parts, blocks, right_factor, tokens)
     gated = pl.pallas_call(
         second_pair_kernel,
         grid=(1,),
@@ -270,27 +310,34 @@
             pl.BlockSpec((2, chans, local), lambda i: (0, 0, 0)),
             ANY,
         ],
-        out_specs=pl.BlockSpec((CHAN, CH, 2 * BROWS), lambda i: (0, 0, 0)),
-        out_shape=shape(CHAN, CH, 3 * BROWS),
+        out_specs=pl.BlockSpec((2, 8, CH, 2 * BROWS), lambda i: (0, 0, 0, 0)),
+        out_shape=shape(2, 8, CH, 3 * BROWS),
         input_output_aliases={3: 0},
-        compiler_params=PARAMS,
+        compiler_params=SMALL,
         name="second_pair",
-    )(middle, right, tokens, gated)
+    )(middle, right_factor, tokens, gated)
+    gated = gated.reshape(CHAN, CH, 3 * BROWS)
     gated = lax.all_to_all(gated, CHAN_AXES, 0, 0, tiled=True)
+    vmem = pl.BlockSpec(memory_space=pltpu.VMEM)
+    width = CHAN * CH
     return pl.pallas_call(
         mlp_kernel,
-        grid=(3,),
-        in_specs=[
-            pl.BlockSpec((CHAN, CH, BROWS), lambda n: (0, 0, n)),
-            pl.BlockSpec((1, CHAN * CH), lambda n: (0, 0)),
-            pl.BlockSpec((WEIGHTS, 16, 512), lambda n: (0, 0, 0)),
-            pl.BlockSpec((WEIGHTS, 16, 512), lambda n: (0, 0, 0)),
-        ],
-        out_specs=pl.BlockSpec((1, BROWS, CHAN * CH), lambda n: (n, 0, 0)),
-        out_shape=shape(3, BROWS, CHAN * CH),
+        in_specs=[ANY, vmem, ANY, ANY],
+        out_specs=ANY,
+        out_shape=shape(3, BROWS, width),
+        scratch_shapes=[
+            pltpu.VMEM((3, CHAN, CH, BROWS), BF16),
+            pltpu.VMEM((3 * BROWS, width), BF16),
+            pltpu.VMEM((3 * BROWS, width), BF16),
+            pltpu.VMEM((3, BROWS, width), BF16),
+            pltpu.VMEM((2 * WEIGHTS, 16, 512), BF16),
+            pltpu.SemaphoreType.DMA((3,)),
+            pltpu.SemaphoreType.DMA((2,)),
+            pltpu.SemaphoreType.DMA((GROUPS,)),
+        ],
         compiler_params=PARAMS,
         name="mlp",
-    )(gated, norm_gain.reshape(1, CHAN * CH), near, far)
+    )(gated, norm_gain.reshape(1, width), near, far)
 
 
 def solution(mesh):

time: 161 us -> 158 us (0.981)
  starting transfers between devices: 73.7 us -> 85.3 us
  Pallas kernels: 31.9 us -> 21.8 us
  local copies, waits for them, and re-layouts: 3.77 us -> 1.42 us
    ppermute x9 -> x12, starting transfers between devices: 43.6 us -> 55.2 us  [shift(): return lax.ppermute(x, axis, [(i, (i + step) % size) for i in range(size)])]
    pallas_call x5, Pallas kernels: 20.6 us -> 10.8 us  [the longest x1 8.02 us: per_device(): pl.pallas_call(mlp_kernel, in_specs=[ANY, vmem, ANY, ANY], out_specs=ANY,...]
    ppermute x9 -> x12, waiting for transfers between devices: 15.9 us -> 9.97 us  [shift(): return lax.ppermute(x, axis, [(i, (i + step) % size) for i in range(size)])]
    all_to_all x1, waiting for transfers between devices: 25.6 us -> 29.4 us  [per_device(): gated = lax.all_to_all(gated, CHAN_AXES, 0, 0, tiled=True)]
    unnamed x24 -> x10, local copies, waits for them, and re-layouts: 3.77 us -> 1.42 us
  transfers between devices with their start and end apart: 13 -> 16, of which waited for: 8 -> 7; matrix products, arithmetic and copies ran while one was open for 0% -> 0% of each run, Pallas kernels for 11% -> 7%
where the time goes in v3:
time: 158 us
  starting transfers between devices  85.3 us (54%)
  waiting for transfers between devices  48.7 us (31%)
  Pallas kernels  21.8 us (14%)
    ppermute x12, starting transfers between devices, shift(): return lax.ppermute(x, axis, [(i, (i + step) % size) for i in range(size)])  55.2 us
    all_to_all x1, waiting for transfers between devices, per_device(): gated = lax.all_to_all(gated, CHAN_AXES, 0, 0, tiled=True)  29.4 us
    all_to_all x1, starting transfers between devices, per_device(): gated = lax.all_to_all(gated, CHAN_AXES, 0, 0, tiled=True)  19.1 us
    ppermute x12, waiting for transfers between devices, shift(): return lax.ppermute(x, axis, [(i, (i + step) % size) for i in range(size)])  9.97 us
    pallas_call x1, Pallas kernels, per_device(): pl.pallas_call(mlp_kernel, in_specs=[ANY, vmem, ANY, ANY], out_specs=ANY,...  8.02 us
    all_to_all x1, starting transfers between devices, per_device(): middle = lax.all_to_all(middle, SEQ_AXES, 0, 0, tiled=True)  6.94 us
    pallas_call x1, Pallas kernels, per_device(): pl.pallas_call(first_pair_kernel, grid=(1,), in_specs=[pl.BlockSpec((2, c...  4.52 us
    ppermute x1, waiting for transfers between devices, per_device(): far = lax.ppermute(near, 'core', [(0, 1), (1, 0)])  4.08 us
  transfers between devices with their start and end apart: 16, of which 7 were waited for; matrix products, arithmetic and copies ran while one was open for 0% of the time, Pallas kernels for 7%

profile of v3, /device:TPU:38, one launch (start us, length us, event | category | flops | bytes accessed | tf_op | source)
XLA Modules:
  0.0 157.6 jit_solution(2331193425975382605)
XLA Ops:
  0.0 3.4 %first_last.1 = (bf16[10,16,512]{2,1,0:T(8,128)(2,1)}, bf16[10,16,512]{2,1,0:T(8,128)(2,1)}, bf16[10,16,512]{2,1,0:T(8,128)(2,1)}, bf16[10,16,512]{2,1,0:T(8,128)(2,1)}) custom-call(bf16[3,64,4096]{2,1,0:T(8,128)(2,1)} %tok_ref.5, bf16[64,4096]{1,0:T(8,128)(2,1)} %ker_ref.3, bf16[512,512]{1,0:T(8,128)(2,1)} %left_ref.3, bf16[4,32,256]{2,1,0:T(8,128)(2,1)} %bitcast.3, ...), custom_call_target="tpu_custom_call" | custom-call | tf_op jit(solution)/shard_map/first_last/pallas_call | solution.py:239
  3.4 9.1 %collective-permute-start = (bf16[10,16,512]{2,1,0:T(8,128)(2,1)}, bf16[10,16,512]{2,1,0:T(8,128)(2,1)S(1)}, u32[]{:S(2)}, u32[]{:S(2)}) collective-permute-start(bf16[10,16,512]{2,1,0:T(8,128)(2,1)} %get-tuple-element.19), channel_id=1, source_target_pairs={{0,128},{128,256},{256,384},{384,0},{1,129},{129,257},{257,385},{3... | collective-permute-start | bytes 491528 | tf_op jit(solution)/shard_map/ppermute | solution.py:211
  12.5 10.0 %collective-permute-start.1 = (bf16[10,16,512]{2,1,0:T(8,128)(2,1)}, bf16[10,16,512]{2,1,0:T(8,128)(2,1)S(1)}, u32[]{:S(2)}, u32[]{:S(2)}) collective-permute-start(bf16[10,16,512]{2,1,0:T(8,128)(2,1)} %get-tuple-element.20), channel_id=1, source_target_pairs={{0,256},{128,384},{256,0},{384,128},{1,257},{129,385},{257,1},{385... | collective-permute-start | bytes 491528 | tf_op jit(solution)/shard_map/ppermute | solution.py:211
  22.5 5.5 %collective-permute-start.2 = (bf16[10,16,512]{2,1,0:T(8,128)(2,1)}, bf16[10,16,512]{2,1,0:T(8,128)(2,1)S(1)}, u32[]{:S(2)}, u32[]{:S(2)}) collective-permute-start(bf16[10,16,512]{2,1,0:T(8,128)(2,1)} %get-tuple-element.21), channel_id=1, source_target_pairs={{0,384},{128,0},{256,128},{384,256},{1,385},{129,1},{257,129},{385... | collective-permute-start | bytes 491528 | tf_op jit(solution)/shard_map/ppermute | solution.py:211
  28.0 4.5 %first_pair.1 = bf16[32,16,1024]{2,1,0:T(8,128)(2,1)} custom-call(bf16[3,64,4096]{2,1,0:T(8,128)(2,1)} %tok_ref.5, bf16[64,4096]{1,0:T(8,128)(2,1)} %ker_ref.3, bf16[512,512]{1,0:T(8,128)(2,1)} %left_ref.3), custom_call_target="tpu_custom_call" | custom-call | tf_op jit(solution)/shard_map/first_pair/pallas_call | solution.py:256
  32.5 0.0 copy-start.4
  32.5 6.9 %all-to-all-start = ((bf16[32,16,1024]{2,1,0:T(8,128)(2,1)}), bf16[32,16,1024]{2,1,0:T(8,128)(2,1)}, u32[]{:S(2)}, u32[]{:S(2)}) async-start(bf16[32,16,1024]{2,1,0:T(8,128)(2,1)} %first_pair.1), calls=%async_computation | async-start | bytes 2097152 | tf_op jit(solution)/shard_map/all_to_all | solution.py:270
  39.4 0.0 collective-permute-done.refs_1_
  39.5 0.0 collective-permute-done.1.refs_2_
  39.5 4.8 %collective-permute-done.2.refs_3_ = bf16[10,16,512]{2,1,0:T(8,128)(2,1)S(1)} collective-permute-done((bf16[10,16,512]{2,1,0:T(8,128)(2,1)}, bf16[10,16,512]{2,1,0:T(8,128)(2,1)S(1)}, u32[]{:S(2)}, u32[]{:S(2)}) %collective-permute-start.2) | collective-permute-done | bytes 163872 | tf_op jit(solution)/shard_map/ppermute | solution.py:211
  44.3 0.0 copy-done.4
  44.3 0.0 copy-start.3
  44.3 2.5 %collective-permute-start.3 = (bf16[8,16,512]{2,1,0:T(8,128)(2,1)S(1)}, bf16[8,16,512]{2,1,0:T(8,128)(2,1)S(1)}, u32[]{:S(2)}, u32[]{:S(2)}) collective-permute-start(bf16[8,16,512]{2,1,0:T(8,128)(2,1)S(1)} %get-tuple-element.23), channel_id=1, source_target_pairs={{0,32},{32,64},{64,96},{96,0},{1,33},{33,65},{65,97},{97,1},{2,34}... | collective-permute-start | bytes 393224 | tf_op jit(solution)/shard_map/ppermute | solution.py:211
  46.8 4.3 %collective-permute-start.4 = (bf16[8,16,512]{2,1,0:T(8,128)(2,1)S(1)}, bf16[8,16,512]{2,1,0:T(8,128)(2,1)S(1)}, u32[]{:S(2)}, u32[]{:S(2)}) collective-permute-start(bf16[8,16,512]{2,1,0:T(8,128)(2,1)S(1)} %get-tuple-element.24), channel_id=1, source_target_pairs={{0,64},{32,96},{64,0},{96,32},{1,65},{33,97},{65,1},{97,33},{2,66}... | collective-permute-start | bytes 393224 | tf_op jit(solution)/shard_map/ppermute | solution.py:211
  51.2 1.9 %collective-permute-start.5 = (bf16[8,16,512]{2,1,0:T(8,128)(2,1)S(1)}, bf16[8,16,512]{2,1,0:T(8,128)(2,1)S(1)}, u32[]{:S(2)}, u32[]{:S(2)}) collective-permute-start(bf16[8,16,512]{2,1,0:T(8,128)(2,1)S(1)} %get-tuple-element.25), channel_id=1, source_target_pairs={{0,96},{32,0},{64,32},{96,64},{1,97},{33,1},{65,33},{97,65},{2,98}... | collective-permute-start | bytes 393224 | tf_op jit(solution)/shard_map/ppermute | solution.py:211
  53.1 4.9 %collective-permute-start.8 = (bf16[8,16,512]{2,1,0:T(8,128)(2,1)S(1)}, bf16[8,16,512]{2,1,0:T(8,128)(2,1)S(1)}, u32[]{:S(2)}, u32[]{:S(2)}) collective-permute-start(bf16[8,16,512]{2,1,0:T(8,128)(2,1)S(1)} %get-tuple-element.26.refs_4_), channel_id=1, source_target_pairs={{0,3},{1,0},{2,1},{3,2},{4,7},{5,4},{6,5},{7,6},{8,11},{9,8},{10,9... | collective-permute-start | bytes 393224 | tf_op jit(solution)/shard_map/ppermute | solution.py:211
  58.0 2.5 %collective-permute-start.7 = (bf16[8,16,512]{2,1,0:T(8,128)(2,1)S(1)}, bf16[8,16,512]{2,1,0:T(8,128)(2,1)S(1)}, u32[]{:S(2)}, u32[]{:S(2)}) collective-permute-start(bf16[8,16,512]{2,1,0:T(8,128)(2,1)S(1)} %get-tuple-element.26.refs_4_), channel_id=1, source_target_pairs={{0,2},{1,3},{2,0},{3,1},{4,6},{5,7},{6,4},{7,5},{8,10},{9,11},{10,... | collective-permute-start | bytes 393224 | tf_op jit(solution)/shard_map/ppermute | solution.py:211
  60.6 0.0 collective-permute-done.3.refs_1_
  60.6 2.9 %collective-permute-start.6 = (bf16[8,16,512]{2,1,0:T(8,128)(2,1)S(1)}, bf16[8,16,512]{2,1,0:T(8,128)(2,1)S(1)}, u32[]{:S(2)}, u32[]{:S(2)}) collective-permute-start(bf16[8,16,512]{2,1,0:T(8,128)(2,1)S(1)} %get-tuple-element.26.refs_4_), channel_id=1, source_target_pairs={{0,1},{1,2},{2,3},{3,0},{4,5},{5,6},{6,7},{7,4},{8,9},{9,10},{10,1... | collective-permute-start | bytes 393224 | tf_op jit(solution)/shard_map/ppermute | solution.py:211
  63.5 0.0 collective-permute-done.4.refs_2_
  63.5 0.0 collective-permute-done.5.refs_3_
  63.5 0.0 collective-permute-done.8.refs_7_
  63.5 2.9 %collective-permute-done.7.refs_6_ = bf16[8,16,512]{2,1,0:T(8,128)(2,1)S(1)} collective-permute-done((bf16[8,16,512]{2,1,0:T(8,128)(2,1)S(1)}, bf16[8,16,512]{2,1,0:T(8,128)(2,1)S(1)}, u32[]{:S(2)}, u32[]{:S(2)}) %collective-permute-start.7) | collective-permute-done | bytes 131104 | tf_op jit(solution)/shard_map/ppermute | solution.py:211
  66.4 2.3 %collective-permute-done.6.refs_5_ = bf16[8,16,512]{2,1,0:T(8,128)(2,1)S(1)} collective-permute-done((bf16[8,16,512]{2,1,0:T(8,128)(2,1)S(1)}, bf16[8,16,512]{2,1,0:T(8,128)(2,1)S(1)}, u32[]{:S(2)}, u32[]{:S(2)}) %collective-permute-start.6) | collective-permute-done | bytes 131104 | tf_op jit(solution)/shard_map/ppermute | solution.py:211
  68.7 0.1 plane_join.1
  68.7 1.9 %collective-permute-start.9 = (bf16[16,16,512]{2,1,0:T(8,128)(2,1)S(1)}, bf16[16,16,512]{2,1,0:T(8,128)(2,1)S(1)}, u32[]{:S(2)}, u32[]{:S(2)}) collective-permute-start(bf16[16,16,512]{2,1,0:T(8,128)(2,1)S(1)} %get-tuple-element.27), channel_id=1, source_target_pairs={{0,16},{16,0},{1,17},{17,1},{2,18},{18,2},{3,19},{19,3},{4,20},{20... | collective-permute-start | bytes 786440 | tf_op jit(solution)/shard_map/ppermute | solution.py:276
  70.7 1.5 collective-permute-done.9.refs_4_
  72.2 2.9 %collective-permute-start.12 = (bf16[32,16,512]{2,1,0:T(8,128)(2,1)S(1)}, bf16[32,16,512]{2,1,0:T(8,128)(2,1)S(1)}, u32[]{:S(2)}, u32[]{:S(2)}) collective-permute-start(bf16[32,16,512]{2,1,0:T(8,128)(2,1)S(1)} %get-tuple-element.30.refs_0_), channel_id=1, source_target_pairs={{0,96},{32,0},{64,32},{96,64},{1,97},{33,1},{65,33},{97,65},{2,98}... | collective-permute-start | bytes 1572872 | tf_op jit(solution)/shard_map/ppermute | solution.py:211
  75.1 5.6 %collective-permute-start.11 = (bf16[32,16,512]{2,1,0:T(8,128)(2,1)S(1)}, bf16[32,16,512]{2,1,0:T(8,128)(2,1)}, u32[]{:S(2)}, u32[]{:S(2)}) collective-permute-start(bf16[32,16,512]{2,1,0:T(8,128)(2,1)S(1)} %get-tuple-element.30.refs_0_), channel_id=1, source_target_pairs={{0,64},{32,96},{64,0},{96,32},{1,65},{33,97},{65,1},{97,33},{2,66}... | collective-permute-start | bytes 1572872 | tf_op jit(solution)/shard_map/ppermute | solution.py:211
  80.7 3.1 %collective-permute-start.10 = (bf16[32,16,512]{2,1,0:T(8,128)(2,1)S(1)}, bf16[32,16,512]{2,1,0:T(8,128)(2,1)}, u32[]{:S(2)}, u32[]{:S(2)}) collective-permute-start(bf16[32,16,512]{2,1,0:T(8,128)(2,1)S(1)} %get-tuple-element.30.refs_0_), channel_id=1, source_target_pairs={{0,32},{32,64},{64,96},{96,0},{1,33},{33,65},{65,97},{97,1},{2,34}... | collective-permute-start | bytes 1572872 | tf_op jit(solution)/shard_map/ppermute | solution.py:211
  83.7 0.0 copy-done.3
  83.8 0.0 copy-start
  83.8 1.4 copy-done
  85.2 1.4 second_last.1.kept_ref
  86.6 3.8 %all-to-all-done.mid_ref = bf16[32,16,1024]{2,1,0:T(8,128)(2,1)} async-done(((bf16[32,16,1024]{2,1,0:T(8,128)(2,1)}), bf16[32,16,1024]{2,1,0:T(8,128)(2,1)}, u32[]{:S(2)}, u32[]{:S(2)}) %all-to-all-start) | async-done | bytes 1048608 | tf_op jit(solution)/shard_map/all_to_all | solution.py:270
  90.4 0.0 copy-done.1
  90.4 3.0 %second_pair.1 = bf16[2,8,64,768]{3,2,1,0:T(8,128)(2,1)} custom-call(bf16[32,16,1024]{2,1,0:T(8,128)(2,1)} %all-to-all-done.mid_ref, bf16[256,256]{1,0:T(8,128)(2,1)S(1)} %copy-done.3, bf16[3,64,4096]{2,1,0:T(8,128)(2,1)S(1)} %copy-done.1, bf16[2,8,64,768]{3,2,1,0:T(8,128)(2,1)} %second_last.1.kept_ref), custom_call_target="tpu_custom_call", output_to_operand_aliasing={{}: (3, {})} | custom-call | tf_op jit(solution)/shard_map/second_pair/pallas_call | solution.py:304
  93.4 19.1 %all-to-all-start.1 = ((bf16[16,64,768]{2,1,0:T(8,128)(2,1)}), bf16[16,64,768]{2,1,0:T(8,128)(2,1)}, u32[]{:S(2)}, u32[]{:S(2)}) async-start(bf16[16,64,768]{2,1,0:T(8,128)(2,1)} %bitcast.1), calls=%async_computation.1 | async-start | bytes 3145728 | tf_op jit(solution)/shard_map/all_to_all | solution.py:320
  112.5 0.0 collective-permute-done.12.refs_3_
  112.5 0.0 collective-permute-done.11.refs_2_
  112.5 0.0 collective-permute-done.10.refs_1_
  112.5 1.3 x_join.1.near_hbm
  113.9 0.0 copy-start.2
  113.9 2.1 %collective-permute-start.13 = (bf16[128,16,512]{2,1,0:T(8,128)(2,1)S(1)}, bf16[128,16,512]{2,1,0:T(8,128)(2,1)}, u32[]{:S(2)}, u32[]{:S(2)}) collective-permute-start(bf16[128,16,512]{2,1,0:T(8,128)(2,1)S(1)} %x_join.1.near_hbm), channel_id=1, source_target_pairs={{0,16},{16,0},{1,17},{17,1},{2,18},{18,2},{3,19},{19,3},{4,20},{20... | collective-permute-start | bytes 6291464 | tf_op jit(solution)/shard_map/ppermute | solution.py:279
  116.0 4.1 %collective-permute-done.13.far_hbm = bf16[128,16,512]{2,1,0:T(8,128)(2,1)} collective-permute-done((bf16[128,16,512]{2,1,0:T(8,128)(2,1)S(1)}, bf16[128,16,512]{2,1,0:T(8,128)(2,1)}, u32[]{:S(2)}, u32[]{:S(2)}) %collective-permute-start.13) | collective-permute-done | bytes 2097184 | tf_op jit(solution)/shard_map/ppermute | solution.py:279
  120.1 29.4 %all-to-all-done.1.x_hbm = bf16[16,64,768]{2,1,0:T(8,128)(2,1)} async-done(((bf16[16,64,768]{2,1,0:T(8,128)(2,1)}), bf16[16,64,768]{2,1,0:T(8,128)(2,1)}, u32[]{:S(2)}, u32[]{:S(2)}) %all-to-all-start.1) | async-done | bytes 1572896 | tf_op jit(solution)/shard_map/all_to_all | solution.py:320
  149.4 0.0 copy-done.2
  149.4 8.0 %mlp.1 = bf16[3,256,1024]{2,1,0:T(8,128)(2,1)} custom-call(bf16[16,64,768]{2,1,0:T(8,128)(2,1)} %all-to-all-done.1.x_hbm, f32[1,1024]{1,0:T(1,128)} %bitcast.4, bf16[128,16,512]{2,1,0:T(8,128)(2,1)} %copy-done.2, bf16[128,16,512]{2,1,0:T(8,128)(2,1)} %collective-permute-done.13.far_hbm), custom_call_target="tpu_custom_call" | custom-call | tf_op jit(solution)/shard_map/mlp/pallas_call | solution.py:323
  (2 shorter events, 0.0 us)
Async XLA Ops:
  3.4 36.1 %collective-permute-start = (bf16[10,16,512]{2,1,0:T(8,128)(2,1)}, bf16[10,16,512]{2,1,0:T(8,128)(2,1)S(1)}, u32[]{:S(2)}, u32[]{:S(2)}) collective-permute-start(bf16[10,16,512]{2,1,0:T(8,128)(2,1)} %get-tuple-element.19), channel_id=1, source_target_pairs={{0,128},{128,256},{256,384},{384,0},{1,129},{129,257},{257,385},{3... | collective-permute-start | bytes 491528 | tf_op jit(solution)/shard_map/ppermute | solution.py:211
  12.5 27.0 %collective-permute-start.1 = (bf16[10,16,512]{2,1,0:T(8,128)(2,1)}, bf16[10,16,512]{2,1,0:T(8,128)(2,1)S(1)}, u32[]{:S(2)}, u32[]{:S(2)}) collective-permute-start(bf16[10,16,512]{2,1,0:T(8,128)(2,1)} %get-tuple-element.20), channel_id=1, source_target_pairs={{0,256},{128,384},{256,0},{384,128},{1,257},{129,385},{257,1},{385... | collective-permute-start | bytes 491528 | tf_op jit(solution)/shard_map/ppermute | solution.py:211
  22.5 21.7 %collective-permute-start.2 = (bf16[10,16,512]{2,1,0:T(8,128)(2,1)}, bf16[10,16,512]{2,1,0:T(8,128)(2,1)S(1)}, u32[]{:S(2)}, u32[]{:S(2)}) collective-permute-start(bf16[10,16,512]{2,1,0:T(8,128)(2,1)} %get-tuple-element.21), channel_id=1, source_target_pairs={{0,384},{128,0},{256,128},{384,256},{1,385},{129,1},{257,129},{385... | collective-permute-start | bytes 491528 | tf_op jit(solution)/shard_map/ppermute | solution.py:211
  32.5 11.8 %copy-start.4 = (bf16[10,16,512]{2,1,0:T(8,128)(2,1)S(1)}, bf16[10,16,512]{2,1,0:T(8,128)(2,1)}, u32[]{:S(2)}) copy-start(bf16[10,16,512]{2,1,0:T(8,128)(2,1)} %get-tuple-element.18.refs_0_) | copy-start | bytes 491524
  32.5 57.9 %all-to-all-start = ((bf16[32,16,1024]{2,1,0:T(8,128)(2,1)}), bf16[32,16,1024]{2,1,0:T(8,128)(2,1)}, u32[]{:S(2)}, u32[]{:S(2)}) async-start(bf16[32,16,1024]{2,1,0:T(8,128)(2,1)} %first_pair.1), calls=%async_computation | async-start | bytes 2097152 | tf_op jit(solution)/shard_map/all_to_all | solution.py:270
  44.3 39.5 %copy-start.3 = (bf16[256,256]{1,0:T(8,128)(2,1)S(1)}, bf16[256,256]{1,0:T(8,128)(2,1)}, u32[]{:S(2)}) copy-start(bf16[256,256]{1,0:T(8,128)(2,1)} %right_ref.1) | copy-start | bytes 393220
  44.3 16.3 %collective-permute-start.3 = (bf16[8,16,512]{2,1,0:T(8,128)(2,1)S(1)}, bf16[8,16,512]{2,1,0:T(8,128)(2,1)S(1)}, u32[]{:S(2)}, u32[]{:S(2)}) collective-permute-start(bf16[8,16,512]{2,1,0:T(8,128)(2,1)S(1)} %get-tuple-element.23), channel_id=1, source_target_pairs={{0,32},{32,64},{64,96},{96,0},{1,33},{33,65},{65,97},{97,1},{2,34}... | collective-permute-start | bytes 393224 | tf_op jit(solution)/shard_map/ppermute | solution.py:211
  46.8 16.6 %collective-permute-start.4 = (bf16[8,16,512]{2,1,0:T(8,128)(2,1)S(1)}, bf16[8,16,512]{2,1,0:T(8,128)(2,1)S(1)}, u32[]{:S(2)}, u32[]{:S(2)}) collective-permute-start(bf16[8,16,512]{2,1,0:T(8,128)(2,1)S(1)} %get-tuple-element.24), channel_id=1, source_target_pairs={{0,64},{32,96},{64,0},{96,32},{1,65},{33,97},{65,1},{97,33},{2,66}... | collective-permute-start | bytes 393224 | tf_op jit(solution)/shard_map/ppermute | solution.py:211
  51.2 12.3 %collective-permute-start.5 = (bf16[8,16,512]{2,1,0:T(8,128)(2,1)S(1)}, bf16[8,16,512]{2,1,0:T(8,128)(2,1)S(1)}, u32[]{:S(2)}, u32[]{:S(2)}) collective-permute-start(bf16[8,16,512]{2,1,0:T(8,128)(2,1)S(1)} %get-tuple-element.25), channel_id=1, source_target_pairs={{0,96},{32,0},{64,32},{96,64},{1,97},{33,1},{65,33},{97,65},{2,98}... | collective-permute-start | bytes 393224 | tf_op jit(solution)/shard_map/ppermute | solution.py:211
  53.1 10.4 %collective-permute-start.8 = (bf16[8,16,512]{2,1,0:T(8,128)(2,1)S(1)}, bf16[8,16,512]{2,1,0:T(8,128)(2,1)S(1)}, u32[]{:S(2)}, u32[]{:S(2)}) collective-permute-start(bf16[8,16,512]{2,1,0:T(8,128)(2,1)S(1)} %get-tuple-element.26.refs_4_), channel_id=1, source_target_pairs={{0,3},{1,0},{2,1},{3,2},{4,7},{5,4},{6,5},{7,6},{8,11},{9,8},{10,9... | collective-permute-start | bytes 393224 | tf_op jit(solution)/shard_map/ppermute | solution.py:211
  58.0 8.4 %collective-permute-start.7 = (bf16[8,16,512]{2,1,0:T(8,128)(2,1)S(1)}, bf16[8,16,512]{2,1,0:T(8,128)(2,1)S(1)}, u32[]{:S(2)}, u32[]{:S(2)}) collective-permute-start(bf16[8,16,512]{2,1,0:T(8,128)(2,1)S(1)} %get-tuple-element.26.refs_4_), channel_id=1, source_target_pairs={{0,2},{1,3},{2,0},{3,1},{4,6},{5,7},{6,4},{7,5},{8,10},{9,11},{10,... | collective-permute-start | bytes 393224 | tf_op jit(solution)/shard_map/ppermute | solution.py:211
  60.6 8.1 %collective-permute-start.6 = (bf16[8,16,512]{2,1,0:T(8,128)(2,1)S(1)}, bf16[8,16,512]{2,1,0:T(8,128)(2,1)S(1)}, u32[]{:S(2)}, u32[]{:S(2)}) collective-permute-start(bf16[8,16,512]{2,1,0:T(8,128)(2,1)S(1)} %get-tuple-element.26.refs_4_), channel_id=1, source_target_pairs={{0,1},{1,2},{2,3},{3,0},{4,5},{5,6},{6,7},{7,4},{8,9},{9,10},{10,1... | collective-permute-start | bytes 393224 | tf_op jit(solution)/shard_map/ppermute | solution.py:211
  68.7 3.4 %collective-permute-start.9 = (bf16[16,16,512]{2,1,0:T(8,128)(2,1)S(1)}, bf16[16,16,512]{2,1,0:T(8,128)(2,1)S(1)}, u32[]{:S(2)}, u32[]{:S(2)}) collective-permute-start(bf16[16,16,512]{2,1,0:T(8,128)(2,1)S(1)} %get-tuple-element.27), channel_id=1, source_target_pairs={{0,16},{16,0},{1,17},{17,1},{2,18},{18,2},{3,19},{19,3},{4,20},{20... | collective-permute-start | bytes 786440 | tf_op jit(solution)/shard_map/ppermute | solution.py:276
  72.2 40.4 %collective-permute-start.12 = (bf16[32,16,512]{2,1,0:T(8,128)(2,1)S(1)}, bf16[32,16,512]{2,1,0:T(8,128)(2,1)S(1)}, u32[]{:S(2)}, u32[]{:S(2)}) collective-permute-start(bf16[32,16,512]{2,1,0:T(8,128)(2,1)S(1)} %get-tuple-element.30.refs_0_), channel_id=1, source_target_pairs={{0,96},{32,0},{64,32},{96,64},{1,97},{33,1},{65,33},{97,65},{2,98}... | collective-permute-start | bytes 1572872 | tf_op jit(solution)/shard_map/ppermute | solution.py:211
  75.1 37.5 %collective-permute-start.11 = (bf16[32,16,512]{2,1,0:T(8,128)(2,1)S(1)}, bf16[32,16,512]{2,1,0:T(8,128)(2,1)}, u32[]{:S(2)}, u32[]{:S(2)}) collective-permute-start(bf16[32,16,512]{2,1,0:T(8,128)(2,1)S(1)} %get-tuple-element.30.refs_0_), channel_id=1, source_target_pairs={{0,64},{32,96},{64,0},{96,32},{1,65},{33,97},{65,1},{97,33},{2,66}... | collective-permute-start | bytes 1572872 | tf_op jit(solution)/shard_map/ppermute | solution.py:211
  80.7 31.9 %collective-permute-start.10 = (bf16[32,16,512]{2,1,0:T(8,128)(2,1)S(1)}, bf16[32,16,512]{2,1,0:T(8,128)(2,1)}, u32[]{:S(2)}, u32[]{:S(2)}) collective-permute-start(bf16[32,16,512]{2,1,0:T(8,128)(2,1)S(1)} %get-tuple-element.30.refs_0_), channel_id=1, source_target_pairs={{0,32},{32,64},{64,96},{96,0},{1,33},{33,65},{65,97},{97,1},{2,34}... | collective-permute-start | bytes 1572872 | tf_op jit(solution)/shard_map/ppermute | solution.py:211
  83.8 1.4 copy-start
  85.2 5.2 %copy-start.1 = (bf16[3,64,4096]{2,1,0:T(8,128)(2,1)S(1)}, bf16[3,64,4096]{2,1,0:T(8,128)(2,1)}, u32[]{:S(2)}) copy-start(bf16[3,64,4096]{2,1,0:T(8,128)(2,1)} %tok_ref.5) | copy-start | bytes 4718596
  93.4 56.0 %all-to-all-start.1 = ((bf16[16,64,768]{2,1,0:T(8,128)(2,1)}), bf16[16,64,768]{2,1,0:T(8,128)(2,1)}, u32[]{:S(2)}, u32[]{:S(2)}) async-start(bf16[16,64,768]{2,1,0:T(8,128)(2,1)} %bitcast.1), calls=%async_computation.1 | async-start | bytes 3145728 | tf_op jit(solution)/shard_map/all_to_all | solution.py:320
  113.9 35.5 %copy-start.2 = (bf16[128,16,512]{2,1,0:T(8,128)(2,1)}, bf16[128,16,512]{2,1,0:T(8,128)(2,1)S(1)}, u32[]{:S(2)}) copy-start(bf16[128,16,512]{2,1,0:T(8,128)(2,1)S(1)} %x_join.1.near_hbm) | copy-start | bytes 6291460
  113.9 6.2 %collective-permute-start.13 = (bf16[128,16,512]{2,1,0:T(8,128)(2,1)S(1)}, bf16[128,16,512]{2,1,0:T(8,128)(2,1)}, u32[]{:S(2)}, u32[]{:S(2)}) collective-permute-start(bf16[128,16,512]{2,1,0:T(8,128)(2,1)S(1)} %x_join.1.near_hbm), channel_id=1, source_target_pairs={{0,16},{16,0},{1,17},{17,1},{2,18},{18,2},{3,19},{19,3},{4,20},{20... | collective-permute-start | bytes 6291464 | tf_op jit(solution)/shard_map/ppermute | solution.py:279

commit v4 on v3

--- a/solution.py
+++ b/solution.py
@@ -34,14 +34,23 @@
     return ref[...].astype(F32).T.astype(BF16)
 
 
-def first_last_kernel(tok_ref, ker_ref, left_ref, up_ref, down_ref, *refs):
-    *outs, work_ref = refs
+def first_last_kernel(tok_hbm, ker_hbm, left_ref, up_ref, down_ref, *refs):
+    out_hbms, (work_ref, tok_ref, ker_ref, out_ref, in_sems, out_sems) = refs[:4], refs[4:]
     own_z, own_x, own_core = lax.axis_index("z_hi"), lax.axis_index("x"), lax.axis_index("core")
+    loads, stores = [], []
+    for quad in range(ROWS // 4):
+        lanes = pl.ds(quad * 4 * BLK, 4 * BLK)
+        loads.append(pltpu.make_async_copy(ker_hbm.at[:, lanes], ker_ref.at[:, lanes], in_sems.at[2 * quad]))
+        loads.append(pltpu.make_async_copy(tok_hbm.at[2, :, lanes], tok_ref.at[:, lanes], in_sems.at[2 * quad + 1]))
+    for load in loads:
+        load.start()
     left_t = transposed(left_ref)
     for quad in range(ROWS // 4):
+        for load in loads[2 * quad:2 * quad + 2]:
+            load.wait()
         rows = range(quad * 4, quad * 4 + 4)
         taps = jnp.concatenate([rows_of(ker_ref, None, a) for a in rows], axis=0).astype(F32).T
-        prod = matmul_t(left_t, jnp.concatenate([rows_of(tok_ref, 0, a) for a in rows], axis=0)) * taps
+        prod = matmul_t(left_t, jnp.concatenate([rows_of(tok_ref, None, a) for a in rows], axis=0)) * taps
         for i, a in enumerate(rows):
             one = prod[:, i * CH:(i + 1) * CH].reshape(SEQ, 2, 8, CH)
             for jh in range(2):
@@ -50,7 +59,7 @@
     for step in range(4):
         for kind, ref in enumerate((up_ref, down_ref)):
             for i in range(2):
-                outs[step][8 + kind, :, i * 256:(i + 1) * 256] = ref[own_y, i * 16:(i + 1) * 16, :]
+                out_ref[step, 8 + kind, :, i * 256:(i + 1) * 256] = ref[own_y, i * 16:(i + 1) * 16, :]
         for x_step in range(4):
             for core_step in range(2):
                 core = own_core if core_step == 0 else 1 - own_core
@@ -58,7 +67,11 @@
                 for jq in range(4):
                     both = [work_ref[pl.ds(dst * 8 + (jm * 4 + jq), 8, stride=256), :] for jm in range(2)]
                     block = jnp.concatenate(both, axis=0).astype(BF16)
-                    outs[step][x_step * 2 + core_step, :, jq * 128:(jq + 1) * 128] = block
+                    out_ref[step, x_step * 2 + core_step, :, jq * 128:(jq + 1) * 128] = block
+        stores.append(pltpu.make_async_copy(out_ref.at[step], out_hbms[step], out_sems.at[step]))
+        stores[step].start()
+    for store in stores:
+        store.wait()
 
 
 def first_pair_kernel(tok_ref, ker_ref, left_ref, out_ref, work_ref):
@@ -139,20 +152,33 @@
                 out_ref[jh, jm * 4 + jq] = gate(x, mixed[jh * CH:(jh + 1) * CH, jm * BROWS:(jm + 1) * BROWS])
 
 
-def second_pair_kernel(mid_ref, right_ref, tok_ref, kept_ref, out_ref):
+def second_pair_kernel(mid_hbm, right_ref, tok_ref, kept_hbm, out_hbm, mid_ref, out_ref, in_sems, out_sems):
+    loads, stores = [], []
+    for i in range(4):
+        at = pl.ds(i * 256, 256)
+        loads.append(pltpu.make_async_copy(mid_hbm.at[:, :, at], mid_ref.at[i], in_sems.at[i]))
+        loads[i].start()
     right = right_ref[...].astype(F32).reshape(SEQ, ROWS, BROWS)
     zero = jnp.zeros_like(right)
     upper = jnp.concatenate([right, zero], axis=1).reshape(512, BROWS)
     lower = jnp.concatenate([zero, right], axis=1).reshape(512, BROWS)
     wide = jnp.concatenate([upper, lower], axis=1).astype(BF16)
     for jl in range(8):
-        mixed = mix(mid_ref[:, :, jl * 128:(jl + 1) * 128].reshape(512, 128), wide)
+        if jl % 2 == 0:
+            loads[jl // 2].wait()
+        lane = jl % 2 * 128
+        mixed = mix(mid_ref[jl // 2, :, :, lane:lane + 128].reshape(512, 128), wide)
         for n in range(2):
             for jh in range(2):
                 j = jh * 8 + jl
                 x = tok_ref[n, :, j * BROWS:(j + 1) * BROWS]
                 value = mixed[n * CH:(n + 1) * CH, jh * BROWS:(jh + 1) * BROWS]
-                out_ref[jh, jl, :, n * BROWS:(n + 1) * BROWS] = gate(x, value)
+                out_ref[jl, jh, :, n * BROWS:(n + 1) * BROWS] = gate(x, value)
+        out_at = out_hbm.at[:, jl, :, pl.ds(0, 2 * BROWS)]
+        stores.append(pltpu.make_async_copy(out_ref.at[jl], out_at, out_sems.at[jl]))
+        stores[jl].start()
+    for store in stores:
+        store.wait()
 
 
 def twice_gelu(x):
@@ -240,15 +266,22 @@
         first_last_kernel,
         grid=(1,),
         in_specs=[
-            pl.BlockSpec((1, chans, local), lambda i: (2, 0, 0)),
-            whole(chans, local),
+            ANY,
+            ANY,
             whole(BLK, BLK),
             whole(GROUPS, 32, 256),
             whole(GROUPS, 32, 256),
         ],
-        out_specs=[whole(10, 16, 512)] * 4,
+        out_specs=[ANY] * 4,
         out_shape=[shape(10, 16, 512)] * 4,
-        scratch_shapes=[pltpu.VMEM((ROWS * 256, 128), F32)],
+        scratch_shapes=[
+            pltpu.VMEM((ROWS * 256, 128), F32),
+            pltpu.VMEM((chans, local), BF16),
+            pltpu.VMEM((chans, local), BF16),
+            pltpu.VMEM((4, 10, 16, 512), BF16),
+            pltpu.SemaphoreType.DMA((4,)),
+            pltpu.SemaphoreType.DMA((4,)),
+        ],
         compiler_params=PARAMS,
         name="first_last",
     )(tokens, kernel, left_factor, up_weight.transpose(0, 2, 1), down_weight)
@@ -305,14 +338,20 @@
         second_pair_kernel,
         grid=(1,),
         in_specs=[
-            whole(SEQ, 16, 1024),
+            ANY,
             whole(BROWS, BROWS),
             pl.BlockSpec((2, chans, local), lambda i: (0, 0, 0)),
             ANY,
         ],
-        out_specs=pl.BlockSpec((2, 8, CH, 2 * BROWS), lambda i: (0, 0, 0, 0)),
+        out_specs=ANY,
         out_shape=shape(2, 8, CH, 3 * BROWS),
         input_output_aliases={3: 0},
+        scratch_shapes=[
+            pltpu.VMEM((4, SEQ, 16, 256), BF16),
+            pltpu.VMEM((8, 2, CH, 2 * BROWS), BF16),
+            pltpu.SemaphoreType.DMA((4,)),
+            pltpu.SemaphoreType.DMA((8,)),
+        ],
         compiler_params=SMALL,
         name="second_pair",
     )(middle, right_factor, tokens, gated)

time: 158 us -> 160 us (1.013)
  Pallas kernels: 21.8 us -> 23.7 us
    pallas_call x2, Pallas kernels: 6.42 us -> 8.37 us  [the longest x1 4.52 us: per_device(): pl.pallas_call(first_last_kernel, grid=(1,), in_specs=[ANY, ANY, whole(BL...]
where the time goes in v4:
time: 160 us
  starting transfers between devices  86 us (54%)
  waiting for transfers between devices  48.1 us (30%)
  Pallas kernels  23.7 us (15%)
    ppermute x12, starting transfers between devices, shift(): return lax.ppermute(x, axis, [(i, (i + step) % size) for i in range(size)])  55.3 us
    all_to_all x1, waiting for transfers between devices, per_device(): gated = lax.all_to_all(gated, CHAN_AXES, 0, 0, tiled=True)  29.4 us
    all_to_all x1, starting transfers between devices, per_device(): gated = lax.all_to_all(gated, CHAN_AXES, 0, 0, tiled=True)  19.7 us
    ppermute x12, waiting for transfers between devices, shift(): return lax.ppermute(x, axis, [(i, (i + step) % size) for i in range(size)])  9.96 us
    pallas_call x1, Pallas kernels, per_device(): pl.pallas_call(mlp_kernel, in_specs=[ANY, vmem, ANY, ANY], out_specs=ANY,...  8.02 us
    all_to_all x1, starting transfers between devices, per_device(): middle = lax.all_to_all(middle, SEQ_AXES, 0, 0, tiled=True)  6.94 us
    pallas_call x1, Pallas kernels, per_device(): pl.pallas_call(first_last_kernel, grid=(1,), in_specs=[ANY, ANY, whole(BL...  4.52 us
    pallas_call x1, Pallas kernels, per_device(): pl.pallas_call(first_pair_kernel, grid=(1,), in_specs=[pl.BlockSpec((2, c...  4.51 us
  transfers between devices with their start and end apart: 16, of which 7 were waited for; matrix products, arithmetic and copies ran while one was open for 0% of the time, Pallas kernels for 7%

profile of v4, /device:TPU:38, one launch (start us, length us, event | category | flops | bytes accessed | tf_op | source)
XLA Modules:
  0.0 159.6 jit_solution(11410636609376822618)
XLA Ops:
  0.0 4.5 %first_last.1 = (bf16[10,16,512]{2,1,0:T(8,128)(2,1)}, bf16[10,16,512]{2,1,0:T(8,128)(2,1)}, bf16[10,16,512]{2,1,0:T(8,128)(2,1)}, bf16[10,16,512]{2,1,0:T(8,128)(2,1)}) custom-call(bf16[3,64,4096]{2,1,0:T(8,128)(2,1)} %tok_ref.3, bf16[64,4096]{1,0:T(8,128)(2,1)} %ker_hbm.1, bf16[512,512]{1,0:T(8,128)(2,1)} %left_ref.3, bf16[4,32,256]{2,1,0:T(8,128)(2,1)} %bitcast.3, ...), custom_call_target="tpu_custom_call" | custom-call | tf_op jit(solution)/shard_map/first_last/pallas_call | solution.py:265
  4.5 9.1 %collective-permute-start = (bf16[10,16,512]{2,1,0:T(8,128)(2,1)}, bf16[10,16,512]{2,1,0:T(8,128)(2,1)S(1)}, u32[]{:S(2)}, u32[]{:S(2)}) collective-permute-start(bf16[10,16,512]{2,1,0:T(8,128)(2,1)} %get-tuple-element.19), channel_id=1, source_target_pairs={{0,128},{128,256},{256,384},{384,0},{1,129},{129,257},{257,385},{3... | collective-permute-start | bytes 491528 | tf_op jit(solution)/shard_map/ppermute | solution.py:237
  13.6 10.0 %collective-permute-start.1 = (bf16[10,16,512]{2,1,0:T(8,128)(2,1)}, bf16[10,16,512]{2,1,0:T(8,128)(2,1)S(1)}, u32[]{:S(2)}, u32[]{:S(2)}) collective-permute-start(bf16[10,16,512]{2,1,0:T(8,128)(2,1)} %get-tuple-element.20), channel_id=1, source_target_pairs={{0,256},{128,384},{256,0},{384,128},{1,257},{129,385},{257,1},{385... | collective-permute-start | bytes 491528 | tf_op jit(solution)/shard_map/ppermute | solution.py:237
  23.7 5.5 %collective-permute-start.2 = (bf16[10,16,512]{2,1,0:T(8,128)(2,1)}, bf16[10,16,512]{2,1,0:T(8,128)(2,1)S(1)}, u32[]{:S(2)}, u32[]{:S(2)}) collective-permute-start(bf16[10,16,512]{2,1,0:T(8,128)(2,1)} %get-tuple-element.21), channel_id=1, source_target_pairs={{0,384},{128,0},{256,128},{384,256},{1,385},{129,1},{257,129},{385... | collective-permute-start | bytes 491528 | tf_op jit(solution)/shard_map/ppermute | solution.py:237
  29.1 4.5 %first_pair.1 = bf16[32,16,1024]{2,1,0:T(8,128)(2,1)} custom-call(bf16[3,64,4096]{2,1,0:T(8,128)(2,1)} %tok_ref.3, bf16[64,4096]{1,0:T(8,128)(2,1)} %ker_hbm.1, bf16[512,512]{1,0:T(8,128)(2,1)} %left_ref.3), custom_call_target="tpu_custom_call" | custom-call | tf_op jit(solution)/shard_map/first_pair/pallas_call | solution.py:289
  33.6 0.0 copy-start.4
  33.6 6.9 %all-to-all-start = ((bf16[32,16,1024]{2,1,0:T(8,128)(2,1)}), bf16[32,16,1024]{2,1,0:T(8,128)(2,1)}, u32[]{:S(2)}, u32[]{:S(2)}) async-start(bf16[32,16,1024]{2,1,0:T(8,128)(2,1)} %first_pair.1), calls=%async_computation | async-start | bytes 2097152 | tf_op jit(solution)/shard_map/all_to_all | solution.py:303
  40.6 0.0 collective-permute-done.refs_1_
  40.6 0.0 collective-permute-done.1.refs_2_
  40.6 4.8 %collective-permute-done.2.refs_3_ = bf16[10,16,512]{2,1,0:T(8,128)(2,1)S(1)} collective-permute-done((bf16[10,16,512]{2,1,0:T(8,128)(2,1)}, bf16[10,16,512]{2,1,0:T(8,128)(2,1)S(1)}, u32[]{:S(2)}, u32[]{:S(2)}) %collective-permute-start.2) | collective-permute-done | bytes 163872 | tf_op jit(solution)/shard_map/ppermute | solution.py:237
  45.4 0.0 copy-done.4
  45.4 0.0 copy-start.3
  45.4 2.5 %collective-permute-start.3 = (bf16[8,16,512]{2,1,0:T(8,128)(2,1)S(1)}, bf16[8,16,512]{2,1,0:T(8,128)(2,1)S(1)}, u32[]{:S(2)}, u32[]{:S(2)}) collective-permute-start(bf16[8,16,512]{2,1,0:T(8,128)(2,1)S(1)} %get-tuple-element.23), channel_id=1, source_target_pairs={{0,32},{32,64},{64,96},{96,0},{1,33},{33,65},{65,97},{97,1},{2,34}... | collective-permute-start | bytes 393224 | tf_op jit(solution)/shard_map/ppermute | solution.py:237
  48.0 4.3 %collective-permute-start.4 = (bf16[8,16,512]{2,1,0:T(8,128)(2,1)S(1)}, bf16[8,16,512]{2,1,0:T(8,128)(2,1)S(1)}, u32[]{:S(2)}, u32[]{:S(2)}) collective-permute-start(bf16[8,16,512]{2,1,0:T(8,128)(2,1)S(1)} %get-tuple-element.24), channel_id=1, source_target_pairs={{0,64},{32,96},{64,0},{96,32},{1,65},{33,97},{65,1},{97,33},{2,66}... | collective-permute-start | bytes 393224 | tf_op jit(solution)/shard_map/ppermute | solution.py:237
  52.3 1.9 %collective-permute-start.5 = (bf16[8,16,512]{2,1,0:T(8,128)(2,1)S(1)}, bf16[8,16,512]{2,1,0:T(8,128)(2,1)S(1)}, u32[]{:S(2)}, u32[]{:S(2)}) collective-permute-start(bf16[8,16,512]{2,1,0:T(8,128)(2,1)S(1)} %get-tuple-element.25), channel_id=1, source_target_pairs={{0,96},{32,0},{64,32},{96,64},{1,97},{33,1},{65,33},{97,65},{2,98}... | collective-permute-start | bytes 393224 | tf_op jit(solution)/shard_map/ppermute | solution.py:237
  54.2 4.9 %collective-permute-start.8 = (bf16[8,16,512]{2,1,0:T(8,128)(2,1)S(1)}, bf16[8,16,512]{2,1,0:T(8,128)(2,1)S(1)}, u32[]{:S(2)}, u32[]{:S(2)}) collective-permute-start(bf16[8,16,512]{2,1,0:T(8,128)(2,1)S(1)} %get-tuple-element.26.refs_4_), channel_id=1, source_target_pairs={{0,3},{1,0},{2,1},{3,2},{4,7},{5,4},{6,5},{7,6},{8,11},{9,8},{10,9... | collective-permute-start | bytes 393224 | tf_op jit(solution)/shard_map/ppermute | solution.py:237
  59.2 2.5 %collective-permute-start.7 = (bf16[8,16,512]{2,1,0:T(8,128)(2,1)S(1)}, bf16[8,16,512]{2,1,0:T(8,128)(2,1)S(1)}, u32[]{:S(2)}, u32[]{:S(2)}) collective-permute-start(bf16[8,16,512]{2,1,0:T(8,128)(2,1)S(1)} %get-tuple-element.26.refs_4_), channel_id=1, source_target_pairs={{0,2},{1,3},{2,0},{3,1},{4,6},{5,7},{6,4},{7,5},{8,10},{9,11},{10,... | collective-permute-start | bytes 393224 | tf_op jit(solution)/shard_map/ppermute | solution.py:237
  61.7 0.0 collective-permute-done.3.refs_1_
  61.7 2.9 %collective-permute-start.6 = (bf16[8,16,512]{2,1,0:T(8,128)(2,1)S(1)}, bf16[8,16,512]{2,1,0:T(8,128)(2,1)S(1)}, u32[]{:S(2)}, u32[]{:S(2)}) collective-permute-start(bf16[8,16,512]{2,1,0:T(8,128)(2,1)S(1)} %get-tuple-element.26.refs_4_), channel_id=1, source_target_pairs={{0,1},{1,2},{2,3},{3,0},{4,5},{5,6},{6,7},{7,4},{8,9},{9,10},{10,1... | collective-permute-start | bytes 393224 | tf_op jit(solution)/shard_map/ppermute | solution.py:237
  64.6 0.0 collective-permute-done.4.refs_2_
  64.6 0.0 collective-permute-done.5.refs_3_
  64.6 0.0 collective-permute-done.8.refs_7_
  64.6 2.9 %collective-permute-done.7.refs_6_ = bf16[8,16,512]{2,1,0:T(8,128)(2,1)S(1)} collective-permute-done((bf16[8,16,512]{2,1,0:T(8,128)(2,1)S(1)}, bf16[8,16,512]{2,1,0:T(8,128)(2,1)S(1)}, u32[]{:S(2)}, u32[]{:S(2)}) %collective-permute-start.7) | collective-permute-done | bytes 131104 | tf_op jit(solution)/shard_map/ppermute | solution.py:237
  67.5 2.3 %collective-permute-done.6.refs_5_ = bf16[8,16,512]{2,1,0:T(8,128)(2,1)S(1)} collective-permute-done((bf16[8,16,512]{2,1,0:T(8,128)(2,1)S(1)}, bf16[8,16,512]{2,1,0:T(8,128)(2,1)S(1)}, u32[]{:S(2)}, u32[]{:S(2)}) %collective-permute-start.6) | collective-permute-done | bytes 131104 | tf_op jit(solution)/shard_map/ppermute | solution.py:237
  69.8 0.1 plane_join.1
  69.9 1.9 %collective-permute-start.9 = (bf16[16,16,512]{2,1,0:T(8,128)(2,1)S(1)}, bf16[16,16,512]{2,1,0:T(8,128)(2,1)S(1)}, u32[]{:S(2)}, u32[]{:S(2)}) collective-permute-start(bf16[16,16,512]{2,1,0:T(8,128)(2,1)S(1)} %get-tuple-element.27), channel_id=1, source_target_pairs={{0,16},{16,0},{1,17},{17,1},{2,18},{18,2},{3,19},{19,3},{4,20},{20... | collective-permute-start | bytes 786440 | tf_op jit(solution)/shard_map/ppermute | solution.py:309
  71.8 1.5 collective-permute-done.9.refs_4_
  73.3 3.0 %collective-permute-start.12 = (bf16[32,16,512]{2,1,0:T(8,128)(2,1)S(1)}, bf16[32,16,512]{2,1,0:T(8,128)(2,1)S(1)}, u32[]{:S(2)}, u32[]{:S(2)}) collective-permute-start(bf16[32,16,512]{2,1,0:T(8,128)(2,1)S(1)} %get-tuple-element.30.refs_0_), channel_id=1, source_target_pairs={{0,96},{32,0},{64,32},{96,64},{1,97},{33,1},{65,33},{97,65},{2,98}... | collective-permute-start | bytes 1572872 | tf_op jit(solution)/shard_map/ppermute | solution.py:237
  76.3 5.5 %collective-permute-start.11 = (bf16[32,16,512]{2,1,0:T(8,128)(2,1)S(1)}, bf16[32,16,512]{2,1,0:T(8,128)(2,1)}, u32[]{:S(2)}, u32[]{:S(2)}) collective-permute-start(bf16[32,16,512]{2,1,0:T(8,128)(2,1)S(1)} %get-tuple-element.30.refs_0_), channel_id=1, source_target_pairs={{0,64},{32,96},{64,0},{96,32},{1,65},{33,97},{65,1},{97,33},{2,66}... | collective-permute-start | bytes 1572872 | tf_op jit(solution)/shard_map/ppermute | solution.py:237
  81.8 3.1 %collective-permute-start.10 = (bf16[32,16,512]{2,1,0:T(8,128)(2,1)S(1)}, bf16[32,16,512]{2,1,0:T(8,128)(2,1)}, u32[]{:S(2)}, u32[]{:S(2)}) collective-permute-start(bf16[32,16,512]{2,1,0:T(8,128)(2,1)S(1)} %get-tuple-element.30.refs_0_), channel_id=1, source_target_pairs={{0,32},{32,64},{64,96},{96,0},{1,33},{33,65},{65,97},{97,1},{2,34}... | collective-permute-start | bytes 1572872 | tf_op jit(solution)/shard_map/ppermute | solution.py:237
  84.9 0.0 copy-done.3
  84.9 0.0 copy-start
  84.9 1.4 copy-done
  86.3 1.4 second_last.1.kept_hbm
  87.7 3.2 %all-to-all-done.mid_hbm = bf16[32,16,1024]{2,1,0:T(8,128)(2,1)} async-done(((bf16[32,16,1024]{2,1,0:T(8,128)(2,1)}), bf16[32,16,1024]{2,1,0:T(8,128)(2,1)}, u32[]{:S(2)}, u32[]{:S(2)}) %all-to-all-start) | async-done | bytes 1048608 | tf_op jit(solution)/shard_map/all_to_all | solution.py:303
  90.9 0.0 copy-done.1
  90.9 3.8 %second_pair.1 = bf16[2,8,64,768]{3,2,1,0:T(8,128)(2,1)} custom-call(bf16[32,16,1024]{2,1,0:T(8,128)(2,1)} %all-to-all-done.mid_hbm, bf16[256,256]{1,0:T(8,128)(2,1)S(1)} %copy-done.3, bf16[3,64,4096]{2,1,0:T(8,128)(2,1)S(1)} %copy-done.1, bf16[2,8,64,768]{3,2,1,0:T(8,128)(2,1)} %second_last.1.kept_hbm), custom_call_target="tpu_custom_call", output_to_operand_aliasing={{}: (3, {})} | custom-call | tf_op jit(solution)/shard_map/second_pair/pallas_call | solution.py:337
  94.8 19.7 %all-to-all-start.1 = ((bf16[16,64,768]{2,1,0:T(8,128)(2,1)}), bf16[16,64,768]{2,1,0:T(8,128)(2,1)}, u32[]{:S(2)}, u32[]{:S(2)}) async-start(bf16[16,64,768]{2,1,0:T(8,128)(2,1)} %bitcast.1), calls=%async_computation.1 | async-start | bytes 3145728 | tf_op jit(solution)/shard_map/all_to_all | solution.py:359
  114.5 0.0 collective-permute-done.12.refs_3_
  114.5 0.0 collective-permute-done.11.refs_2_
  114.5 0.0 collective-permute-done.10.refs_1_
  114.5 1.3 x_join.1.near_hbm
  115.9 0.0 copy-start.2
  115.9 2.1 %collective-permute-start.13 = (bf16[128,16,512]{2,1,0:T(8,128)(2,1)S(1)}, bf16[128,16,512]{2,1,0:T(8,128)(2,1)}, u32[]{:S(2)}, u32[]{:S(2)}) collective-permute-start(bf16[128,16,512]{2,1,0:T(8,128)(2,1)S(1)} %x_join.1.near_hbm), channel_id=1, source_target_pairs={{0,16},{16,0},{1,17},{17,1},{2,18},{18,2},{3,19},{19,3},{4,20},{20... | collective-permute-start | bytes 6291464 | tf_op jit(solution)/shard_map/ppermute | solution.py:312
  118.0 4.1 %collective-permute-done.13.far_hbm = bf16[128,16,512]{2,1,0:T(8,128)(2,1)} collective-permute-done((bf16[128,16,512]{2,1,0:T(8,128)(2,1)S(1)}, bf16[128,16,512]{2,1,0:T(8,128)(2,1)}, u32[]{:S(2)}, u32[]{:S(2)}) %collective-permute-start.13) | collective-permute-done | bytes 2097184 | tf_op jit(solution)/shard_map/ppermute | solution.py:312
  122.1 29.4 %all-to-all-done.1.x_hbm = bf16[16,64,768]{2,1,0:T(8,128)(2,1)} async-done(((bf16[16,64,768]{2,1,0:T(8,128)(2,1)}), bf16[16,64,768]{2,1,0:T(8,128)(2,1)}, u32[]{:S(2)}, u32[]{:S(2)}) %all-to-all-start.1) | async-done | bytes 1572896 | tf_op jit(solution)/shard_map/all_to_all | solution.py:359
  151.4 0.0 copy-done.2
  151.4 8.0 %mlp.1 = bf16[3,256,1024]{2,1,0:T(8,128)(2,1)} custom-call(bf16[16,64,768]{2,1,0:T(8,128)(2,1)} %all-to-all-done.1.x_hbm, f32[1,1024]{1,0:T(1,128)} %bitcast.4, bf16[128,16,512]{2,1,0:T(8,128)(2,1)} %copy-done.2, bf16[128,16,512]{2,1,0:T(8,128)(2,1)} %collective-permute-done.13.far_hbm), custom_call_target="tpu_custom_call" | custom-call | tf_op jit(solution)/shard_map/mlp/pallas_call | solution.py:362
  (2 shorter events, 0.0 us)
Async XLA Ops:
  4.5 36.1 %collective-permute-start = (bf16[10,16,512]{2,1,0:T(8,128)(2,1)}, bf16[10,16,512]{2,1,0:T(8,128)(2,1)S(1)}, u32[]{:S(2)}, u32[]{:S(2)}) collective-permute-start(bf16[10,16,512]{2,1,0:T(8,128)(2,1)} %get-tuple-element.19), channel_id=1, source_target_pairs={{0,128},{128,256},{256,384},{384,0},{1,129},{129,257},{257,385},{3... | collective-permute-start | bytes 491528 | tf_op jit(solution)/shard_map/ppermute | solution.py:237
  13.6 27.0 %collective-permute-start.1 = (bf16[10,16,512]{2,1,0:T(8,128)(2,1)}, bf16[10,16,512]{2,1,0:T(8,128)(2,1)S(1)}, u32[]{:S(2)}, u32[]{:S(2)}) collective-permute-start(bf16[10,16,512]{2,1,0:T(8,128)(2,1)} %get-tuple-element.20), channel_id=1, source_target_pairs={{0,256},{128,384},{256,0},{384,128},{1,257},{129,385},{257,1},{385... | collective-permute-start | bytes 491528 | tf_op jit(solution)/shard_map/ppermute | solution.py:237
  23.7 21.7 %collective-permute-start.2 = (bf16[10,16,512]{2,1,0:T(8,128)(2,1)}, bf16[10,16,512]{2,1,0:T(8,128)(2,1)S(1)}, u32[]{:S(2)}, u32[]{:S(2)}) collective-permute-start(bf16[10,16,512]{2,1,0:T(8,128)(2,1)} %get-tuple-element.21), channel_id=1, source_target_pairs={{0,384},{128,0},{256,128},{384,256},{1,385},{129,1},{257,129},{385... | collective-permute-start | bytes 491528 | tf_op jit(solution)/shard_map/ppermute | solution.py:237
  33.6 11.8 %copy-start.4 = (bf16[10,16,512]{2,1,0:T(8,128)(2,1)S(1)}, bf16[10,16,512]{2,1,0:T(8,128)(2,1)}, u32[]{:S(2)}) copy-start(bf16[10,16,512]{2,1,0:T(8,128)(2,1)} %get-tuple-element.18.refs_0_) | copy-start | bytes 491524
  33.6 57.3 %all-to-all-start = ((bf16[32,16,1024]{2,1,0:T(8,128)(2,1)}), bf16[32,16,1024]{2,1,0:T(8,128)(2,1)}, u32[]{:S(2)}, u32[]{:S(2)}) async-start(bf16[32,16,1024]{2,1,0:T(8,128)(2,1)} %first_pair.1), calls=%async_computation | async-start | bytes 2097152 | tf_op jit(solution)/shard_map/all_to_all | solution.py:303
  45.4 39.5 %copy-start.3 = (bf16[256,256]{1,0:T(8,128)(2,1)S(1)}, bf16[256,256]{1,0:T(8,128)(2,1)}, u32[]{:S(2)}) copy-start(bf16[256,256]{1,0:T(8,128)(2,1)} %right_ref.1) | copy-start | bytes 393220
  45.4 16.3 %collective-permute-start.3 = (bf16[8,16,512]{2,1,0:T(8,128)(2,1)S(1)}, bf16[8,16,512]{2,1,0:T(8,128)(2,1)S(1)}, u32[]{:S(2)}, u32[]{:S(2)}) collective-permute-start(bf16[8,16,512]{2,1,0:T(8,128)(2,1)S(1)} %get-tuple-element.23), channel_id=1, source_target_pairs={{0,32},{32,64},{64,96},{96,0},{1,33},{33,65},{65,97},{97,1},{2,34}... | collective-permute-start | bytes 393224 | tf_op jit(solution)/shard_map/ppermute | solution.py:237
  48.0 16.6 %collective-permute-start.4 = (bf16[8,16,512]{2,1,0:T(8,128)(2,1)S(1)}, bf16[8,16,512]{2,1,0:T(8,128)(2,1)S(1)}, u32[]{:S(2)}, u32[]{:S(2)}) collective-permute-start(bf16[8,16,512]{2,1,0:T(8,128)(2,1)S(1)} %get-tuple-element.24), channel_id=1, source_target_pairs={{0,64},{32,96},{64,0},{96,32},{1,65},{33,97},{65,1},{97,33},{2,66}... | collective-permute-start | bytes 393224 | tf_op jit(solution)/shard_map/ppermute | solution.py:237
  52.3 12.3 %collective-permute-start.5 = (bf16[8,16,512]{2,1,0:T(8,128)(2,1)S(1)}, bf16[8,16,512]{2,1,0:T(8,128)(2,1)S(1)}, u32[]{:S(2)}, u32[]{:S(2)}) collective-permute-start(bf16[8,16,512]{2,1,0:T(8,128)(2,1)S(1)} %get-tuple-element.25), channel_id=1, source_target_pairs={{0,96},{32,0},{64,32},{96,64},{1,97},{33,1},{65,33},{97,65},{2,98}... | collective-permute-start | bytes 393224 | tf_op jit(solution)/shard_map/ppermute | solution.py:237
  54.2 10.4 %collective-permute-start.8 = (bf16[8,16,512]{2,1,0:T(8,128)(2,1)S(1)}, bf16[8,16,512]{2,1,0:T(8,128)(2,1)S(1)}, u32[]{:S(2)}, u32[]{:S(2)}) collective-permute-start(bf16[8,16,512]{2,1,0:T(8,128)(2,1)S(1)} %get-tuple-element.26.refs_4_), channel_id=1, source_target_pairs={{0,3},{1,0},{2,1},{3,2},{4,7},{5,4},{6,5},{7,6},{8,11},{9,8},{10,9... | collective-permute-start | bytes 393224 | tf_op jit(solution)/shard_map/ppermute | solution.py:237
  59.2 8.4 %collective-permute-start.7 = (bf16[8,16,512]{2,1,0:T(8,128)(2,1)S(1)}, bf16[8,16,512]{2,1,0:T(8,128)(2,1)S(1)}, u32[]{:S(2)}, u32[]{:S(2)}) collective-permute-start(bf16[8,16,512]{2,1,0:T(8,128)(2,1)S(1)} %get-tuple-element.26.refs_4_), channel_id=1, source_target_pairs={{0,2},{1,3},{2,0},{3,1},{4,6},{5,7},{6,4},{7,5},{8,10},{9,11},{10,... | collective-permute-start | bytes 393224 | tf_op jit(solution)/shard_map/ppermute | solution.py:237
  61.7 8.1 %collective-permute-start.6 = (bf16[8,16,512]{2,1,0:T(8,128)(2,1)S(1)}, bf16[8,16,512]{2,1,0:T(8,128)(2,1)S(1)}, u32[]{:S(2)}, u32[]{:S(2)}) collective-permute-start(bf16[8,16,512]{2,1,0:T(8,128)(2,1)S(1)} %get-tuple-element.26.refs_4_), channel_id=1, source_target_pairs={{0,1},{1,2},{2,3},{3,0},{4,5},{5,6},{6,7},{7,4},{8,9},{9,10},{10,1... | collective-permute-start | bytes 393224 | tf_op jit(solution)/shard_map/ppermute | solution.py:237
  69.9 3.4 %collective-permute-start.9 = (bf16[16,16,512]{2,1,0:T(8,128)(2,1)S(1)}, bf16[16,16,512]{2,1,0:T(8,128)(2,1)S(1)}, u32[]{:S(2)}, u32[]{:S(2)}) collective-permute-start(bf16[16,16,512]{2,1,0:T(8,128)(2,1)S(1)} %get-tuple-element.27), channel_id=1, source_target_pairs={{0,16},{16,0},{1,17},{17,1},{2,18},{18,2},{3,19},{19,3},{4,20},{20... | collective-permute-start | bytes 786440 | tf_op jit(solution)/shard_map/ppermute | solution.py:309
  73.3 41.2 %collective-permute-start.12 = (bf16[32,16,512]{2,1,0:T(8,128)(2,1)S(1)}, bf16[32,16,512]{2,1,0:T(8,128)(2,1)S(1)}, u32[]{:S(2)}, u32[]{:S(2)}) collective-permute-start(bf16[32,16,512]{2,1,0:T(8,128)(2,1)S(1)} %get-tuple-element.30.refs_0_), channel_id=1, source_target_pairs={{0,96},{32,0},{64,32},{96,64},{1,97},{33,1},{65,33},{97,65},{2,98}... | collective-permute-start | bytes 1572872 | tf_op jit(solution)/shard_map/ppermute | solution.py:237
  76.3 38.3 %collective-permute-start.11 = (bf16[32,16,512]{2,1,0:T(8,128)(2,1)S(1)}, bf16[32,16,512]{2,1,0:T(8,128)(2,1)}, u32[]{:S(2)}, u32[]{:S(2)}) collective-permute-start(bf16[32,16,512]{2,1,0:T(8,128)(2,1)S(1)} %get-tuple-element.30.refs_0_), channel_id=1, source_target_pairs={{0,64},{32,96},{64,0},{96,32},{1,65},{33,97},{65,1},{97,33},{2,66}... | collective-permute-start | bytes 1572872 | tf_op jit(solution)/shard_map/ppermute | solution.py:237
  81.8 32.7 %collective-permute-start.10 = (bf16[32,16,512]{2,1,0:T(8,128)(2,1)S(1)}, bf16[32,16,512]{2,1,0:T(8,128)(2,1)}, u32[]{:S(2)}, u32[]{:S(2)}) collective-permute-start(bf16[32,16,512]{2,1,0:T(8,128)(2,1)S(1)} %get-tuple-element.30.refs_0_), channel_id=1, source_target_pairs={{0,32},{32,64},{64,96},{96,0},{1,33},{33,65},{65,97},{97,1},{2,34}... | collective-permute-start | bytes 1572872 | tf_op jit(solution)/shard_map/ppermute | solution.py:237
  84.9 1.4 copy-start
  86.3 4.6 %copy-start.1 = (bf16[3,64,4096]{2,1,0:T(8,128)(2,1)S(1)}, bf16[3,64,4096]{2,1,0:T(8,128)(2,1)}, u32[]{:S(2)}) copy-start(bf16[3,64,4096]{2,1,0:T(8,128)(2,1)} %tok_ref.3) | copy-start | bytes 4718596
  94.8 56.7 %all-to-all-start.1 = ((bf16[16,64,768]{2,1,0:T(8,128)(2,1)}), bf16[16,64,768]{2,1,0:T(8,128)(2,1)}, u32[]{:S(2)}, u32[]{:S(2)}) async-start(bf16[16,64,768]{2,1,0:T(8,128)(2,1)} %bitcast.1), calls=%async_computation.1 | async-start | bytes 3145728 | tf_op jit(solution)/shard_map/all_to_all | solution.py:359
  115.9 35.6 %copy-start.2 = (bf16[128,16,512]{2,1,0:T(8,128)(2,1)}, bf16[128,16,512]{2,1,0:T(8,128)(2,1)S(1)}, u32[]{:S(2)}) copy-start(bf16[128,16,512]{2,1,0:T(8,128)(2,1)S(1)} %x_join.1.near_hbm) | copy-start | bytes 6291460
  115.9 6.2 %collective-permute-start.13 = (bf16[128,16,512]{2,1,0:T(8,128)(2,1)S(1)}, bf16[128,16,512]{2,1,0:T(8,128)(2,1)}, u32[]{:S(2)}, u32[]{:S(2)}) collective-permute-start(bf16[128,16,512]{2,1,0:T(8,128)(2,1)S(1)} %x_join.1.near_hbm), channel_id=1, source_target_pairs={{0,16},{16,0},{1,17},{17,1},{2,18},{18,2},{3,19},{19,3},{4,20},{20... | collective-permute-start | bytes 6291464 | tf_op jit(solution)/shard_map/ppermute | solution.py:312

commit v5 on v3

--- a/solution.py
+++ b/solution.py
@@ -159,7 +159,7 @@
     return x + x * jnp.tanh(x * (0.7978845608028654 + 0.035677408136300125 * (x * x)))
 
 
-def mlp_kernel(x_hbm, gain_ref, near_hbm, far_hbm, out_hbm, x_ref, rows_ref, normed_ref, out_ref, weight_ref, *sems):
+def mlp_kernel(x_hbm, gain_ref, near_hbm, far_hbm, out_hbm, x_ref, rows_ref, normed_ref, out_ref, weight_ref, acc_ref, *sems):
     in_sems, weight_sems, out_sems = sems
     loads = [
         pltpu.make_async_copy(x_hbm.at[:, :, pl.ds(n * BROWS, BROWS)], x_ref.at[n], in_sems.at[n]) for n in range(3)
@@ -182,27 +182,33 @@
         normed_ref[n * BROWS:(n + 1) * BROWS, :] = normed
     own_y, own_z = lax.axis_index("y"), lax.axis_index("z_hi")
 
-    def weight(y, z, kind):
-        base = lax.rem(own_y + 4 - y, 4) * 8 + lax.rem(own_z + 4 - z, 4) * 2 + kind
-        blocks = [weight_ref[base + step * 32] for step in range(8)]
+    def half(y, z, kind, core):
+        base = lax.rem(own_y + 4 - y, 4) * 8 + lax.rem(own_z + 4 - z, 4) * 2 + kind + core * WEIGHTS
+        blocks = [weight_ref[base + x_step * 32] for x_step in range(4)]
         return jnp.concatenate([block[:, i * 256:(i + 1) * 256] for block in blocks for i in range(2)], axis=0)
 
-    for load in weights:
-        load.wait()
     stores = []
-    for h in range(GROUPS):
-        lanes = slice(h * 256, (h + 1) * 256)
-        hidden = [
-            twice_gelu(matmul_t(normed_ref[:, g * 256:(g + 1) * 256], weight(g, h, 0))).astype(BF16)
-            for g in range(GROUPS)
-        ]
-        down = jnp.concatenate([weight(h, g, 1) for g in range(GROUPS)], axis=0)
-        acc = jnp.dot(jnp.concatenate(hidden, axis=1), down, preferred_element_type=F32)
-        out = (rows_ref[:, lanes].astype(F32) + 0.5 * acc).astype(BF16)
-        out_ref[:, :, lanes] = out.reshape(3, BROWS, 256)
-        at = pl.ds(h * 256, 256)
-        stores.append(pltpu.make_async_copy(out_ref.at[:, :, at], out_hbm.at[:, :, at], out_sems.at[h]))
-        stores[h].start()
+    for core in range(2):
+        weights[core].wait()
+        for pair in range(2):
+            hidden = []
+            for g in range(GROUPS):
+                up = jnp.concatenate([half(g, pair * 2 + k, 0, core) for k in range(2)], axis=0)
+                hidden.append(twice_gelu(matmul_t(normed_ref[:, g * 256:(g + 1) * 256], up)).astype(BF16))
+            for k in range(2):
+                h = pair * 2 + k
+                lanes = slice(h * 256, (h + 1) * 256)
+                down = jnp.concatenate([half(h, g, 1, core) for g in range(GROUPS)], axis=0)
+                mine = jnp.concatenate([part[:, k * 128:(k + 1) * 128] for part in hidden], axis=1)
+                term = jnp.dot(mine, down, preferred_element_type=F32)
+                if core == 0:
+                    acc_ref[h] = term
+                    continue
+                out = (rows_ref[:, lanes].astype(F32) + 0.5 * (acc_ref[h] + term)).astype(BF16)
+                out_ref[:, :, lanes] = out.reshape(3, BROWS, 256)
+                at = pl.ds(h * 256, 256)
+                stores.append(pltpu.make_async_copy(out_ref.at[:, :, at], out_hbm.at[:, :, at], out_sems.at[h]))
+                stores[h].start()
     for store in stores:
         store.wait()
 
@@ -331,6 +337,7 @@
             pltpu.VMEM((3 * BROWS, width), BF16),
             pltpu.VMEM((3, BROWS, width), BF16),
             pltpu.VMEM((2 * WEIGHTS, 16, 512), BF16),
+            pltpu.VMEM((GROUPS, 3 * BROWS, 256), F32),
             pltpu.SemaphoreType.DMA((3,)),
             pltpu.SemaphoreType.DMA((2,)),
             pltpu.SemaphoreType.DMA((GROUPS,)),

time: 158 us -> 160 us (1.013)
  no operation moved by 1% of the time
where the time goes in v5:
time: 160 us; the launch traced here: 159 us
  starting transfers between devices  85.3 us (53%)
  waiting for transfers between devices  48.7 us (30%)
  Pallas kernels  23 us (14%)
    ppermute x12, starting transfers between devices, shift(): return lax.ppermute(x, axis, [(i, (i + step) % size) for i in range(size)])  55.2 us
    all_to_all x1, waiting for transfers between devices, per_device(): gated = lax.all_to_all(gated, CHAN_AXES, 0, 0, tiled=True)  29.4 us
    all_to_all x1, starting transfers between devices, per_device(): gated = lax.all_to_all(gated, CHAN_AXES, 0, 0, tiled=True)  19.1 us
    ppermute x12, waiting for transfers between devices, shift(): return lax.ppermute(x, axis, [(i, (i + step) % size) for i in range(size)])  9.97 us
    pallas_call x1, Pallas kernels, per_device(): pl.pallas_call(mlp_kernel, in_specs=[ANY, vmem, ANY, ANY], out_specs=ANY,...  9.21 us
    all_to_all x1, starting transfers between devices, per_device(): middle = lax.all_to_all(middle, SEQ_AXES, 0, 0, tiled=True)  6.94 us
    pallas_call x1, Pallas kernels, per_device(): pl.pallas_call(first_pair_kernel, grid=(1,), in_specs=[pl.BlockSpec((2, c...  4.52 us
    ppermute x1, waiting for transfers between devices, per_device(): far = lax.ppermute(near, 'core', [(0, 1), (1, 0)])  4.08 us
  transfers between devices with their start and end apart: 16, of which 7 were waited for; matrix products, arithmetic and copies ran while one was open for 0% of the time, Pallas kernels for 7%

profile of v5, /device:TPU:38, one launch (start us, length us, event | category | flops | bytes accessed | tf_op | source)
XLA Modules:
  0.0 158.8 jit_solution(423353418089573945)
XLA Ops:
  0.0 3.4 %first_last.1 = (bf16[10,16,512]{2,1,0:T(8,128)(2,1)}, bf16[10,16,512]{2,1,0:T(8,128)(2,1)}, bf16[10,16,512]{2,1,0:T(8,128)(2,1)}, bf16[10,16,512]{2,1,0:T(8,128)(2,1)}) custom-call(bf16[3,64,4096]{2,1,0:T(8,128)(2,1)} %tok_ref.5, bf16[64,4096]{1,0:T(8,128)(2,1)} %ker_ref.3, bf16[512,512]{1,0:T(8,128)(2,1)} %left_ref.3, bf16[4,32,256]{2,1,0:T(8,128)(2,1)} %bitcast.3, ...), custom_call_target="tpu_custom_call" | custom-call | tf_op jit(solution)/shard_map/first_last/pallas_call | solution.py:245
  3.4 9.1 %collective-permute-start = (bf16[10,16,512]{2,1,0:T(8,128)(2,1)}, bf16[10,16,512]{2,1,0:T(8,128)(2,1)S(1)}, u32[]{:S(2)}, u32[]{:S(2)}) collective-permute-start(bf16[10,16,512]{2,1,0:T(8,128)(2,1)} %get-tuple-element.19), channel_id=1, source_target_pairs={{0,128},{128,256},{256,384},{384,0},{1,129},{129,257},{257,385},{3... | collective-permute-start | bytes 491528 | tf_op jit(solution)/shard_map/ppermute | solution.py:217
  12.5 10.0 %collective-permute-start.1 = (bf16[10,16,512]{2,1,0:T(8,128)(2,1)}, bf16[10,16,512]{2,1,0:T(8,128)(2,1)S(1)}, u32[]{:S(2)}, u32[]{:S(2)}) collective-permute-start(bf16[10,16,512]{2,1,0:T(8,128)(2,1)} %get-tuple-element.20), channel_id=1, source_target_pairs={{0,256},{128,384},{256,0},{384,128},{1,257},{129,385},{257,1},{385... | collective-permute-start | bytes 491528 | tf_op jit(solution)/shard_map/ppermute | solution.py:217
  22.5 5.5 %collective-permute-start.2 = (bf16[10,16,512]{2,1,0:T(8,128)(2,1)}, bf16[10,16,512]{2,1,0:T(8,128)(2,1)S(1)}, u32[]{:S(2)}, u32[]{:S(2)}) collective-permute-start(bf16[10,16,512]{2,1,0:T(8,128)(2,1)} %get-tuple-element.21), channel_id=1, source_target_pairs={{0,384},{128,0},{256,128},{384,256},{1,385},{129,1},{257,129},{385... | collective-permute-start | bytes 491528 | tf_op jit(solution)/shard_map/ppermute | solution.py:217
  28.0 4.5 %first_pair.1 = bf16[32,16,1024]{2,1,0:T(8,128)(2,1)} custom-call(bf16[3,64,4096]{2,1,0:T(8,128)(2,1)} %tok_ref.5, bf16[64,4096]{1,0:T(8,128)(2,1)} %ker_ref.3, bf16[512,512]{1,0:T(8,128)(2,1)} %left_ref.3), custom_call_target="tpu_custom_call" | custom-call | tf_op jit(solution)/shard_map/first_pair/pallas_call | solution.py:262
  32.5 0.0 copy-start.4
  32.5 6.9 %all-to-all-start = ((bf16[32,16,1024]{2,1,0:T(8,128)(2,1)}), bf16[32,16,1024]{2,1,0:T(8,128)(2,1)}, u32[]{:S(2)}, u32[]{:S(2)}) async-start(bf16[32,16,1024]{2,1,0:T(8,128)(2,1)} %first_pair.1), calls=%async_computation | async-start | bytes 2097152 | tf_op jit(solution)/shard_map/all_to_all | solution.py:276
  39.4 0.0 collective-permute-done.refs_1_
  39.5 0.0 collective-permute-done.1.refs_2_
  39.5 4.8 %collective-permute-done.2.refs_3_ = bf16[10,16,512]{2,1,0:T(8,128)(2,1)S(1)} collective-permute-done((bf16[10,16,512]{2,1,0:T(8,128)(2,1)}, bf16[10,16,512]{2,1,0:T(8,128)(2,1)S(1)}, u32[]{:S(2)}, u32[]{:S(2)}) %collective-permute-start.2) | collective-permute-done | bytes 163872 | tf_op jit(solution)/shard_map/ppermute | solution.py:217
  44.3 0.0 copy-done.4
  44.3 0.0 copy-start.3
  44.3 2.5 %collective-permute-start.3 = (bf16[8,16,512]{2,1,0:T(8,128)(2,1)S(1)}, bf16[8,16,512]{2,1,0:T(8,128)(2,1)S(1)}, u32[]{:S(2)}, u32[]{:S(2)}) collective-permute-start(bf16[8,16,512]{2,1,0:T(8,128)(2,1)S(1)} %get-tuple-element.23), channel_id=1, source_target_pairs={{0,32},{32,64},{64,96},{96,0},{1,33},{33,65},{65,97},{97,1},{2,34}... | collective-permute-start | bytes 393224 | tf_op jit(solution)/shard_map/ppermute | solution.py:217
  46.8 4.3 %collective-permute-start.4 = (bf16[8,16,512]{2,1,0:T(8,128)(2,1)S(1)}, bf16[8,16,512]{2,1,0:T(8,128)(2,1)S(1)}, u32[]{:S(2)}, u32[]{:S(2)}) collective-permute-start(bf16[8,16,512]{2,1,0:T(8,128)(2,1)S(1)} %get-tuple-element.24), channel_id=1, source_target_pairs={{0,64},{32,96},{64,0},{96,32},{1,65},{33,97},{65,1},{97,33},{2,66}... | collective-permute-start | bytes 393224 | tf_op jit(solution)/shard_map/ppermute | solution.py:217
  51.2 1.9 %collective-permute-start.5 = (bf16[8,16,512]{2,1,0:T(8,128)(2,1)S(1)}, bf16[8,16,512]{2,1,0:T(8,128)(2,1)S(1)}, u32[]{:S(2)}, u32[]{:S(2)}) collective-permute-start(bf16[8,16,512]{2,1,0:T(8,128)(2,1)S(1)} %get-tuple-element.25), channel_id=1, source_target_pairs={{0,96},{32,0},{64,32},{96,64},{1,97},{33,1},{65,33},{97,65},{2,98}... | collective-permute-start | bytes 393224 | tf_op jit(solution)/shard_map/ppermute | solution.py:217
  53.1 4.9 %collective-permute-start.8 = (bf16[8,16,512]{2,1,0:T(8,128)(2,1)S(1)}, bf16[8,16,512]{2,1,0:T(8,128)(2,1)S(1)}, u32[]{:S(2)}, u32[]{:S(2)}) collective-permute-start(bf16[8,16,512]{2,1,0:T(8,128)(2,1)S(1)} %get-tuple-element.26.refs_4_), channel_id=1, source_target_pairs={{0,3},{1,0},{2,1},{3,2},{4,7},{5,4},{6,5},{7,6},{8,11},{9,8},{10,9... | collective-permute-start | bytes 393224 | tf_op jit(solution)/shard_map/ppermute | solution.py:217
  58.0 2.5 %collective-permute-start.7 = (bf16[8,16,512]{2,1,0:T(8,128)(2,1)S(1)}, bf16[8,16,512]{2,1,0:T(8,128)(2,1)S(1)}, u32[]{:S(2)}, u32[]{:S(2)}) collective-permute-start(bf16[8,16,512]{2,1,0:T(8,128)(2,1)S(1)} %get-tuple-element.26.refs_4_), channel_id=1, source_target_pairs={{0,2},{1,3},{2,0},{3,1},{4,6},{5,7},{6,4},{7,5},{8,10},{9,11},{10,... | collective-permute-start | bytes 393224 | tf_op jit(solution)/shard_map/ppermute | solution.py:217
  60.6 0.0 collective-permute-done.3.refs_1_
  60.6 2.9 %collective-permute-start.6 = (bf16[8,16,512]{2,1,0:T(8,128)(2,1)S(1)}, bf16[8,16,512]{2,1,0:T(8,128)(2,1)S(1)}, u32[]{:S(2)}, u32[]{:S(2)}) collective-permute-start(bf16[8,16,512]{2,1,0:T(8,128)(2,1)S(1)} %get-tuple-element.26.refs_4_), channel_id=1, source_target_pairs={{0,1},{1,2},{2,3},{3,0},{4,5},{5,6},{6,7},{7,4},{8,9},{9,10},{10,1... | collective-permute-start | bytes 393224 | tf_op jit(solution)/shard_map/ppermute | solution.py:217
  63.5 0.0 collective-permute-done.4.refs_2_
  63.5 0.0 collective-permute-done.5.refs_3_
  63.5 0.0 collective-permute-done.8.refs_7_
  63.5 2.9 %collective-permute-done.7.refs_6_ = bf16[8,16,512]{2,1,0:T(8,128)(2,1)S(1)} collective-permute-done((bf16[8,16,512]{2,1,0:T(8,128)(2,1)S(1)}, bf16[8,16,512]{2,1,0:T(8,128)(2,1)S(1)}, u32[]{:S(2)}, u32[]{:S(2)}) %collective-permute-start.7) | collective-permute-done | bytes 131104 | tf_op jit(solution)/shard_map/ppermute | solution.py:217
  66.4 2.3 %collective-permute-done.6.refs_5_ = bf16[8,16,512]{2,1,0:T(8,128)(2,1)S(1)} collective-permute-done((bf16[8,16,512]{2,1,0:T(8,128)(2,1)S(1)}, bf16[8,16,512]{2,1,0:T(8,128)(2,1)S(1)}, u32[]{:S(2)}, u32[]{:S(2)}) %collective-permute-start.6) | collective-permute-done | bytes 131104 | tf_op jit(solution)/shard_map/ppermute | solution.py:217
  68.7 0.1 plane_join.1
  68.7 1.9 %collective-permute-start.9 = (bf16[16,16,512]{2,1,0:T(8,128)(2,1)S(1)}, bf16[16,16,512]{2,1,0:T(8,128)(2,1)S(1)}, u32[]{:S(2)}, u32[]{:S(2)}) collective-permute-start(bf16[16,16,512]{2,1,0:T(8,128)(2,1)S(1)} %get-tuple-element.27), channel_id=1, source_target_pairs={{0,16},{16,0},{1,17},{17,1},{2,18},{18,2},{3,19},{19,3},{4,20},{20... | collective-permute-start | bytes 786440 | tf_op jit(solution)/shard_map/ppermute | solution.py:282
  70.7 1.5 collective-permute-done.9.refs_4_
  72.2 2.9 %collective-permute-start.12 = (bf16[32,16,512]{2,1,0:T(8,128)(2,1)S(1)}, bf16[32,16,512]{2,1,0:T(8,128)(2,1)S(1)}, u32[]{:S(2)}, u32[]{:S(2)}) collective-permute-start(bf16[32,16,512]{2,1,0:T(8,128)(2,1)S(1)} %get-tuple-element.30.refs_0_), channel_id=1, source_target_pairs={{0,96},{32,0},{64,32},{96,64},{1,97},{33,1},{65,33},{97,65},{2,98}... | collective-permute-start | bytes 1572872 | tf_op jit(solution)/shard_map/ppermute | solution.py:217
  75.1 5.6 %collective-permute-start.11 = (bf16[32,16,512]{2,1,0:T(8,128)(2,1)S(1)}, bf16[32,16,512]{2,1,0:T(8,128)(2,1)}, u32[]{:S(2)}, u32[]{:S(2)}) collective-permute-start(bf16[32,16,512]{2,1,0:T(8,128)(2,1)S(1)} %get-tuple-element.30.refs_0_), channel_id=1, source_target_pairs={{0,64},{32,96},{64,0},{96,32},{1,65},{33,97},{65,1},{97,33},{2,66}... | collective-permute-start | bytes 1572872 | tf_op jit(solution)/shard_map/ppermute | solution.py:217
  80.7 3.1 %collective-permute-start.10 = (bf16[32,16,512]{2,1,0:T(8,128)(2,1)S(1)}, bf16[32,16,512]{2,1,0:T(8,128)(2,1)}, u32[]{:S(2)}, u32[]{:S(2)}) collective-permute-start(bf16[32,16,512]{2,1,0:T(8,128)(2,1)S(1)} %get-tuple-element.30.refs_0_), channel_id=1, source_target_pairs={{0,32},{32,64},{64,96},{96,0},{1,33},{33,65},{65,97},{97,1},{2,34}... | collective-permute-start | bytes 1572872 | tf_op jit(solution)/shard_map/ppermute | solution.py:217
  83.7 0.0 copy-done.3
  83.8 0.0 copy-start
  83.8 1.4 copy-done
  85.2 1.4 second_last.1.kept_ref
  86.6 3.8 %all-to-all-done.mid_ref = bf16[32,16,1024]{2,1,0:T(8,128)(2,1)} async-done(((bf16[32,16,1024]{2,1,0:T(8,128)(2,1)}), bf16[32,16,1024]{2,1,0:T(8,128)(2,1)}, u32[]{:S(2)}, u32[]{:S(2)}) %all-to-all-start) | async-done | bytes 1048608 | tf_op jit(solution)/shard_map/all_to_all | solution.py:276
  90.4 0.0 copy-done.1
  90.4 3.0 %second_pair.1 = bf16[2,8,64,768]{3,2,1,0:T(8,128)(2,1)} custom-call(bf16[32,16,1024]{2,1,0:T(8,128)(2,1)} %all-to-all-done.mid_ref, bf16[256,256]{1,0:T(8,128)(2,1)S(1)} %copy-done.3, bf16[3,64,4096]{2,1,0:T(8,128)(2,1)S(1)} %copy-done.1, bf16[2,8,64,768]{3,2,1,0:T(8,128)(2,1)} %second_last.1.kept_ref), custom_call_target="tpu_custom_call", output_to_operand_aliasing={{}: (3, {})} | custom-call | tf_op jit(solution)/shard_map/second_pair/pallas_call | solution.py:310
  93.4 19.1 %all-to-all-start.1 = ((bf16[16,64,768]{2,1,0:T(8,128)(2,1)}), bf16[16,64,768]{2,1,0:T(8,128)(2,1)}, u32[]{:S(2)}, u32[]{:S(2)}) async-start(bf16[16,64,768]{2,1,0:T(8,128)(2,1)} %bitcast.1), calls=%async_computation.1 | async-start | bytes 3145728 | tf_op jit(solution)/shard_map/all_to_all | solution.py:326
  112.5 0.0 collective-permute-done.12.refs_3_
  112.5 0.0 collective-permute-done.11.refs_2_
  112.5 0.0 collective-permute-done.10.refs_1_
  112.5 1.3 x_join.1.near_hbm
  113.9 0.0 copy-start.2
  113.9 2.1 %collective-permute-start.13 = (bf16[128,16,512]{2,1,0:T(8,128)(2,1)S(1)}, bf16[128,16,512]{2,1,0:T(8,128)(2,1)}, u32[]{:S(2)}, u32[]{:S(2)}) collective-permute-start(bf16[128,16,512]{2,1,0:T(8,128)(2,1)S(1)} %x_join.1.near_hbm), channel_id=1, source_target_pairs={{0,16},{16,0},{1,17},{17,1},{2,18},{18,2},{3,19},{19,3},{4,20},{20... | collective-permute-start | bytes 6291464 | tf_op jit(solution)/shard_map/ppermute | solution.py:285
  116.0 4.1 %collective-permute-done.13.far_hbm = bf16[128,16,512]{2,1,0:T(8,128)(2,1)} collective-permute-done((bf16[128,16,512]{2,1,0:T(8,128)(2,1)S(1)}, bf16[128,16,512]{2,1,0:T(8,128)(2,1)}, u32[]{:S(2)}, u32[]{:S(2)}) %collective-permute-start.13) | collective-permute-done | bytes 2097184 | tf_op jit(solution)/shard_map/ppermute | solution.py:285
  120.1 29.4 %all-to-all-done.1.x_hbm = bf16[16,64,768]{2,1,0:T(8,128)(2,1)} async-done(((bf16[16,64,768]{2,1,0:T(8,128)(2,1)}), bf16[16,64,768]{2,1,0:T(8,128)(2,1)}, u32[]{:S(2)}, u32[]{:S(2)}) %all-to-all-start.1) | async-done | bytes 1572896 | tf_op jit(solution)/shard_map/all_to_all | solution.py:326
  149.4 0.0 copy-done.2
  149.4 9.2 %mlp.1 = bf16[3,256,1024]{2,1,0:T(8,128)(2,1)} custom-call(bf16[16,64,768]{2,1,0:T(8,128)(2,1)} %all-to-all-done.1.x_hbm, f32[1,1024]{1,0:T(1,128)} %bitcast.4, bf16[128,16,512]{2,1,0:T(8,128)(2,1)} %copy-done.2, bf16[128,16,512]{2,1,0:T(8,128)(2,1)} %collective-permute-done.13.far_hbm), custom_call_target="tpu_custom_call" | custom-call | tf_op jit(solution)/shard_map/mlp/pallas_call | solution.py:329
  (2 shorter events, 0.0 us)
Async XLA Ops:
  3.4 36.1 %collective-permute-start = (bf16[10,16,512]{2,1,0:T(8,128)(2,1)}, bf16[10,16,512]{2,1,0:T(8,128)(2,1)S(1)}, u32[]{:S(2)}, u32[]{:S(2)}) collective-permute-start(bf16[10,16,512]{2,1,0:T(8,128)(2,1)} %get-tuple-element.19), channel_id=1, source_target_pairs={{0,128},{128,256},{256,384},{384,0},{1,129},{129,257},{257,385},{3... | collective-permute-start | bytes 491528 | tf_op jit(solution)/shard_map/ppermute | solution.py:217
  12.5 27.0 %collective-permute-start.1 = (bf16[10,16,512]{2,1,0:T(8,128)(2,1)}, bf16[10,16,512]{2,1,0:T(8,128)(2,1)S(1)}, u32[]{:S(2)}, u32[]{:S(2)}) collective-permute-start(bf16[10,16,512]{2,1,0:T(8,128)(2,1)} %get-tuple-element.20), channel_id=1, source_target_pairs={{0,256},{128,384},{256,0},{384,128},{1,257},{129,385},{257,1},{385... | collective-permute-start | bytes 491528 | tf_op jit(solution)/shard_map/ppermute | solution.py:217
  22.5 21.7 %collective-permute-start.2 = (bf16[10,16,512]{2,1,0:T(8,128)(2,1)}, bf16[10,16,512]{2,1,0:T(8,128)(2,1)S(1)}, u32[]{:S(2)}, u32[]{:S(2)}) collective-permute-start(bf16[10,16,512]{2,1,0:T(8,128)(2,1)} %get-tuple-element.21), channel_id=1, source_target_pairs={{0,384},{128,0},{256,128},{384,256},{1,385},{129,1},{257,129},{385... | collective-permute-start | bytes 491528 | tf_op jit(solution)/shard_map/ppermute | solution.py:217
  32.5 11.8 %copy-start.4 = (bf16[10,16,512]{2,1,0:T(8,128)(2,1)S(1)}, bf16[10,16,512]{2,1,0:T(8,128)(2,1)}, u32[]{:S(2)}) copy-start(bf16[10,16,512]{2,1,0:T(8,128)(2,1)} %get-tuple-element.18.refs_0_) | copy-start | bytes 491524
  32.5 57.9 %all-to-all-start = ((bf16[32,16,1024]{2,1,0:T(8,128)(2,1)}), bf16[32,16,1024]{2,1,0:T(8,128)(2,1)}, u32[]{:S(2)}, u32[]{:S(2)}) async-start(bf16[32,16,1024]{2,1,0:T(8,128)(2,1)} %first_pair.1), calls=%async_computation | async-start | bytes 2097152 | tf_op jit(solution)/shard_map/all_to_all | solution.py:276
  44.3 39.5 %copy-start.3 = (bf16[256,256]{1,0:T(8,128)(2,1)S(1)}, bf16[256,256]{1,0:T(8,128)(2,1)}, u32[]{:S(2)}) copy-start(bf16[256,256]{1,0:T(8,128)(2,1)} %right_ref.1) | copy-start | bytes 393220
  44.3 16.3 %collective-permute-start.3 = (bf16[8,16,512]{2,1,0:T(8,128)(2,1)S(1)}, bf16[8,16,512]{2,1,0:T(8,128)(2,1)S(1)}, u32[]{:S(2)}, u32[]{:S(2)}) collective-permute-start(bf16[8,16,512]{2,1,0:T(8,128)(2,1)S(1)} %get-tuple-element.23), channel_id=1, source_target_pairs={{0,32},{32,64},{64,96},{96,0},{1,33},{33,65},{65,97},{97,1},{2,34}... | collective-permute-start | bytes 393224 | tf_op jit(solution)/shard_map/ppermute | solution.py:217
  46.8 16.6 %collective-permute-start.4 = (bf16[8,16,512]{2,1,0:T(8,128)(2,1)S(1)}, bf16[8,16,512]{2,1,0:T(8,128)(2,1)S(1)}, u32[]{:S(2)}, u32[]{:S(2)}) collective-permute-start(bf16[8,16,512]{2,1,0:T(8,128)(2,1)S(1)} %get-tuple-element.24), channel_id=1, source_target_pairs={{0,64},{32,96},{64,0},{96,32},{1,65},{33,97},{65,1},{97,33},{2,66}... | collective-permute-start | bytes 393224 | tf_op jit(solution)/shard_map/ppermute | solution.py:217
  51.2 12.3 %collective-permute-start.5 = (bf16[8,16,512]{2,1,0:T(8,128)(2,1)S(1)}, bf16[8,16,512]{2,1,0:T(8,128)(2,1)S(1)}, u32[]{:S(2)}, u32[]{:S(2)}) collective-permute-start(bf16[8,16,512]{2,1,0:T(8,128)(2,1)S(1)} %get-tuple-element.25), channel_id=1, source_target_pairs={{0,96},{32,0},{64,32},{96,64},{1,97},{33,1},{65,33},{97,65},{2,98}... | collective-permute-start | bytes 393224 | tf_op jit(solution)/shard_map/ppermute | solution.py:217
  53.1 10.4 %collective-permute-start.8 = (bf16[8,16,512]{2,1,0:T(8,128)(2,1)S(1)}, bf16[8,16,512]{2,1,0:T(8,128)(2,1)S(1)}, u32[]{:S(2)}, u32[]{:S(2)}) collective-permute-start(bf16[8,16,512]{2,1,0:T(8,128)(2,1)S(1)} %get-tuple-element.26.refs_4_), channel_id=1, source_target_pairs={{0,3},{1,0},{2,1},{3,2},{4,7},{5,4},{6,5},{7,6},{8,11},{9,8},{10,9... | collective-permute-start | bytes 393224 | tf_op jit(solution)/shard_map/ppermute | solution.py:217
  58.0 8.4 %collective-permute-start.7 = (bf16[8,16,512]{2,1,0:T(8,128)(2,1)S(1)}, bf16[8,16,512]{2,1,0:T(8,128)(2,1)S(1)}, u32[]{:S(2)}, u32[]{:S(2)}) collective-permute-start(bf16[8,16,512]{2,1,0:T(8,128)(2,1)S(1)} %get-tuple-element.26.refs_4_), channel_id=1, source_target_pairs={{0,2},{1,3},{2,0},{3,1},{4,6},{5,7},{6,4},{7,5},{8,10},{9,11},{10,... | collective-permute-start | bytes 393224 | tf_op jit(solution)/shard_map/ppermute | solution.py:217
  60.6 8.1 %collective-permute-start.6 = (bf16[8,16,512]{2,1,0:T(8,128)(2,1)S(1)}, bf16[8,16,512]{2,1,0:T(8,128)(2,1)S(1)}, u32[]{:S(2)}, u32[]{:S(2)}) collective-permute-start(bf16[8,16,512]{2,1,0:T(8,128)(2,1)S(1)} %get-tuple-element.26.refs_4_), channel_id=1, source_target_pairs={{0,1},{1,2},{2,3},{3,0},{4,5},{5,6},{6,7},{7,4},{8,9},{9,10},{10,1... | collective-permute-start | bytes 393224 | tf_op jit(solution)/shard_map/ppermute | solution.py:217
  68.7 3.4 %collective-permute-start.9 = (bf16[16,16,512]{2,1,0:T(8,128)(2,1)S(1)}, bf16[16,16,512]{2,1,0:T(8,128)(2,1)S(1)}, u32[]{:S(2)}, u32[]{:S(2)}) collective-permute-start(bf16[16,16,512]{2,1,0:T(8,128)(2,1)S(1)} %get-tuple-element.27), channel_id=1, source_target_pairs={{0,16},{16,0},{1,17},{17,1},{2,18},{18,2},{3,19},{19,3},{4,20},{20... | collective-permute-start | bytes 786440 | tf_op jit(solution)/shard_map/ppermute | solution.py:282
  72.2 40.4 %collective-permute-start.12 = (bf16[32,16,512]{2,1,0:T(8,128)(2,1)S(1)}, bf16[32,16,512]{2,1,0:T(8,128)(2,1)S(1)}, u32[]{:S(2)}, u32[]{:S(2)}) collective-permute-start(bf16[32,16,512]{2,1,0:T(8,128)(2,1)S(1)} %get-tuple-element.30.refs_0_), channel_id=1, source_target_pairs={{0,96},{32,0},{64,32},{96,64},{1,97},{33,1},{65,33},{97,65},{2,98}... | collective-permute-start | bytes 1572872 | tf_op jit(solution)/shard_map/ppermute | solution.py:217
  75.1 37.5 %collective-permute-start.11 = (bf16[32,16,512]{2,1,0:T(8,128)(2,1)S(1)}, bf16[32,16,512]{2,1,0:T(8,128)(2,1)}, u32[]{:S(2)}, u32[]{:S(2)}) collective-permute-start(bf16[32,16,512]{2,1,0:T(8,128)(2,1)S(1)} %get-tuple-element.30.refs_0_), channel_id=1, source_target_pairs={{0,64},{32,96},{64,0},{96,32},{1,65},{33,97},{65,1},{97,33},{2,66}... | collective-permute-start | bytes 1572872 | tf_op jit(solution)/shard_map/ppermute | solution.py:217
  80.7 31.9 %collective-permute-start.10 = (bf16[32,16,512]{2,1,0:T(8,128)(2,1)S(1)}, bf16[32,16,512]{2,1,0:T(8,128)(2,1)}, u32[]{:S(2)}, u32[]{:S(2)}) collective-permute-start(bf16[32,16,512]{2,1,0:T(8,128)(2,1)S(1)} %get-tuple-element.30.refs_0_), channel_id=1, source_target_pairs={{0,32},{32,64},{64,96},{96,0},{1,33},{33,65},{65,97},{97,1},{2,34}... | collective-permute-start | bytes 1572872 | tf_op jit(solution)/shard_map/ppermute | solution.py:217
  83.8 1.4 copy-start
  85.2 5.2 %copy-start.1 = (bf16[3,64,4096]{2,1,0:T(8,128)(2,1)S(1)}, bf16[3,64,4096]{2,1,0:T(8,128)(2,1)}, u32[]{:S(2)}) copy-start(bf16[3,64,4096]{2,1,0:T(8,128)(2,1)} %tok_ref.5) | copy-start | bytes 4718596
  93.4 56.0 %all-to-all-start.1 = ((bf16[16,64,768]{2,1,0:T(8,128)(2,1)}), bf16[16,64,768]{2,1,0:T(8,128)(2,1)}, u32[]{:S(2)}, u32[]{:S(2)}) async-start(bf16[16,64,768]{2,1,0:T(8,128)(2,1)} %bitcast.1), calls=%async_computation.1 | async-start | bytes 3145728 | tf_op jit(solution)/shard_map/all_to_all | solution.py:326
  113.9 35.5 %copy-start.2 = (bf16[128,16,512]{2,1,0:T(8,128)(2,1)}, bf16[128,16,512]{2,1,0:T(8,128)(2,1)S(1)}, u32[]{:S(2)}) copy-start(bf16[128,16,512]{2,1,0:T(8,128)(2,1)S(1)} %x_join.1.near_hbm) | copy-start | bytes 6291460
  113.9 6.2 %collective-permute-start.13 = (bf16[128,16,512]{2,1,0:T(8,128)(2,1)S(1)}, bf16[128,16,512]{2,1,0:T(8,128)(2,1)}, u32[]{:S(2)}, u32[]{:S(2)}) collective-permute-start(bf16[128,16,512]{2,1,0:T(8,128)(2,1)S(1)} %x_join.1.near_hbm), channel_id=1, source_target_pairs={{0,16},{16,0},{1,17},{17,1},{2,18},{18,2},{3,19},{19,3},{4,20},{20... | collective-permute-start | bytes 6291464 | tf_op jit(solution)/shard_map/ppermute | solution.py:285
